TPU v7x, 256 devices: a whole 4x4x8 slice. The times are simulated.
256 devices in a mesh: curve: 64 (over z, y_lo, x), mp: 4 (over y_hi, core).
Axes of the slice: x: 4, y: 4 (y_hi: 2, y_lo: 2; y = y_hi * 2 + y_lo), z: 8, core: 2. Of those that a mesh axis runs over, the one named last changes fastest.
Arguments:
- points: bfloat16 [192, 1024, 512], P('curve'), may hold values from -6 to 6
- order: int32 [192, 1024], P('curve'), may hold values from 0 to 1023, each once within a row
- counts: int32 [64], P('curve'), may hold values from 1 to 3, as said below
- cotangent: bfloat16 [192, 1024, 512], P('curve'), may hold values from -6 to 6
- norm_gain: float32 [512], replicated, may hold values from 0.5 to 1.5
- w_qkv: bfloat16 [512, 3, 512], P(None, None, 'mp')
- w_out: bfloat16 [512, 512], P('mp'), may hold values from -0.25 to 0.25
Outputs:
- grad_points: bfloat16 [192, 1024, 512], P('curve', None, 'mp')
- grad_gain: float32 [512], P('mp')
- grad_qkv: float32 [512, 3, 512], P(None, None, 'mp')
- grad_out: float32 [512, 512], P('mp')
Inputs may be any that keep to these rules, and one draw needn't show every extreme that they name: `counts`: in every aligned group of 4 indices of curve one index, at one of the group's first three places, holds 3; the index after it holds 1; every other index holds 1.
All inputs are finite; a program needn't handle non-finite values.
Results may differ from a plain program's by a relative error of at most 0.013.
Values may be sent and summed in bfloat16 or wider, within the bound.
No kernel may reach another device: no remote copies, remote signals or barrier semaphores. Data moves between devices by JAX's collectives and lax.ppermute only.
A program may use at most 128 MiB of HBM per device.

v0:
```python
import math

import jax
import jax.numpy as jnp
from jax import lax
from jax.sharding import PartitionSpec as P

D = 512
HEADS = 8


EPSILON = 1e-05


def passed_along(shard, axis, by):
    devices = lax.axis_size(axis)
    return lax.ppermute(shard, axis, [(i, (i + by) % devices) for i in range(devices)])


def attention_terms(normed, weight_qkv, weight_out, grad_rows, head_size):
    row_count = normed.shape[0]
    group_width = weight_out.shape[0]
    group_heads = group_width // head_size
    factor = head_size ** (-0.5)
    projected = jnp.einsum(
        "kd,dtg->tkg", normed, weight_qkv, preferred_element_type=jnp.float32
    ).astype(jnp.bfloat16)
    queries = projected[0].reshape(row_count, group_heads, head_size)
    key_rows = projected[1].reshape(row_count, group_heads, head_size)
    value_rows = projected[2].reshape(row_count, group_heads, head_size)
    scores = (
        jnp.einsum("qhe,khe->hqk", queries, key_rows, preferred_element_type=jnp.float32) * factor
    )
    highest = jnp.max(scores, axis=-1, keepdims=True)
    expos = jnp.exp(scores - highest)
    probs = expos / jnp.sum(expos, axis=-1, keepdims=True)
    probs_low = probs.astype(jnp.bfloat16)
    attended = (
        jnp.einsum("hqk,khe->qhe", probs_low, value_rows, preferred_element_type=jnp.float32)
        .astype(jnp.bfloat16)
        .reshape(row_count, group_width)
    )
    grad_attended = jnp.einsum(
        "kd,gd->kg", grad_rows, weight_out, preferred_element_type=jnp.float32
    ).astype(jnp.bfloat16)
    out_term = jnp.einsum("kg,kd->gd", attended, grad_rows, preferred_element_type=jnp.float32)
    grad_heads = grad_attended.reshape(row_count, group_heads, head_size)
    grad_values = jnp.einsum(
        "hqk,qhe->khe", probs_low, grad_heads, preferred_element_type=jnp.float32
    ).astype(jnp.bfloat16)
    grad_probs = jnp.einsum(
        "qhe,khe->hqk", grad_heads, value_rows, preferred_element_type=jnp.float32
    )
    inner_sum = jnp.sum(probs * grad_probs, axis=-1, keepdims=True)
    grad_scores = (probs * (grad_probs - inner_sum) * factor).astype(jnp.bfloat16)
    grad_queries = jnp.einsum(
        "hqk,khe->qhe", grad_scores, key_rows, preferred_element_type=jnp.float32
    ).astype(jnp.bfloat16)
    grad_keys = jnp.einsum(
        "hqk,qhe->khe", grad_scores, queries, preferred_element_type=jnp.float32
    ).astype(jnp.bfloat16)
    grad_projected = jnp.stack([grad_queries, grad_keys, grad_values]).reshape(
        3, row_count, group_width
    )
    qkv_term = jnp.einsum("kd,tkg->dtg", normed, grad_projected, preferred_element_type=jnp.float32)
    group_normed = jnp.einsum(
        "tkg,dtg->kd", grad_projected, weight_qkv, preferred_element_type=jnp.float32
    ).astype(jnp.bfloat16)
    return (group_normed, qkv_term, out_term)


def place_rows(placed, back_rows, slot, live_count, branch, half_rows):
    slot_count = placed.shape[0]
    placed = lax.dynamic_update_slice(placed, branch[None, :half_rows], (slot, half_rows, 0))
    onward = slot + 1 < live_count
    target = jnp.minimum(slot + 1, slot_count - 1)
    present = lax.dynamic_slice(placed, (target, 0, 0), (1, half_rows, placed.shape[2]))
    placed = lax.dynamic_update_slice(
        placed, jnp.where(onward, branch[None, half_rows:], present), (target, 0, 0)
    )
    back_rows = jnp.where(onward, back_rows, branch[half_rows:])
    return (placed, back_rows)


def shards(points, order, counts, cotangent, norm_gain, w_qkv, w_out):
    slot_count, patch_rows, width = points.shape
    half_rows = patch_rows // 2
    group_width = w_out.shape[0]
    head_size = D // HEADS
    model_part = lax.axis_index("mp")
    slot_index = jnp.arange(slot_count, dtype=jnp.int32)[:, None]
    series_x = points[slot_index, order]
    series_dy = cotangent[slot_index, order]
    next_x, next_dy = passed_along((series_x[0, :half_rows], series_dy[0, :half_rows]), "curve", -1)
    live_count = counts[0]

    def assemble(series, borrowed, slot):
        tail_rows = lax.dynamic_index_in_dim(
            series, jnp.minimum(slot, slot_count - 1), 0, keepdims=False
        )[half_rows:]
        ahead = lax.dynamic_index_in_dim(
            series, jnp.minimum(slot + 1, slot_count - 1), 0, keepdims=False
        )[:half_rows]
        head_rows = jnp.where(slot + 1 < live_count, ahead, borrowed)
        return jnp.concatenate([tail_rows, head_rows], axis=0)

    def run_patch(rows_x, rows_dy):
        values = rows_x.astype(jnp.float32)
        centre = values - jnp.mean(values, axis=-1, keepdims=True)
        inverse = lax.rsqrt(jnp.mean(centre * centre, axis=-1, keepdims=True) + EPSILON)
        unit = centre * inverse
        normed = (unit * norm_gain).astype(jnp.bfloat16)
        group_normed, qkv_term, out_term = attention_terms(normed, w_qkv, w_out, rows_dy, head_size)
        total = lax.psum(group_normed.astype(jnp.float32).astype(jnp.bfloat16), "mp").astype(
            jnp.float32
        )
        scaled = total * norm_gain
        branch_full = inverse * (
            scaled
            - jnp.mean(scaled, axis=-1, keepdims=True)
            - unit * jnp.mean(scaled * unit, axis=-1, keepdims=True)
        )
        branch = lax.dynamic_slice_in_dim(branch_full, model_part * group_width, group_width, 1)
        gain_term = lax.dynamic_slice_in_dim(
            jnp.sum(total * unit, axis=0), model_part * group_width, group_width
        )
        return (branch, qkv_term, out_term, gain_term)

    def make_visit(limit):

        def visit_patch(slot, state_now):
            placed, back_rows, qkv_total, out_total, gain_total = state_now
            alive = slot < limit
            weight_alive = alive.astype(jnp.float32)
            branch, qkv_term, out_term, gain_term = run_patch(
                assemble(series_x, next_x, slot), assemble(series_dy, next_dy, slot)
            )
            new_placed, new_back = place_rows(
                placed, back_rows, slot, live_count, branch, half_rows
            )
            placed = jnp.where(alive, new_placed, placed)
            back_rows = jnp.where(alive, new_back, back_rows)
            return (
                placed,
                back_rows,
                qkv_total + weight_alive * qkv_term,
                out_total + weight_alive * out_term,
                gain_total + weight_alive * gain_term,
            )

        return visit_patch

    start = (
        jnp.zeros((slot_count, patch_rows, group_width), jnp.float32),
        jnp.zeros((half_rows, group_width), jnp.float32),
        jnp.zeros(w_qkv.shape, jnp.float32),
        jnp.zeros(w_out.shape, jnp.float32),
        jnp.zeros((group_width,), jnp.float32),
    )
    placed, back_rows, qkv_total, out_total, gain_total = lax.fori_loop(
        0, slot_count, make_visit(live_count), start
    )
    returned = passed_along(back_rows.astype(jnp.bfloat16), "curve", 1).astype(back_rows.dtype)
    placed = lax.dynamic_update_slice(placed, returned[None], (0, 0, 0))
    own_dy = lax.dynamic_slice_in_dim(series_dy, model_part * group_width, group_width, 2).astype(
        jnp.float32
    )
    grad_series = own_dy + placed
    grad_points = (
        jnp.zeros((slot_count, patch_rows, group_width), jnp.float32)
        .at[slot_index, order]
        .set(grad_series)
        .astype(jnp.bfloat16)
    )
    factor = 1.0 / math.sqrt(lax.axis_size("curve") * slot_count * patch_rows)
    qkv_sum, out_sum, gain_sum = lax.psum(
        (qkv_total * factor, out_total * factor, gain_total * factor), "curve"
    )
    return (grad_points, gain_sum, qkv_sum, out_sum)


def solution(mesh):
    in_specs = (
        P("curve", None, None),
        P("curve", None),
        P("curve"),
        P("curve", None, None),
        P(),
        P(None, None, "mp"),
        P("mp", None),
    )
    out_specs = (P("curve", None, "mp"), P("mp"), P(None, None, "mp"), P("mp", None))
    return jax.shard_map(shards, mesh=mesh, in_specs=in_specs, out_specs=out_specs, check_vma=False)
```

profile of v0, /device:TPU:16, one launch (start us, length us, event | category | flops | bytes accessed | tf_op | source)
XLA Modules:
  0.0 1116.2 jit_solution(4780791840511522858)
XLA Ops:
  9.9 35.8 %gather_fusion = bf16[3072,512]{1,0:T(8,128)(2,1)} fusion(bf16[3,1024,512]{2,1,0:T(8,128)(2,1)S(1)} %copy-done, s32[3072]{0:T(1024)S(1)} %reshape.111), kind=kCustom, calls=%fused_computation | custom fusion | bytes 6316032 | tf_op jit(solution)/shard_map/gather | solution.py:93
  47.6 8.8 collective-permute-start.1
  56.4 56.8 %gather_fusion.1 = bf16[3072,512]{1,0:T(8,128)(2,1)} fusion(bf16[3,1024,512]{2,1,0:T(8,128)(2,1)} %param.9, s32[3072]{0:T(1024)S(1)} %reshape.111), kind=kCustom, calls=%fused_computation.1 | custom fusion | bytes 6316032 | tf_op jit(solution)/shard_map/gather | solution.py:92
  117.9 10.8 collective-permute-done
  128.7 363.5 %while.24 = (s32[]{:T(128)}, f32[3,1024,128]{2,1,0:T(8,128)}, bf16[512,128]{1,0:T(8,128)(2,1)}, f32[512,3,128]{2,0,1:T(8,128)}, f32[128,512]{1,0:T(8,128)}, /*in...) while((s32[]{:T(128)}, f32[3,1024,128]{2,1,0:T(8,128)}, ...), condition=%wide.region_10.11_spmd.clone, body=%wide.region_0.10_spmd.clone.sunk | while | flops 3165265920 | bytes 160627248 | solution.py:160
  131.4 2.3 fusion.131
  138.6 7.0 fusion.135
  147.3 4.5 fusion.137
  151.8 14.3 %fusion.139 = bf16[2,64,1024]{2,1,0:T(8,128)(2,1)} fusion(bf16[1024,2,64]{0,2,1:T(8,128)(2,1)} %bitcast.151, f32[2,1024,1024]{1,2,0:T(8,128)} %fusion.137, f32[2,1024,1024]{1,2,0:T(8,128)} %get-tuple-element.559, f32[2,1024]{1,0:T(2,128)S(1)} %get-tuple-element.560), kind=kOutput, calls=%fused_computation.32.clone.1 | convolution fusion | flops 283249664 | bytes 17309696 | tf_op jit(solution)/shard_map/while/body/eval_jaxpr/hqk,khe->qhe/dot_general | solution.py:56
  166.1 14.3 %fusion.138 = bf16[2,64,1024]{2,1,0:T(8,128)(2,1)} fusion(bf16[1024,2,64]{0,2,1:T(8,128)(2,1)} %bitcast.149, f32[2,1024,1024]{1,2,0:T(8,128)} %fusion.137, f32[2,1024,1024]{1,2,0:T(8,128)} %get-tuple-element.559, f32[2,1024]{1,0:T(2,128)S(1)} %get-tuple-element.560), kind=kOutput, calls=%fused_computation.33.clone.1 | convolution fusion | flops 283249664 | bytes 17309696 | tf_op jit(solution)/shard_map/while/body/eval_jaxpr/hqk,qhe->khe/dot_general | solution.py:59
  180.4 5.6 fusion.136
  191.4 2.9 bitcast_convert_fusion.2
  194.4 4.9 fusion.145
  200.0 2.4 fusion.146
  206.4 34.7 %all-reduce.6.cloned.1.call-done = bf16[1024,512]{1,0:T(8,128)(2,1)} async-done(((bf16[1024,512]{1,0:T(8,128)(2,1)}), bf16[1024,512]{1,0:T(8,128)(2,1)}) %all-reduce.6.cloned.1.call-update) | async-done | bytes 1048592 | tf_op jit(solution)/shard_map/while/body/eval_jaxpr/psum | solution.py:114
  241.1 3.1 fusion.140
  250.0 2.3 fusion.131
  254.1 2.1 fusion.133
  257.1 7.0 fusion.135
  265.8 4.5 fusion.137
  270.3 14.3 %fusion.139 = bf16[2,64,1024]{2,1,0:T(8,128)(2,1)} fusion(bf16[1024,2,64]{0,2,1:T(8,128)(2,1)} %bitcast.151, f32[2,1024,1024]{1,2,0:T(8,128)} %fusion.137, f32[2,1024,1024]{1,2,0:T(8,128)} %get-tuple-element.559, f32[2,1024]{1,0:T(2,128)S(1)} %get-tuple-element.560), kind=kOutput, calls=%fused_computation.32.clone.1 | convolution fusion | flops 283249664 | bytes 17309696 | tf_op jit(solution)/shard_map/while/body/eval_jaxpr/hqk,khe->qhe/dot_general | solution.py:56
  284.6 14.3 %fusion.138 = bf16[2,64,1024]{2,1,0:T(8,128)(2,1)} fusion(bf16[1024,2,64]{0,2,1:T(8,128)(2,1)} %bitcast.149, f32[2,1024,1024]{1,2,0:T(8,128)} %fusion.137, f32[2,1024,1024]{1,2,0:T(8,128)} %get-tuple-element.559, f32[2,1024]{1,0:T(2,128)S(1)} %get-tuple-element.560), kind=kOutput, calls=%fused_computation.33.clone.1 | convolution fusion | flops 283249664 | bytes 17309696 | tf_op jit(solution)/shard_map/while/body/eval_jaxpr/hqk,qhe->khe/dot_general | solution.py:59
  298.9 5.6 fusion.136
  309.9 2.9 bitcast_convert_fusion.2
  312.9 4.9 fusion.145
  318.5 2.5 fusion.146
  323.0 3.1 fusion.144
  326.1 37.5 %all-reduce.6.cloned.1.call-done = bf16[1024,512]{1,0:T(8,128)(2,1)} async-done(((bf16[1024,512]{1,0:T(8,128)(2,1)}), bf16[1024,512]{1,0:T(8,128)(2,1)}) %all-reduce.6.cloned.1.call-update) | async-done | bytes 1048592 | tf_op jit(solution)/shard_map/while/body/eval_jaxpr/psum | solution.py:114
  363.6 3.1 fusion.140
  372.5 2.6 fusion.131
  376.9 2.1 fusion.133
  379.9 7.0 fusion.135
  388.6 4.5 fusion.137
  393.1 14.3 %fusion.139 = bf16[2,64,1024]{2,1,0:T(8,128)(2,1)} fusion(bf16[1024,2,64]{0,2,1:T(8,128)(2,1)} %bitcast.151, f32[2,1024,1024]{1,2,0:T(8,128)} %fusion.137, f32[2,1024,1024]{1,2,0:T(8,128)} %get-tuple-element.559, f32[2,1024]{1,0:T(2,128)S(1)} %get-tuple-element.560), kind=kOutput, calls=%fused_computation.32.clone.1 | convolution fusion | flops 283249664 | bytes 17309696 | tf_op jit(solution)/shard_map/while/body/eval_jaxpr/hqk,khe->qhe/dot_general | solution.py:56
  407.4 14.3 %fusion.138 = bf16[2,64,1024]{2,1,0:T(8,128)(2,1)} fusion(bf16[1024,2,64]{0,2,1:T(8,128)(2,1)} %bitcast.149, f32[2,1024,1024]{1,2,0:T(8,128)} %fusion.137, f32[2,1024,1024]{1,2,0:T(8,128)} %get-tuple-element.559, f32[2,1024]{1,0:T(2,128)S(1)} %get-tuple-element.560), kind=kOutput, calls=%fused_computation.33.clone.1 | convolution fusion | flops 283249664 | bytes 17309696 | tf_op jit(solution)/shard_map/while/body/eval_jaxpr/hqk,qhe->khe/dot_general | solution.py:59
  421.7 5.6 fusion.136
  432.7 2.9 bitcast_convert_fusion.2
  435.7 4.9 fusion.145
  441.3 2.5 fusion.146
  445.8 3.1 fusion.144
  448.9 37.1 %all-reduce.6.cloned.1.call-done = bf16[1024,512]{1,0:T(8,128)(2,1)} async-done(((bf16[1024,512]{1,0:T(8,128)(2,1)}), bf16[1024,512]{1,0:T(8,128)(2,1)}) %all-reduce.6.cloned.1.call-update) | async-done | bytes 1048592 | tf_op jit(solution)/shard_map/while/body/eval_jaxpr/psum | solution.py:114
  486.0 3.1 fusion.140
  492.3 2.1 broadcast_multiply_fusion.3
  497.8 157.6 %psum.34 = f32[128]{0:T(128)} all-reduce(f32[128]{0:T(128)S(1)} %broadcast_multiply_fusion.5), channel_id=1, replica_groups=mesh['curve'=64,'mp'=4] {'curve'}, use_global_device_ids=true, to_apply=%region_12.13 | all-reduce | flops 128 | bytes 1024 | tf_op jit(solution)/shard_map/psum | solution.py:176
  656.1 2.9 convert_add_fusion
  659.0 9.7 scatter_custom_fusion
  668.7 2.4 convert_element_type.151
  671.1 434.3 %all-reduce.4.cloned.1.call-done = (f32[512,3,128]{2,0,1:T(8,128)}, f32[128,512]{1,0:T(8,128)}) async-done(((f32[512,3,128]{2,0,1:T(8,128)}, f32[128,512]{1,0:T(8,128)}), (f32[512,3,128]{2,0,1:T(8,128)}, f32[128,512]{1,0:T(8,128)})) %all-reduce.4.cloned.1.call-update) | async-done | bytes 1048592 | tf_op jit(solution)/shard_map/psum | solution.py:176
  (251 shorter events, 71.0 us)
Async XLA Ops:
  8.0 1.9 copy-start
  47.6 69.6 %copy-start.31 = (s32[2]{0:T(128)S(1)}, s32[2]{0:T(128)}, u32[]{:S(2)}) copy-start(s32[2]{0:T(128)} %constant.152) | copy-start | bytes 28
  47.6 81.1 %copy-start.9 = (bf16[512,3,128]{2,0,1:T(8,128)(2,1)S(1)}, bf16[512,3,128]{2,0,1:T(8,128)(2,1)}, u32[]{:S(2)}) copy-start(bf16[512,3,128]{2,0,1:T(8,128)(2,1)} %param.14) | copy-start | bytes 1179652
  47.6 70.3 %collective-permute-start.1 = (bf16[512,512]{1,0:T(8,128)(2,1)}, bf16[512,512]{1,0:T(8,128)(2,1)}, u32[]{:S(2)}, u32[]{:S(2)}) collective-permute-start(bf16[512,512]{1,0:T(8,128)(2,1)} %slice_bitcast_fusion.1), channel_id=1, source_target_pairs={{0,252},{4,0},{8,4},{12,8},{16,12},{20,16},{24,20},{28,24},{32,28}... | collective-permute-start | bytes 1572872 | tf_op jit(solution)/shard_map/ppermute | solution.py:17
  115.0 13.7 %collective-permute-start = (bf16[512,512]{1,0:T(8,128)(2,1)}, bf16[512,512]{1,0:T(8,128)(2,1)}, u32[]{:S(2)}, u32[]{:S(2)}) collective-permute-start(bf16[512,512]{1,0:T(8,128)(2,1)} %slice_bitcast_fusion.2), channel_id=1, source_target_pairs={{0,252},{4,0},{8,4},{12,8},{16,12},{20,16},{24,20},{28,24},{32,28}... | collective-permute-start | bytes 1572872 | tf_op jit(solution)/shard_map/ppermute | solution.py:17
  128.7 112.4 %all-reduce.6.cloned.1.call-start = ((), (), s32[]{:S(2)}) async-start(), calls=%async_computation.1 | async-start | bytes 2097152 | tf_op jit(solution)/shard_map/while/body/eval_jaxpr/psum | solution.py:114
  131.4 2.5 copy-start.1
  134.0 3.6 copy-start.18
  138.6 7.0 copy-start.32
  147.3 4.5 copy-start.11
  200.0 2.5 copy-start.5
  202.4 1.9 copy-start.12
  202.4 1.9 copy-start.13
  202.4 2.0 copy-start.14
  202.4 2.0 copy-start.19
  202.4 2.0 copy-start.25
  241.1 3.6 copy-start.8
  247.2 116.3 %all-reduce.6.cloned.1.call-start = ((), (), s32[]{:S(2)}) async-start(), calls=%async_computation.1 | async-start | bytes 2097152 | tf_op jit(solution)/shard_map/while/body/eval_jaxpr/psum | solution.py:114
  250.0 2.5 copy-start.1
  252.5 3.6 copy-start.18
  257.1 7.0 copy-start.32
  265.8 4.5 copy-start.11
  318.5 2.5 copy-start.5
  321.0 1.8 copy-start.12
  321.0 1.9 copy-start.13
  321.0 2.0 copy-start.14
  321.0 2.0 copy-start.19
  321.0 2.0 copy-start.25
  363.5 3.6 copy-start.8
  369.7 116.3 %all-reduce.6.cloned.1.call-start = ((), (), s32[]{:S(2)}) async-start(), calls=%async_computation.1 | async-start | bytes 2097152 | tf_op jit(solution)/shard_map/while/body/eval_jaxpr/psum | solution.py:114
  372.5 2.8 copy-start.1
  375.3 3.6 copy-start.18
  379.9 7.0 copy-start.32
  388.6 4.5 copy-start.11
  441.3 2.5 copy-start.5
  443.8 1.9 copy-start.13
  443.8 2.0 copy-start.14
  443.8 2.0 copy-start.19
  443.8 2.0 copy-start.25
  486.0 3.6 copy-start.8
  492.2 3.9 copy-start.21
  492.2 3.9 copy-start.23
  492.2 3.9 copy-start.30
  492.2 4.0 copy-start.26
  492.2 4.0 copy-start.17
  492.2 5.6 copy-start.29
  492.2 613.1 %all-reduce.4.cloned.1.call-start = ((), (), s32[]{:S(2)}) async-start(), calls=%async_computation | async-start | bytes 2097152 | tf_op jit(solution)/shard_map/psum | solution.py:176
  496.3 159.2 %collective-permute-start.2 = (bf16[512,128]{1,0:T(8,128)(2,1)S(1)}, bf16[512,128]{1,0:T(8,128)(2,1)S(1)}, u32[]{:S(2)}, u32[]{:S(2)}) collective-permute-start(bf16[512,128]{1,0:T(8,128)(2,1)S(1)} %copy-done.17), channel_id=1, source_target_pairs={{0,4},{4,8},{8,12},{12,16},{16,20},{20,24},{24,28},{28,32},{32,36}... | collective-permute-start | bytes 393224 | tf_op jit(solution)/shard_map/ppermute | solution.py:17
  (36 other events, 41.9 us)
Sparse Core Ops, SparseCore 0:
  194.5 46.5 all-reduce.5
  313.0 50.4 all-reduce.5
  435.8 50.1 all-reduce.5
Sparse Core Ops, SparseCore 1:
  496.2 609.1 all-reduce.3
where the time goes:
time: 1120 us
  waiting for transfers between devices  554 us (49%)
  matrix products  188 us (17%)
  blocking collectives  158 us (14%)
  local copies, waits for them, and re-layouts  147 us (13%)
  other arithmetic  38.3 us (3%)
  between operations  15.3 us (1%)
    psum x1, waiting for transfers between devices, shards(): lax.psum((qkv_total * factor, out_total * factor, gain_total * factor), '...  434 us
    psum x1, blocking collectives, shards(): lax.psum((qkv_total * factor, out_total * factor, gain_total * factor), '...  158 us
    psum x3, waiting for transfers between devices, run_patch(): lax.psum(group_normed.astype(jnp.float32).astype(jnp.bfloat16), 'mp')  109 us
    gather x1, local copies, waits for them, and re-layouts, shards(): series_x = points[slot_index, order]  56.8 us
    dot_general x3, matrix products, attention_terms(): jnp.einsum('hqk,qhe->khe', grad_scores, queries, preferred_element_type=j...  42.9 us
    dot_general x3, matrix products, attention_terms(): jnp.einsum('hqk,khe->qhe', grad_scores, key_rows, preferred_element_type=...  42.9 us
    gather x1, local copies, waits for them, and re-layouts, shards(): series_dy = cotangent[slot_index, order]  35.8 us
  transfers between devices with their start and end apart: 7, of which 5 were waited for; matrix products, arithmetic and copies ran while one was open for 10% of the time, Pallas kernels for 0%

commit v1 on v0

v1 whole, which is shorter than its diff:
```python
import functools
import math

import jax
import jax.numpy as jnp
from jax import lax
from jax.experimental import pallas as pl
from jax.experimental.pallas import tpu as pltpu
from jax.sharding import PartitionSpec as P

D = 512
HEADS = 8
HEAD = D // HEADS
EPSILON = 1e-05
LOG2E = math.log2(math.e)

F32 = jnp.float32
BF16 = jnp.bfloat16
NT = (((1,), (1,)), ((), ()))
VMEM = pl.BlockSpec(memory_space=pltpu.VMEM)
SMEM = pl.BlockSpec(memory_space=pltpu.SMEM)


def mm(a, b):
    return jnp.dot(a, b, preferred_element_type=F32)


def mm_nt(a, b):
    return lax.dot_general(a, b, NT, preferred_element_type=F32)


def params(mib):
    return pltpu.CompilerParams(vmem_limit_bytes=mib * 1024 * 1024)


def cost(flops, bytes_accessed):
    return pl.CostEstimate(flops=flops, bytes_accessed=bytes_accessed, transcendentals=0)


def one_hot_rows(places, patch):
    count = places.shape[1]
    column = jnp.broadcast_to(places, (128, count)).T
    lanes = lax.broadcasted_iota(jnp.int32, (count, 128), 1)
    return jnp.concatenate(
        [(column == lanes + 128 * b).astype(BF16) for b in range(patch // 128)], axis=1
    )


def halo_kernel(scal, order, points, cotangent, out):
    rows = out.shape[1]
    start = pl.multiple_of(scal[0] * rows, rows)
    chosen = one_hot_rows(order[0:1, pl.ds(start, rows)], points.shape[1])
    out[0] = mm(chosen, points[0]).astype(BF16)
    out[1] = mm(chosen, cotangent[0]).astype(BF16)


def norm_half(x, gain, own):
    values = x.astype(F32)
    mean = jnp.mean(values, axis=1, keepdims=True)
    centre = values - mean
    inverse = lax.rsqrt(jnp.mean(centre * centre, axis=1, keepdims=True) + EPSILON)
    normed = (centre * inverse * gain).astype(BF16)
    unit = ((own.astype(F32) - mean) * inverse).T
    inverse_row = jnp.broadcast_to(inverse, (x.shape[0], 128)).T[0:8]
    return normed, unit, inverse_row


def patch_core(nrm, dy, w3, wt, wo, prj, kr, vr, dat, acc, gp, att, wacc):
    rows = nrm.shape[0]
    block = 256
    prj[...] = mm_nt(wt[...], nrm[...]).astype(BF16)
    kr[...] = mm(nrm[...], w3[1]).astype(BF16)
    vr[...] = mm(nrm[...], w3[2]).astype(BF16)
    dat[...] = mm_nt(wo[...], dy[...]).astype(BF16)
    acc[...] = jnp.zeros_like(acc)
    scale = HEAD ** (-0.5) * LOG2E
    zeros = jnp.zeros((HEAD, block), BF16)

    def pad(x, h):
        return jnp.concatenate([x, zeros] if h == 0 else [zeros, x], axis=0)

    def step(i, carry):
        cols = pl.ds(pl.multiple_of(i * block, block), block)
        for h in range(2):
            lo = h * HEAD
            q = prj[lo:lo + HEAD, cols]
            scores = mm(kr[...], pad(q, h))
            high = jnp.max(scores, axis=0, keepdims=True) * scale
            expos = jnp.exp2(scores * scale - high)
            recip = 1.0 / jnp.sum(expos, axis=0, keepdims=True)
            low = expos.astype(BF16)
            attended = mm(prj[256 + lo:256 + lo + HEAD, :], low) * recip
            att[lo:lo + HEAD, cols] = attended.astype(BF16)
            grad = dat[lo:lo + HEAD, cols].astype(F32) * recip
            inner = jnp.sum(grad * attended, axis=0, keepdims=True)
            grad = grad.astype(BF16)
            grad_probs = mm(vr[...], pad(grad, h))
            grad_scores = (expos * (grad_probs - inner)).astype(BF16)
            dq = mm(prj[128 + lo:128 + lo + HEAD, :], grad_scores) * (HEAD ** (-0.5))
            gp[lo:lo + HEAD, cols] = dq.astype(BF16)
            acc[lo:lo + HEAD, :] += mm_nt(q, grad_scores)
            acc[128 + lo:128 + lo + HEAD, :] += mm_nt(grad, low)
        return carry

    lax.fori_loop(0, rows // block, step, 0)
    gp[128:256, :] = (acc[0:128] * (HEAD ** (-0.5))).astype(BF16)
    gp[256:384, :] = acc[128:256].astype(BF16)
    wacc[0:384] += mm(gp[...], nrm[...])
    wacc[384:512] += mm(att[...], dy[...])


def second_stat(gp, prj):
    return jnp.sum(gp[...].astype(F32) * prj[...].astype(F32), axis=0, keepdims=True)


def local_kernel(scal, order, points, cotangent, gain, w3, wo,
                 gp_i, unit_i, stat_i, wacc, nrm_l, dy_l, unit_l, stat_l, wt,
                 nrm, dy, own, prj, kr, vr, dat, acc, att):
    count = scal[2]
    patch = points.shape[1]
    half = patch // 2
    first = pl.multiple_of(scal[1] * 128, 128)
    for t in range(3):
        wt[128 * t:128 * t + 128, :] = w3[t].astype(F32).T.astype(BF16)
    wacc[...] = jnp.zeros_like(wacc)

    def gather(slot, side, into_x, into_dy, at):
        chosen = one_hot_rows(order[pl.ds(slot, 1), half * side:half * side + half], patch)
        x = mm(chosen, points[slot]).astype(BF16)
        into_dy[at:at + half, :] = mm(chosen, cotangent[slot]).astype(BF16)
        own[...] = x
        normed, unit, inverse = norm_half(x, gain[...], own[:, pl.ds(first, 128)])
        into_x[at:at + half, :] = normed
        return unit, inverse

    def interior(p, carry):
        for side in range(2):
            unit, inverse = gather(p + side, 1 - side, nrm, dy, half * side)
            unit_i[p, :, half * side:half * side + half] = unit
            stat_i[p, :, half * side:half * side + half] = inverse
        gp_p = gp_i.at[p]
        patch_core(nrm, dy, w3, wt, wo, prj, kr, vr, dat, acc, gp_p, att, wacc)
        stat_i[p, 1:2, :] = second_stat(gp_p, prj)
        return carry

    lax.fori_loop(0, count - 1, interior, 0)
    unit, inverse = gather(count - 1, 1, nrm_l, dy_l, 0)
    unit_l[...] = unit
    stat_l[...] = inverse


def last_kernel(factor, scal, mine, other, nrm_l, dy_l, unit_l, stat_l, wacc_i, gain, w3, wt, wo,
                gp, unit_o, stat_o, pieces, gain_o,
                nrm, dy, own, prj, kr, vr, dat, acc, att, wacc):
    half = nrm_l.shape[0]
    part = half // 2
    first = pl.multiple_of(scal[1] * 128, 128)
    is_first = scal[0] == 0
    nrm[0:half, :] = nrm_l[...]
    dy[0:half, :] = dy_l[...]
    unit_o[:, 0:half] = unit_l[...]
    stat_o[:, 0:half] = stat_l[...]
    own_at = pl.multiple_of(scal[0] * part, part)
    other_at = pl.multiple_of((1 - scal[0]) * part, part)
    own[pl.ds(own_at, part), :] = mine[0]
    own[pl.ds(other_at, part), :] = other[0]
    dy[pl.ds(half + own_at, part), :] = mine[1]
    dy[pl.ds(half + other_at, part), :] = other[1]
    normed, unit, inverse = norm_half(own[...], gain[...], own[:, pl.ds(first, 128)])
    nrm[half:, :] = normed
    unit_o[:, half:] = unit
    stat_o[:, half:] = inverse
    wacc[...] = wacc_i[...]
    patch_core(nrm, dy, w3, wt, wo, prj, kr, vr, dat, acc, gp, att, wacc)
    stat_o[1:2, :] = second_stat(gp, prj)
    total = wacc[0:384] * factor
    gain_row = jnp.sum(total * wt[...].astype(F32), axis=0, keepdims=True) / gain[...]
    gain_o[...] = jnp.broadcast_to(gain_row, gain_o.shape)
    for r in range(16):
        for c in range(4):
            block = wacc[32 * r:32 * r + 32, 128 * c:128 * c + 128]
            pieces[4 * r + c] = (block * factor).astype(BF16)


def spread_kernel(scal, gp_i, gp_l, stat_i, stat_l, gain_row, w3, gain_column,
                  send, keep, stats, grads):
    core, count = scal[0], scal[2]
    patch = gp_l.shape[1]
    weights = jnp.concatenate([w3[0], w3[1], w3[2]], axis=1)
    stats[:, 3 * patch:] = gain_row[...]

    def one(p, gp, stat):
        cols = pl.ds(pl.multiple_of(p * patch, patch), patch)
        grads[...] = mm(weights, gp).astype(BF16)
        mean = jnp.sum(grads[...].astype(F32) * gain_column[...], axis=0, keepdims=True)
        stats[0:1, cols] = mean
        stats[1:2, cols] = stat
        for j in range(2):
            kept = pl.multiple_of((2 * j + core) * 128, 128)
            sent = pl.multiple_of((2 * j + 1 - core) * 128, 128)
            keep[j, :, cols] = grads[pl.ds(kept, 128), :]
            send[j, :, cols] = grads[pl.ds(sent, 128), :]

    def interior(p, carry):
        one(p, gp_i[p], stat_i[p, 1:2, :])
        return carry

    lax.fori_loop(0, count - 1, interior, 0)
    one(2, gp_l[...], stat_l[1:2, :])


def pair_kernel(scal, keep, received, stats, stats_received, send, kept, stats_o):
    far = scal[3]
    send[...] = (keep[1 - far].astype(F32) + received[1 - far].astype(F32)).astype(BF16)
    kept[...] = keep[far].astype(F32) + received[far].astype(F32)
    stats_o[...] = stats[...] + stats_received[...]


def branch_kernel(scal, kept, received, stats, stats_received, unit_i, unit_l, stat_i, stat_l,
                  gain_column, branch, back, gain_o):
    count = scal[2]
    patch = unit_l.shape[1]
    first = pl.multiple_of(scal[1] * 128, 128)
    own_gain = gain_column[pl.ds(first, 128), :]

    def one(p, unit, inverse):
        cols = pl.ds(pl.multiple_of(p * patch, patch), patch)
        scaled = (kept[:, cols] + received[:, cols].astype(F32)) * own_gain
        mean = (stats[0:1, cols] + stats_received[0:1, cols]) * (1.0 / D)
        slope = (stats[1:2, cols] + stats_received[1:2, cols]) * (1.0 / D)
        return (inverse * (scaled - mean - unit * slope)).astype(BF16)

    def interior(p, carry):
        branch[p] = one(p, unit_i[p], stat_i[p, 0:1, :])
        return carry

    lax.fori_loop(0, count - 1, interior, 0)
    last = one(2, unit_l[...], stat_l[0:1, :])
    branch[2] = last
    back[...] = last[:, patch // 2:]
    at = pl.ds(pl.multiple_of(3 * patch + first, 128), 128)
    gain_o[...] = stats[:, at] + stats_received[:, at]


def total_kernel(received, gain, out):
    def add(i, total):
        return total + received[i].astype(F32)

    total = lax.fori_loop(0, received.shape[0], add, jnp.zeros(received.shape[1:], F32), unroll=8)
    low = total.astype(BF16)
    gain_low = gain[...].astype(BF16)

    def put(i, carry):
        out[i, 0:32, :] = low
        out[i, 32:40, :] = gain_low
        return carry

    lax.fori_loop(0, received.shape[0], put, 0, unroll=8)


def place_kernel(scal, order, cotangent, branch, returned, out, placed):
    slot = pl.program_id(0)
    count = scal[2]
    patch = out.shape[1]
    half = patch // 2

    @pl.when(slot >= count)
    def _():
        out[...] = cotangent[...]

    @pl.when(slot < count)
    def _():
        @pl.when(slot == 0)
        def _():
            placed[:, 0:half] = returned[...]

        @pl.when(slot > 0)
        def _():
            placed[:, 0:half] = branch[jnp.maximum(slot - 1, 0), :, half:]

        placed[:, half:] = branch[jnp.where(slot + 1 < count, slot, 2), :, 0:half]
        places = order[pl.ds(slot, 1), :]
        rows = 256
        for r in range(patch // rows):
            index = lax.broadcasted_iota(jnp.int32, (rows, patch), 0) + rows * r
            chosen = (index == places).astype(BF16)
            moved = mm_nt(chosen, placed[...])
            own = cotangent[0, rows * r:rows * r + rows, :].astype(F32)
            out[0, rows * r:rows * r + rows, :] = (own + moved).astype(BF16)


def finish_kernel(received, qkv, out, gain):
    gain[...] = jnp.sum(received[:, 32:40, :].astype(F32), axis=0)
    for t in range(3):
        for c in range(4):
            block = jnp.concatenate(
                [received[4 * (4 * t + r) + c, 0:32, :].astype(F32) for r in range(4)], axis=0
            )
            qkv[t, 128 * c:128 * c + 128, :] = block.T
    for r in range(4):
        for c in range(4):
            out[32 * r:32 * r + 32, 128 * c:128 * c + 128] = received[
                4 * (12 + r) + c, 0:32, :
            ].astype(F32)


def shards(points, order, counts, cotangent, norm_gain, w_qkv, w_out):
    slots, patch, width = points.shape
    half = patch // 2
    curve = lax.axis_size("curve")
    model_part = lax.axis_index("mp")
    core = model_part % 2
    far = model_part // 2
    scal = jnp.stack([core, model_part, counts[0], far]).astype(jnp.int32)
    gain_row = norm_gain.reshape(1, width)
    gain_column = norm_gain.reshape(width, 1)
    w3 = jnp.transpose(w_qkv, (1, 0, 2))
    sds = jax.ShapeDtypeStruct

    def passed(x, by):
        return lax.ppermute(x, "curve", [(i, (i + by) % curve) for i in range(curve)])

    def swapped(x, bit):
        return lax.ppermute(x, "mp", [(i, i ^ bit) for i in range(4)])

    slot_block = pl.BlockSpec((1, patch, width), lambda i: (0, 0, 0))
    head = pl.pallas_call(
        halo_kernel,
        grid=(1,),
        in_specs=[SMEM, pl.BlockSpec((slots, patch), lambda i: (0, 0)), slot_block, slot_block],
        out_specs=pl.BlockSpec((2, half // 2, width), lambda i: (0, 0, 0)),
        out_shape=sds((2, half // 2, width), BF16),
        compiler_params=params(32),
        name="halo",
    )(scal, order, points, cotangent)
    mine = passed(head, -1)

    work = [
        pltpu.VMEM((patch, width), BF16),
        pltpu.VMEM((patch, width), BF16),
        pltpu.VMEM((half, width), BF16),
        pltpu.VMEM((384, patch), BF16),
        pltpu.VMEM((patch, 128), BF16),
        pltpu.VMEM((patch, 128), BF16),
        pltpu.VMEM((128, patch), BF16),
        pltpu.VMEM((256, patch), F32),
        pltpu.VMEM((128, patch), BF16),
    ]
    gp_i, unit_i, stat_i, wacc, nrm_l, dy_l, unit_l, stat_l, wt = pl.pallas_call(
        local_kernel,
        in_specs=[SMEM] + [VMEM] * 6,
        out_specs=[VMEM] * 9,
        out_shape=[
            sds((slots - 1, 384, patch), BF16),
            sds((slots - 1, 128, patch), F32),
            sds((slots - 1, 8, patch), F32),
            sds((512, width), F32),
            sds((half, width), BF16),
            sds((half, width), BF16),
            sds((128, half), F32),
            sds((8, half), F32),
            sds((384, width), BF16),
        ],
        scratch_shapes=work,
        compiler_params=params(56),
        cost_estimate=cost(8 * 10**9, 16 * 10**6),
        name="local",
    )(scal, order, points, cotangent, gain_row, w3, w_out)

    other = swapped(mine, 1)
    factor = 1.0 / math.sqrt(curve * slots * patch)
    gp_l, unit_l, stat_l, pieces, gain_part = pl.pallas_call(
        functools.partial(last_kernel, factor),
        in_specs=[SMEM] + [VMEM] * 11,
        out_specs=[VMEM] * 5,
        out_shape=[
            sds((384, patch), BF16),
            sds((128, patch), F32),
            sds((8, patch), F32),
            sds((64, 32, 128), BF16),
            sds((8, width), F32),
        ],
        scratch_shapes=work + [pltpu.VMEM((512, width), F32)],
        compiler_params=params(56),
        cost_estimate=cost(4 * 10**9, 8 * 10**6),
        name="last",
    )(scal, mine, other, nrm_l, dy_l, unit_l, stat_l, wacc, gain_row, w3, wt, w_out)

    received = lax.all_to_all(pieces, "curve", 0, 0)

    lanes = slots * patch
    send, keep, stats = pl.pallas_call(
        spread_kernel,
        in_specs=[SMEM] + [VMEM] * 7,
        out_specs=[VMEM] * 3,
        out_shape=[
            sds((2, 128, lanes), BF16),
            sds((2, 128, lanes), BF16),
            sds((8, lanes + width), F32),
        ],
        scratch_shapes=[pltpu.VMEM((width, patch), BF16)],
        compiler_params=params(48),
        cost_estimate=cost(2 * 10**9, 8 * 10**6),
        name="spread",
    )(scal, gp_i, gp_l, stat_i, stat_l, gain_part, w3, gain_column)
    near, near_stats = swapped(send, 1), swapped(stats, 1)
    send, kept, stats = pl.pallas_call(
        pair_kernel,
        in_specs=[SMEM] + [VMEM] * 4,
        out_specs=[VMEM] * 3,
        out_shape=[sds((128, lanes), BF16), sds((128, lanes), F32), sds((8, lanes + width), F32)],
        compiler_params=params(48),
        name="pair",
    )(scal, keep, near, stats, near_stats)
    away, away_stats = swapped(send, 2), swapped(stats, 2)
    branch, back, gain_own = pl.pallas_call(
        branch_kernel,
        in_specs=[SMEM] + [VMEM] * 9,
        out_specs=[VMEM] * 3,
        out_shape=[sds((slots, 128, patch), BF16), sds((128, half), BF16), sds((8, 128), F32)],
        compiler_params=params(48),
        name="branch",
    )(scal, kept, away, stats, away_stats, unit_i, unit_l, stat_i, stat_l, gain_column)
    returned = passed(back, 1)

    totals = pl.pallas_call(
        total_kernel,
        in_specs=[VMEM] * 2,
        out_specs=VMEM,
        out_shape=sds((64, 40, 128), BF16),
        compiler_params=params(32),
        name="total",
    )(received, gain_own)
    gathered = lax.all_to_all(totals, "curve", 0, 0)

    grad_points = pl.pallas_call(
        place_kernel,
        grid_spec=pltpu.PrefetchScalarGridSpec(
            num_scalar_prefetch=1,
            grid=(slots,),
            in_specs=[
                pl.BlockSpec((slots, patch), lambda i, s: (0, 0)),
                pl.BlockSpec((1, patch, 128), lambda i, s: (i, 0, s[1])),
                pl.BlockSpec((slots, 128, patch), lambda i, s: (0, 0, 0)),
                pl.BlockSpec((128, half), lambda i, s: (0, 0)),
            ],
            out_specs=pl.BlockSpec((1, patch, 128), lambda i, s: (i, 0, 0)),
            scratch_shapes=[pltpu.VMEM((128, patch), BF16)],
        ),
        out_shape=sds((slots, patch, 128), BF16),
        compiler_params=params(32),
        name="place",
    )(scal, order, cotangent, branch, returned)

    grad_qkv, grad_out, grad_gain = pl.pallas_call(
        finish_kernel,
        in_specs=[VMEM],
        out_specs=[VMEM] * 3,
        out_shape=[sds((3, width, 128), F32), sds((128, width), F32), sds((8, 128), F32)],
        compiler_params=params(32),
        name="finish",
    )(gathered)
    return grad_points, grad_gain[0], jnp.transpose(grad_qkv, (1, 0, 2)), grad_out


def solution(mesh):
    in_specs = (
        P("curve", None, None),
        P("curve", None),
        P("curve"),
        P("curve", None, None),
        P(),
        P(None, None, "mp"),
        P("mp", None),
    )
    out_specs = (P("curve", None, "mp"), P("mp"), P(None, None, "mp"), P("mp", None))
    return jax.shard_map(shards, mesh=mesh, in_specs=in_specs, out_specs=out_specs, check_vma=False)
```

time: 1120 us -> 170 us (0.15)
  waiting for transfers between devices: 554 us -> 56.8 us
  matrix products: 188 us -> 0 us
  blocking collectives: 158 us -> 0 us
  local copies, waits for them, and re-layouts: 147 us -> 12.1 us
  Pallas kernels: 0 us -> 68.6 us
  other arithmetic: 38.3 us -> 0.08 us
  starting transfers between devices: 11.2 us -> 30.2 us
  between operations: 15.3 us -> 1.49 us
    psum x4 -> x0, waiting for transfers between devices: 544 us -> none  [the longest x1 434 us: shards(): lax.psum((qkv_total * factor, out_total * factor, gain_total * factor), '...]
    dot_general x27 -> x0, matrix products: 160 us -> none  [the longest x3 42.9 us: attention_terms(): jnp.einsum('hqk,qhe->khe', grad_scores, queries, preferred_element_type=j...]
    psum x1 -> x0, blocking collectives: 158 us -> none  [shards(): lax.psum((qkv_total * factor, out_total * factor, gain_total * factor), '...]
    gather x2 -> x0, local copies, waits for them, and re-layouts: 92.6 us -> none  [the longest x1 56.8 us: shards(): series_x = points[slot_index, order]]
    pallas_call x0 -> x9, Pallas kernels: none -> 68.6 us  [the longest x1 36.8 us: shards(): pl.pallas_call(local_kernel, in_specs=[SMEM] + [VMEM] * 6, out_specs=[VME...]
    ppermute x3 -> x7, waiting for transfers between devices: 10.9 us -> 56.8 us  [the longest x2 31.9 us: passed(): lax.ppermute(x, 'curve', [(i, (i + by) % curve) for i in range(curve)])]
    sub x3 -> x0, matrix products: 21 us -> none  [attention_terms(): expos = jnp.exp(scores - highest)]
    another operation x9 -> x0, local copies, waits for them, and re-layouts: 16.2 us -> none  [attention_terms(): jnp.stack([grad_queries, grad_keys, grad_values])]
  transfers between devices with their start and end apart: 7 -> 9, of which waited for: 5 -> 4; matrix products, arithmetic and copies ran while one was open for 10% -> 0% of each run, Pallas kernels for 0% -> 25%
where the time goes in v1:
time: 170 us; the launch traced here: 169 us
  Pallas kernels  68.6 us (40%)
  waiting for transfers between devices  56.8 us (33%)
  starting transfers between devices  30.2 us (18%)
  local copies, waits for them, and re-layouts  12.1 us (7%)
    pallas_call x1, Pallas kernels, shards(): pl.pallas_call(local_kernel, in_specs=[SMEM] + [VMEM] * 6, out_specs=[VME...  36.8 us
    ppermute x2, waiting for transfers between devices, passed(): lax.ppermute(x, 'curve', [(i, (i + by) % curve) for i in range(curve)])  31.9 us
    ppermute x5, waiting for transfers between devices, swapped(): return lax.ppermute(x, 'mp', [(i, i ^ bit) for i in range(4)])  24.9 us
    pallas_call x1, Pallas kernels, shards(): pl.pallas_call(functools.partial(last_kernel, factor), in_specs=[SMEM] +...  16.4 us
    unnamed x48, local copies, waits for them, and re-layouts  11.5 us
    ppermute x2, starting transfers between devices, passed(): lax.ppermute(x, 'curve', [(i, (i + by) % curve) for i in range(curve)])  10.4 us
    all_to_all x1, starting transfers between devices, shards(): gathered = lax.all_to_all(totals, 'curve', 0, 0)  9.91 us
    all_to_all x1, starting transfers between devices, shards(): received = lax.all_to_all(pieces, 'curve', 0, 0)  5.91 us
  transfers between devices with their start and end apart: 9, of which 4 were waited for; matrix products, arithmetic and copies ran while one was open for 0% of the time, Pallas kernels for 25%

profile of v1, /device:TPU:16, one launch (start us, length us, event | category | flops | bytes accessed | tf_op | source)
XLA Modules:
  0.0 169.3 jit_solution(2829949236616311908)
XLA Ops:
  1.3 0.1 pad_add_fusion.scal
  1.4 1.9 %copy-done = bf16[3,1024,512]{2,1,0:T(8,128)(2,1)S(1)} copy-done((bf16[3,1024,512]{2,1,0:T(8,128)(2,1)S(1)}, bf16[3,1024,512]{2,1,0:T(8,128)(2,1)}, u32[]{:S(2)}) %copy-start) | copy-done | bytes 3145752
  3.3 1.9 %copy-done.2 = bf16[3,1024,512]{2,1,0:T(8,128)(2,1)S(1)} copy-done((bf16[3,1024,512]{2,1,0:T(8,128)(2,1)S(1)}, bf16[3,1024,512]{2,1,0:T(8,128)(2,1)}, u32[]{:S(2)}) %copy-start.2) | copy-done | bytes 3145752
  5.2 0.7 copy-done.10
  5.9 1.3 halo.1
  7.2 0.0 copy-done.14
  7.2 8.8 %collective-permute-start = (bf16[2,256,512]{2,1,0:T(8,128)(2,1)S(1)}, bf16[2,256,512]{2,1,0:T(8,128)(2,1)S(1)}, u32[]{:S(2)}, u32[]{:S(2)}) collective-permute-start(bf16[2,256,512]{2,1,0:T(8,128)(2,1)S(1)} %halo.1), channel_id=1, source_target_pairs={{0,252},{4,0},{8,4},{12,8},{16,12},{20,16},{24,20},{28,24},{32,28}... | collective-permute-start | bytes 1572872 | tf_op jit(solution)/shard_map/ppermute | solution.py:321
  16.1 0.1 copy.11.gain_column
  16.2 11.0 %collective-permute-done.mine = bf16[2,256,512]{2,1,0:T(8,128)(2,1)S(1)} collective-permute-done((bf16[2,256,512]{2,1,0:T(8,128)(2,1)S(1)}, bf16[2,256,512]{2,1,0:T(8,128)(2,1)S(1)}, u32[]{:S(2)}, u32[]{:S(2)}) %collective-permute-start) | collective-permute-done | bytes 524320 | tf_op jit(solution)/shard_map/ppermute | solution.py:321
  27.3 0.0 collective-permute-start.1
  27.3 36.8 %local.1 = (bf16[2,384,1024]{2,1,0:T(8,128)(2,1)}, f32[2,128,1024]{2,1,0:T(8,128)}, f32[2,8,1024]{2,1,0:T(8,128)}, f32[512,512]{1,0:T(8,128)}, bf16[512,512]{1,0...) custom-call(s32[4]{0:T(128)} %copy-done.14, ...), custom_call_target="tpu_custom_call" | custom-call | flops 8000000000 | bytes 16000000 | tf_op jit(solution)/shard_map/local/pallas_call | solution.py:349
  64.1 0.0 collective-permute-done.1.other
  64.1 0.0 copy-start.23
  64.1 0.8 copy-done.23
  64.9 16.4 %last.1 = (bf16[384,1024]{1,0:T(8,128)(2,1)}, f32[128,1024]{1,0:T(8,128)}, f32[8,1024]{1,0:T(8,128)}, bf16[64,32,128]{2,1,0:T(8,128)(2,1)}, f32[8,512]{1,0:T(8,128)}) custom-call(s32[4]{0:T(128)} %copy-done.14, bf16[2,256,512]{2,1,0:T(8,128)(2,1)} %copy-done.22, bf16[2,256,512]{2,1,0:T(8,128)(2,1)} %copy-done.23, bf16[512,512]{1,0:T(8,128)(2,1)} %get-tuple-element.31.nrm_l, ...), custom_call_target="tpu_custom_call" | custom-call | flops 4000000000 | bytes 8000000 | tf_op jit(solution)/shard_map/last/pallas_call | solution.py:372
  81.4 0.7 copy-done.12
  82.1 1.1 copy-done.19
  83.3 0.7 copy-done.20
  84.0 5.0 %spread.1 = (bf16[2,128,3072]{2,1,0:T(8,128)(2,1)}, bf16[2,128,3072]{2,1,0:T(8,128)(2,1)S(1)}, f32[8,3584]{1,0:T(8,128)S(1)}) custom-call(s32[4]{0:T(128)S(1)} %copy-done.15, bf16[2,384,1024]{2,1,0:T(8,128)(2,1)} %get-tuple-element.30.gp_i, bf16[384,1024]{1,0:T(8,128)(2,1)S(1)} %copy-done.19, f32[2,8,1024]{2,1,0:T(8,128)S(1)} %copy-done.8, ...), custom_call_target="tpu_custom_call" | custom-call | flops 2000000000 | bytes 8000000 | tf_op jit(solution)/shard_map/spread/pallas_call | solution.py:392
  88.9 0.3 collective-permute-start.2
  89.2 5.9 %all-to-all-start = ((bf16[64,32,128]{2,1,0:T(8,128)(2,1)}), bf16[64,32,128]{2,1,0:T(8,128)(2,1)}, u32[]{:S(2)}, u32[]{:S(2)}) async-start(bf16[64,32,128]{2,1,0:T(8,128)(2,1)} %get-tuple-element.51), calls=%async_computation | async-start | bytes 1048576 | tf_op jit(solution)/shard_map/all_to_all | solution.py:389
  95.1 0.1 collective-permute-start.3
  95.2 1.3 collective-permute-done.3.stats_received
  96.6 0.0 collective-permute-done.2.received
  96.6 0.9 pair.1
  97.5 0.4 collective-permute-start.4
  97.9 3.2 %collective-permute-start.5 = (f32[8,3584]{1,0:T(8,128)S(1)}, f32[8,3584]{1,0:T(8,128)S(1)}, u32[]{:S(2)}, u32[]{:S(2)}) collective-permute-start(f32[8,3584]{1,0:T(8,128)S(1)} %get-tuple-element.46.stats), channel_id=1, source_target_pairs={{0,2},{1,3},{2,0},{3,1},{4,6},{5,7},{6,4},{7,5},{8,10},{9,11},{10,... | collective-permute-start | bytes 344072 | tf_op jit(solution)/shard_map/ppermute | solution.py:324
  101.1 23.5 %collective-permute-done.5.stats_received = f32[8,3584]{1,0:T(8,128)S(1)} collective-permute-done((f32[8,3584]{1,0:T(8,128)S(1)}, f32[8,3584]{1,0:T(8,128)S(1)}, u32[]{:S(2)}, u32[]{:S(2)}) %collective-permute-start.5) | collective-permute-done | bytes 114720 | tf_op jit(solution)/shard_map/ppermute | solution.py:324
  124.6 0.0 collective-permute-done.4.received
  124.6 0.0 copy-done.4
  124.7 0.0 copy-start.1
  124.7 1.0 branch.1
  125.7 0.0 copy-start.5
  125.7 0.9 copy-done.5
  126.6 0.7 copy-done.17
  127.3 0.0 all-to-all-done.received
  127.3 1.2 total.1
  128.5 0.0 copy-start.3
  128.5 0.9 copy-done.3
  129.4 9.9 %all-to-all-start.1 = ((bf16[64,40,128]{2,1,0:T(8,128)(2,1)}), bf16[64,40,128]{2,1,0:T(8,128)(2,1)}, u32[]{:S(2)}, u32[]{:S(2)}) async-start(bf16[64,40,128]{2,1,0:T(8,128)(2,1)} %copy-done.3), calls=%async_computation.1 | async-start | bytes 1310720 | tf_op jit(solution)/shard_map/all_to_all | solution.py:434
  139.3 0.0 copy-done.18
  139.3 1.6 collective-permute-start.6
  140.9 20.9 %collective-permute-done.6.returned = bf16[128,512]{1,0:T(8,128)(2,1)S(1)} collective-permute-done((bf16[128,512]{1,0:T(8,128)(2,1)S(1)}, bf16[128,512]{1,0:T(8,128)(2,1)S(1)}, u32[]{:S(2)}, u32[]{:S(2)}) %collective-permute-start.6) | collective-permute-done | bytes 131104 | tf_op jit(solution)/shard_map/ppermute | solution.py:321
  161.8 1.1 copy-done.6
  162.9 3.7 %place.1 = bf16[3,1024,128]{2,1,0:T(8,128)(2,1)} custom-call(s32[4]{0:T(128)S(1)} %copy-done.15, s32[3,1024]{1,0:T(4,128)S(1)} %copy-done.11, bf16[3,1024,512]{2,1,0:T(8,128)(2,1)S(1)} %copy-done.1, bf16[3,128,1024]{2,1,0:T(8,128)(2,1)S(1)} %copy-done.6, bf16[128,512]{1,0:T(8,128)(2,1)S(1)} %collective-permute-done.6.returned), custom_call_target="tpu_custom_call" | custom-call | tf_op jit(solution)/shard_map/place/pallas_call | solution.py:436
  166.6 0.0 all-to-all-done.1.received
  166.6 2.2 %finish.1 = (f32[3,512,128]{2,1,0:T(8,128)}, f32[128,512]{1,0:T(8,128)}, f32[8,128]{1,0:T(8,128)S(1)}) custom-call(bf16[64,40,128]{2,1,0:T(8,128)(2,1)} %all-to-all-done.1.received), custom_call_target="tpu_custom_call" | custom-call | tf_op jit(solution)/shard_map/finish/pallas_call | solution.py:455
  168.8 0.5 slice_bitcast_fusion
  (30 shorter events, 0.1 us)
Async XLA Ops:
  1.4 1.9 %copy-start = (bf16[3,1024,512]{2,1,0:T(8,128)(2,1)S(1)}, bf16[3,1024,512]{2,1,0:T(8,128)(2,1)}, u32[]{:S(2)}) copy-start(bf16[3,1024,512]{2,1,0:T(8,128)(2,1)} %cotangent.5) | copy-start | bytes 9437188
  3.3 1.9 %copy-start.2 = (bf16[3,1024,512]{2,1,0:T(8,128)(2,1)S(1)}, bf16[3,1024,512]{2,1,0:T(8,128)(2,1)}, u32[]{:S(2)}) copy-start(bf16[3,1024,512]{2,1,0:T(8,128)(2,1)} %points.3) | copy-start | bytes 9437188
  5.2 0.7 copy-start.10
  5.9 1.3 copy-start.14
  5.9 10.2 %copy-start.21 = (f32[512]{0:T(512)S(1)}, f32[512]{0:T(512)}, u32[]{:S(2)}) copy-start(f32[512]{0:T(512)} %param.11) | copy-start | bytes 6148
  7.2 20.0 %collective-permute-start = (bf16[2,256,512]{2,1,0:T(8,128)(2,1)S(1)}, bf16[2,256,512]{2,1,0:T(8,128)(2,1)S(1)}, u32[]{:S(2)}, u32[]{:S(2)}) collective-permute-start(bf16[2,256,512]{2,1,0:T(8,128)(2,1)S(1)} %halo.1), channel_id=1, source_target_pairs={{0,252},{4,0},{8,4},{12,8},{16,12},{20,16},{24,20},{28,24},{32,28}... | collective-permute-start | bytes 1572872 | tf_op jit(solution)/shard_map/ppermute | solution.py:321
  27.3 36.8 %copy-start.22 = (bf16[2,256,512]{2,1,0:T(8,128)(2,1)}, bf16[2,256,512]{2,1,0:T(8,128)(2,1)S(1)}, u32[]{:S(2)}) copy-start(bf16[2,256,512]{2,1,0:T(8,128)(2,1)S(1)} %collective-permute-done.mine) | copy-start | bytes 1572868
  27.3 36.9 %collective-permute-start.1 = (bf16[2,256,512]{2,1,0:T(8,128)(2,1)S(1)}, bf16[2,256,512]{2,1,0:T(8,128)(2,1)S(1)}, u32[]{:S(2)}, u32[]{:S(2)}) collective-permute-start(bf16[2,256,512]{2,1,0:T(8,128)(2,1)S(1)} %collective-permute-done.mine), channel_id=1, source_target_pairs={{0,1},{1,0},{2,3},{3,2},{4,5},{5,4},{6,7},{7,6},{8,9},{9,8},{10,11... | collective-permute-start | bytes 1572872 | tf_op jit(solution)/shard_map/ppermute | solution.py:324
  64.1 0.8 copy-start.23
  64.9 16.4 %copy-start.8 = (f32[2,8,1024]{2,1,0:T(8,128)S(1)}, f32[2,8,1024]{2,1,0:T(8,128)}, u32[]{:S(2)}) copy-start(f32[2,8,1024]{2,1,0:T(8,128)} %get-tuple-element.38.stat_i) | copy-start | bytes 196612
  64.9 16.4 %copy-start.15 = (s32[4]{0:T(128)S(1)}, s32[4]{0:T(128)}, u32[]{:S(2)}) copy-start(s32[4]{0:T(128)} %copy-done.14) | copy-start | bytes 52
  64.9 16.4 %copy-start.16 = (bf16[512,3,128]{2,0,1:T(8,128)(2,1)S(1)}, bf16[512,3,128]{2,0,1:T(8,128)(2,1)}, u32[]{:S(2)}) copy-start(bf16[512,3,128]{2,0,1:T(8,128)(2,1)} %param.12) | copy-start | bytes 1179652
  81.4 0.8 copy-start.12
  82.1 1.1 copy-start.19
  83.3 0.7 copy-start.20
  88.9 7.6 %collective-permute-start.2 = (bf16[2,128,3072]{2,1,0:T(8,128)(2,1)}, bf16[2,128,3072]{2,1,0:T(8,128)(2,1)S(1)}, u32[]{:S(2)}, u32[]{:S(2)}) collective-permute-start(bf16[2,128,3072]{2,1,0:T(8,128)(2,1)} %get-tuple-element.42), channel_id=1, source_target_pairs={{0,1},{1,0},{2,3},{3,2},{4,5},{5,4},{6,7},{7,6},{8,9},{9,8},{10,11... | collective-permute-start | bytes 4718600 | tf_op jit(solution)/shard_map/ppermute | solution.py:324
  89.2 38.0 %all-to-all-start = ((bf16[64,32,128]{2,1,0:T(8,128)(2,1)}), bf16[64,32,128]{2,1,0:T(8,128)(2,1)}, u32[]{:S(2)}, u32[]{:S(2)}) async-start(bf16[64,32,128]{2,1,0:T(8,128)(2,1)} %get-tuple-element.51), calls=%async_computation | async-start | bytes 1048576 | tf_op jit(solution)/shard_map/all_to_all | solution.py:389
  95.1 1.4 collective-permute-start.3
  96.6 28.1 %copy-start.4 = (f32[2,128,1024]{2,1,0:T(8,128)S(1)}, f32[2,128,1024]{2,1,0:T(8,128)}, u32[]{:S(2)}) copy-start(f32[2,128,1024]{2,1,0:T(8,128)} %get-tuple-element.47.unit_i) | copy-start | bytes 3145732
  96.6 28.1 %copy-start.7 = (f32[128,1024]{1,0:T(8,128)S(1)}, f32[128,1024]{1,0:T(8,128)}, u32[]{:S(2)}) copy-start(f32[128,1024]{1,0:T(8,128)} %get-tuple-element.48.unit_l) | copy-start | bytes 1572868
  96.6 28.1 %copy-start.9 = (f32[2,8,1024]{2,1,0:T(8,128)S(1)}, f32[2,8,1024]{2,1,0:T(8,128)}, u32[]{:S(2)}) copy-start(f32[2,8,1024]{2,1,0:T(8,128)} %get-tuple-element.38.stat_i) | copy-start | bytes 196612
  96.6 28.1 %copy-start.13 = (f32[8,1024]{1,0:T(8,128)S(1)}, f32[8,1024]{1,0:T(8,128)}, u32[]{:S(2)}) copy-start(f32[8,1024]{1,0:T(8,128)} %get-tuple-element.39.stat_l) | copy-start | bytes 98308
  97.5 27.2 %collective-permute-start.4 = (bf16[128,3072]{1,0:T(8,128)(2,1)S(1)}, bf16[128,3072]{1,0:T(8,128)(2,1)S(1)}, u32[]{:S(2)}, u32[]{:S(2)}) collective-permute-start(bf16[128,3072]{1,0:T(8,128)(2,1)S(1)} %get-tuple-element.45), channel_id=1, source_target_pairs={{0,2},{1,3},{2,0},{3,1},{4,6},{5,7},{6,4},{7,5},{8,10},{9,11},{10,... | collective-permute-start | bytes 2359304 | tf_op jit(solution)/shard_map/ppermute | solution.py:324
  97.9 26.7 %collective-permute-start.5 = (f32[8,3584]{1,0:T(8,128)S(1)}, f32[8,3584]{1,0:T(8,128)S(1)}, u32[]{:S(2)}, u32[]{:S(2)}) collective-permute-start(f32[8,3584]{1,0:T(8,128)S(1)} %get-tuple-element.46.stats), channel_id=1, source_target_pairs={{0,2},{1,3},{2,0},{3,1},{4,6},{5,7},{6,4},{7,5},{8,10},{9,11},{10,... | collective-permute-start | bytes 344072 | tf_op jit(solution)/shard_map/ppermute | solution.py:324
  124.7 37.1 %copy-start.1 = (bf16[3,1024,512]{2,1,0:T(8,128)(2,1)S(1)}, bf16[3,1024,512]{2,1,0:T(8,128)(2,1)}, u32[]{:S(2)}) copy-start(bf16[3,1024,512]{2,1,0:T(8,128)(2,1)} %cotangent.5) | copy-start | bytes 9437188
  125.7 0.9 copy-start.5
  126.6 0.7 copy-start.17
  127.3 34.5 %copy-start.11 = (s32[3,1024]{1,0:T(4,128)S(1)}, s32[3,1024]{1,0:T(4,128)}, u32[]{:S(2)}) copy-start(s32[3,1024]{1,0:T(4,128)} %order.5) | copy-start | bytes 36868
  127.3 12.0 %copy-start.18 = (bf16[128,512]{1,0:T(8,128)(2,1)S(1)}, bf16[128,512]{1,0:T(8,128)(2,1)}, u32[]{:S(2)}) copy-start(bf16[128,512]{1,0:T(8,128)(2,1)} %copy-done.17) | copy-start | bytes 393220
  128.5 0.9 copy-start.3
  129.4 37.2 %all-to-all-start.1 = ((bf16[64,40,128]{2,1,0:T(8,128)(2,1)}), bf16[64,40,128]{2,1,0:T(8,128)(2,1)}, u32[]{:S(2)}, u32[]{:S(2)}) async-start(bf16[64,40,128]{2,1,0:T(8,128)(2,1)} %copy-done.3), calls=%async_computation.1 | async-start | bytes 1310720 | tf_op jit(solution)/shard_map/all_to_all | solution.py:434
  139.3 22.5 %collective-permute-start.6 = (bf16[128,512]{1,0:T(8,128)(2,1)S(1)}, bf16[128,512]{1,0:T(8,128)(2,1)S(1)}, u32[]{:S(2)}, u32[]{:S(2)}) collective-permute-start(bf16[128,512]{1,0:T(8,128)(2,1)S(1)} %copy-done.18), channel_id=1, source_target_pairs={{0,4},{4,8},{8,12},{12,16},{16,20},{20,24},{24,28},{28,32},{32,36}... | collective-permute-start | bytes 393224 | tf_op jit(solution)/shard_map/ppermute | solution.py:321
  161.8 1.1 copy-start.6

commit v2 on v1

v2 whole, which is shorter than its diff:
```python
import functools
import math

import jax
import jax.numpy as jnp
from jax import lax
from jax.experimental import pallas as pl
from jax.experimental.pallas import tpu as pltpu
from jax.sharding import PartitionSpec as P

D = 512
HEADS = 8
HEAD = D // HEADS
EPSILON = 1e-05
SCALE = HEAD ** (-0.5) * math.log2(math.e)

F32 = jnp.float32
BF16 = jnp.bfloat16
NT = (((1,), (1,)), ((), ()))
VMEM = pl.BlockSpec(memory_space=pltpu.VMEM)
SMEM = pl.BlockSpec(memory_space=pltpu.SMEM)
ANY = pl.BlockSpec(memory_space=pl.ANY)


def mm(a, b):
    return jnp.dot(a, b, preferred_element_type=F32)


def mm_nt(a, b):
    return lax.dot_general(a, b, NT, preferred_element_type=F32)


def params(mib):
    return pltpu.CompilerParams(vmem_limit_bytes=mib * 1024 * 1024)


def cost(flops, bytes_accessed):
    return pl.CostEstimate(flops=flops, bytes_accessed=bytes_accessed, transcendentals=0)


def one_hot_rows(places, patch):
    count = places.shape[1]
    column = jnp.broadcast_to(places, (128, count)).T
    lanes = lax.broadcasted_iota(jnp.int32, (count, 128), 1)
    return jnp.concatenate(
        [(column == lanes + 128 * b).astype(BF16) for b in range(patch // 128)], axis=1
    )


def halo_kernel(scal, order, first_x, first_dy, last_x, last_dy, pull, push, chosen):
    rows = pull.shape[1]
    patch = first_x.shape[1]

    @pl.when(pl.program_id(0) == 0)
    def _():
        for k, slot, base in ((0, 0, 0), (1, order.shape[0] - 1, patch // 2)):
            at = pl.ds(pl.multiple_of(base + scal[0] * rows, rows), rows)
            chosen[k] = one_hot_rows(order[slot:slot + 1, at], patch)

    pull[0] = mm(chosen[0], first_x[0]).astype(BF16)
    pull[1] = mm(chosen[0], first_dy[0]).astype(BF16)
    push[0] = mm(chosen[1], last_x[0]).astype(BF16)
    push[1] = mm(chosen[1], last_dy[0]).astype(BF16)


def norm_half(x, gain, own):
    values = x.astype(F32)
    mean = jnp.mean(values, axis=1, keepdims=True)
    centre = values - mean
    inverse = lax.rsqrt(jnp.mean(centre * centre, axis=1, keepdims=True) + EPSILON)
    normed = (centre * inverse * gain).astype(BF16)
    unit = ((own.astype(F32) - mean) * inverse).T.astype(BF16)
    inverse_row = jnp.broadcast_to(inverse, (x.shape[0], 128)).T[0:8]
    return normed, unit, inverse_row


def project(nrm, dy, w3, wt, wo, prj, kr, vr, dat):
    prj[0:128, :] = (mm_nt(wt[0:128, :], nrm[...]) * SCALE).astype(BF16)
    prj[128:384, :] = mm_nt(wt[128:384, :], nrm[...]).astype(BF16)
    kr[...] = mm(nrm[...], w3[1]).astype(BF16)
    vr[...] = mm(nrm[...], w3[2]).astype(BF16)
    dat[...] = mm_nt(wo[...], dy[...]).astype(BF16)


def attend(prj, kr, vr, dat, gp, att):
    zeros = jnp.zeros((HEAD, prj.shape[1]), BF16)

    def pad(x, h):
        return jnp.concatenate([x, zeros] if h == 0 else [zeros, x], axis=0)

    def soft(scores):
        expos = jnp.exp2(scores - jnp.max(scores, axis=0, keepdims=True))
        recip = 1.0 / jnp.sum(expos, axis=0, keepdims=True)
        return expos, expos.astype(BF16), recip

    def middle(lo, expos, low, recip):
        attended = mm(prj[256 + lo:256 + lo + HEAD, :], low) * recip
        att[lo:lo + HEAD, :] = attended.astype(BF16)
        grad = dat[lo:lo + HEAD, :].astype(F32) * recip
        inner = jnp.sum(grad * attended, axis=0, keepdims=True)
        grad = grad.astype(BF16)
        grad_probs = mm(vr[...], pad(grad, lo // HEAD))
        return grad, (expos * (grad_probs - inner)).astype(BF16)

    def end(lo, low, grad, grad_scores):
        dq = mm(prj[128 + lo:128 + lo + HEAD, :], grad_scores) * (HEAD ** (-0.5))
        gp[lo:lo + HEAD, :] = dq.astype(BF16)
        dk = mm_nt(prj[lo:lo + HEAD, :], grad_scores) * (HEAD ** (-0.5) / SCALE)
        gp[128 + lo:128 + lo + HEAD, :] = dk.astype(BF16)
        gp[256 + lo:256 + lo + HEAD, :] = mm_nt(grad, low).astype(BF16)

    heads = (0, HEAD)
    scores = [mm(kr[...], pad(prj[lo:lo + HEAD, :], lo // HEAD)) for lo in heads]
    softs = [soft(x) for x in scores]
    middles = [middle(lo, *x) for lo, x in zip(heads, softs)]
    for lo, x, y in zip(heads, softs, middles):
        end(lo, x[1], *y)


def patch_core(core, p, nrm, dy, w3, wt, wo, gain_column, send, keep, stats,
               prj, kr, vr, dat, att, wacc, gp, grads, done):
    project(nrm, dy, w3, wt, wo, prj, kr, vr, dat)
    attend(prj, kr, vr, dat, gp, att)
    patch = gp.shape[1]
    cols = pl.ds(pl.multiple_of(p * patch, patch), patch)
    weights = jnp.concatenate([w3[0], w3[1], w3[2]], axis=1)
    grads[...] = mm(weights, gp[...]).astype(BF16)
    copies = []
    for j in range(2):
        for k, (block, into) in enumerate(((2 * j + 1 - core, send), (2 * j + core, keep))):
            rows = pl.ds(pl.multiple_of(block * 128, 128), 128)
            copies.append(
                pltpu.make_async_copy(grads.at[rows], into.at[j, :, cols], done.at[2 * j + k])
            )
            copies[-1].start()
    wacc[0:384] += mm(gp[...], nrm[...])
    wacc[384:512] += mm(att[...], dy[...])
    stats[0:1, cols] = jnp.sum(grads[...].astype(F32) * gain_column[...], axis=0, keepdims=True)
    stats[1:2, cols] = second_stat(gp, prj)
    for copy in copies:
        copy.wait()


def second_stat(gp, prj):
    product = gp[...].astype(F32) * prj[...].astype(F32)
    queries = jnp.sum(product[0:128], axis=0, keepdims=True) * (1.0 / SCALE)
    return queries + jnp.sum(product[128:384], axis=0, keepdims=True)


def gather_rows(scal, order, points, cotangent, gain, own, slot, side, into_x, into_dy):
    patch = points.shape[1]
    half = patch // 2
    first = pl.multiple_of(scal[1] * 128, 128)
    chosen = one_hot_rows(order[pl.ds(slot, 1), half * side:half * side + half], patch)
    x = mm(chosen, points[slot]).astype(BF16)
    into_dy[...] = mm(chosen, cotangent[slot]).astype(BF16)
    own[...] = x
    normed, unit, inverse = norm_half(x, gain[...], own[:, pl.ds(first, 128)])
    into_x[...] = normed
    return unit, inverse


def local_kernel(scal, order, points, cotangent, gain, gain_column, w3, wo,
                 send, keep, stats, unit_o, inv_o, wacc, wt, nrm_o, dy_o,
                 nrm, dy, own, *work):
    half = points.shape[1] // 2
    for t in range(3):
        wt[128 * t:128 * t + 128, :] = w3[t].astype(F32).T.astype(BF16)
    wacc[...] = jnp.zeros_like(wacc)

    def interior(p, carry):
        for side in range(2):
            rows = slice(half * side, half * side + half)
            unit, inverse = gather_rows(scal, order, points, cotangent, gain, own, p + side,
                                        1 - side, nrm.at[rows], dy.at[rows])
            unit_o[p, :, rows] = unit
            inv_o[p, :, rows] = inverse
        patch_core(scal[0], p, nrm, dy, w3, wt, wo, gain_column, send, keep, stats,
                   *work[:5], wacc, *work[5:])
        return carry

    lax.fori_loop(0, scal[2] - 1, interior, 0)

    @pl.when(scal[2] == 1)
    def _():
        for p in range(2):
            rows = slice(half * p, half * p + half)
            unit, inverse = gather_rows(scal, order, points, cotangent, gain, own, 0, 1 - p,
                                        nrm_o.at[p], dy_o.at[p])
            unit_o[p, :, rows] = unit
            inv_o[p, :, rows] = inverse


def cross_kernel(factor, scal, before, pull, pull_other, push, push_other, send_i, keep_i, stats_i,
                 unit_i, inv_i, wacc_i, nrm_i, dy_i, gain, gain_column, w3, wt, wo,
                 send, keep, stats, unit_o, inv_o, pieces, gain_o,
                 nrm, dy, own, *work_wacc):
    wacc, work = work_wacc[-1], work_wacc[:-1]
    half = nrm_i.shape[1]
    part = half // 2
    first = pl.multiple_of(scal[1] * 128, 128)
    light = scal[2] == 1
    stats[...] = stats_i[...]
    unit_o[...] = unit_i[...]
    inv_o[...] = inv_i[...]
    wacc[...] = wacc_i[...]

    def cross(p, carry):
        here = pl.multiple_of(half * p, half)
        there = pl.multiple_of(half * (1 - p), half)
        nrm[pl.ds(here, half), :] = nrm_i[p]
        dy[pl.ds(here, half), :] = dy_i[p]

        def take(one, other):
            for source, core in ((one, scal[0]), (other, 1 - scal[0])):
                at = pl.multiple_of(core * part, part)
                own[pl.ds(at, part), :] = source[0]
                dy[pl.ds(pl.multiple_of(there + at, part), part), :] = source[1]

        @pl.when(p == 0)
        def _():
            take(pull, pull_other)

        @pl.when(p == 1)
        def _():
            take(push, push_other)

        normed, unit, inverse = norm_half(own[...], gain[...], own[:, pl.ds(first, 128)])
        nrm[pl.ds(there, half), :] = normed
        unit_o[p, :, pl.ds(there, half)] = unit
        inv_o[p, :, pl.ds(there, half)] = inverse
        patch_core(scal[0], p, nrm, dy, w3, wt, wo, gain_column, send, keep, stats,
                   *work[:5], wacc, *work[5:])
        return carry

    lax.fori_loop(0, jnp.where(light, jnp.where(before[0] > 1, 2, 1), 0), cross, 0)
    total = wacc[0:384] * factor
    gain_o[...] = jnp.sum(total * wt[...].astype(F32), axis=0, keepdims=True) / gain[...]
    for r in range(16):
        for c in range(4):
            block = wacc[32 * r:32 * r + 32, 128 * c:128 * c + 128]
            pieces[4 * r + c] = (block * factor).astype(BF16)


def pair_kernel(scal, keep, received, stats, stats_received, send, kept, stats_o):
    far = scal[3]
    send[...] = (keep[1 - far].astype(F32) + received[1 - far].astype(F32)).astype(BF16)
    kept[...] = (keep[far].astype(F32) + received[far].astype(F32)).astype(BF16)
    stats_o[...] = stats[...] + stats_received[...]


def branch_kernel(scal, kept, received, stats, stats_received, unit, stat, gain_column,
                  branch, back, ahead):
    half = branch.shape[2] // 2
    own_gain = gain_column[pl.ds(pl.multiple_of(scal[1] * 128, 128), 128), :]
    scaled = (kept[...].astype(F32) + received[...].astype(F32)) * own_gain
    mean = (stats[0:1, :] + stats_received[0:1, :]) * (1.0 / D)
    slope = (stats[1:2, :] + stats_received[1:2, :]) * (1.0 / D)
    rows = (stat[0, 0:1, :] * (scaled - mean - unit[0].astype(F32) * slope)).astype(BF16)
    branch[0] = rows

    @pl.when(pl.program_id(0) == 0)
    def _():
        ahead[...] = rows[:, half:]

    @pl.when(pl.program_id(0) == 1)
    def _():
        back[...] = rows[:, :half]


def total_kernel(scal, received, gain, gain_received, out):
    def add(i, total):
        return total + received[i].astype(F32)

    total = lax.fori_loop(0, received.shape[0], add, jnp.zeros(received.shape[1:], F32), unroll=8)
    low = total.astype(BF16)
    at = pl.ds(pl.multiple_of(scal[1] * 128, 128), 128)
    own_gain = jnp.broadcast_to(gain[:, at] + gain_received[:, at], (8, 128)).astype(BF16)

    def put(i, carry):
        out[i, 0:32, :] = low
        out[i, 32:40, :] = own_gain
        return carry

    lax.fori_loop(0, received.shape[0], put, 0, unroll=8)


def place_kernel(scal, order, before, cotangent, branch, from_before, from_after, out, placed):
    slot = pl.program_id(0)
    count = scal[2]
    patch = out.shape[1]
    half = patch // 2

    @pl.when(slot >= count)
    def _():
        out[...] = cotangent[...]

    @pl.when(slot < count)
    def _():
        local = before[0] > 1

        @pl.when(jnp.logical_and(slot == 0, jnp.logical_not(local)))
        def _():
            placed[:, 0:half] = from_before[...]

        @pl.when(jnp.logical_and(slot == 0, local))
        def _():
            placed[:, 0:half] = branch[1, :, half:]

        @pl.when(slot > 0)
        def _():
            placed[:, 0:half] = branch[jnp.maximum(slot - 1, 0), :, half:]

        @pl.when(slot < 2)
        def _():
            placed[:, half:] = branch[jnp.minimum(slot, 1), :, 0:half]

        @pl.when(slot == 2)
        def _():
            placed[:, half:] = from_after[...]

        places = order[pl.ds(slot, 1), :]
        rows = 256
        for r in range(patch // rows):
            index = lax.broadcasted_iota(jnp.int32, (rows, patch), 0) + rows * r
            chosen = (index == places).astype(BF16)
            moved = mm_nt(chosen, placed[...])
            own = cotangent[0, rows * r:rows * r + rows, :].astype(F32)
            out[0, rows * r:rows * r + rows, :] = (own + moved).astype(BF16)


def finish_kernel(received, qkv, out, gain):
    gain[...] = jnp.sum(received[:, 32:40, :].astype(F32), axis=0)[0:1]
    for t in range(3):
        for c in range(4):
            block = jnp.concatenate(
                [received[4 * (4 * t + r) + c, 0:32, :].astype(F32) for r in range(4)], axis=0
            )
            qkv[t, 128 * c:128 * c + 128, :] = block.T
    for r in range(4):
        for c in range(4):
            out[32 * r:32 * r + 32, 128 * c:128 * c + 128] = received[
                4 * (12 + r) + c, 0:32, :
            ].astype(F32)


def shards(points, order, counts, cotangent, norm_gain, w_qkv, w_out):
    slots, patch, width = points.shape
    half = patch // 2
    curve = lax.axis_size("curve")
    model_part = lax.axis_index("mp")
    core = model_part % 2
    far = model_part // 2
    scal = jnp.stack([core, model_part, counts[0], far]).astype(jnp.int32)
    gain_row = norm_gain.reshape(1, width)
    gain_column = norm_gain.reshape(width, 1)
    w3 = jnp.transpose(w_qkv, (1, 0, 2))
    sds = jax.ShapeDtypeStruct

    def passed(x, by):
        return lax.ppermute(x, "curve", [(i, (i + by) % curve) for i in range(curve)])

    def swapped(x, bit):
        return lax.ppermute(x, "mp", [(i, i ^ bit) for i in range(4)])

    first_block = pl.BlockSpec((1, patch, width // 2), lambda i: (0, 0, i))
    last_block = pl.BlockSpec((1, patch, width // 2), lambda i: (slots - 1, 0, i))
    part_block = pl.BlockSpec((2, half // 2, width // 2), lambda i: (0, 0, i))
    pull, push = pl.pallas_call(
        halo_kernel,
        grid=(2,),
        in_specs=[SMEM, pl.BlockSpec((slots, patch), lambda i: (0, 0)),
                  first_block, first_block, last_block, last_block],
        out_specs=[part_block] * 2,
        out_shape=[sds((2, half // 2, width), BF16)] * 2,
        scratch_shapes=[pltpu.VMEM((2, half // 2, patch), BF16)],
        compiler_params=params(60),
        name="halo",
    )(scal, order, points, cotangent, points, cotangent)
    counts, pull = lax.optimization_barrier((counts, pull))
    before = passed(counts, 1)
    pull, push = passed(pull, -1), passed(push, 1)
    scal_local, before = lax.optimization_barrier((scal, before))

    work = [
        pltpu.VMEM((patch, width), BF16),
        pltpu.VMEM((patch, width), BF16),
        pltpu.VMEM((half, width), BF16),
        pltpu.VMEM((384, patch), BF16),
        pltpu.VMEM((patch, 128), BF16),
        pltpu.VMEM((patch, 128), BF16),
        pltpu.VMEM((128, patch), BF16),
        pltpu.VMEM((128, patch), BF16),
        pltpu.VMEM((384, patch), BF16),
        pltpu.VMEM((width, patch), BF16),
        pltpu.SemaphoreType.DMA((4,)),
    ]
    lanes = 2 * patch
    shared = [
        sds((2, 128, lanes), BF16),
        sds((2, 128, lanes), BF16),
        sds((2, lanes), F32),
        sds((2, 128, patch), BF16),
        sds((2, 8, patch), F32),
    ]
    send, keep, stats, unit, inverse, wacc, wt, nrm, dy = pl.pallas_call(
        local_kernel,
        in_specs=[SMEM] + [VMEM] * 7,
        out_specs=[ANY] * 2 + [VMEM] * 7,
        out_shape=shared + [
            sds((512, width), F32),
            sds((384, width), BF16),
            sds((2, half, width), BF16),
            sds((2, half, width), BF16),
        ],
        scratch_shapes=work,
        compiler_params=params(60),
        cost_estimate=cost(16 * 10**9, 16 * 10**6),
        name="local",
    )(scal_local, order, points, cotangent, gain_row, gain_column, w3, w_out)
    pull, push, wacc = lax.optimization_barrier((pull, push, wacc))

    factor = 1.0 / math.sqrt(curve * slots * patch)
    send, keep, stats, unit, inverse, pieces, gain_part = pl.pallas_call(
        functools.partial(cross_kernel, factor),
        in_specs=[SMEM] * 2 + [VMEM] * 4 + [ANY] * 2 + [VMEM] * 11,
        out_specs=[ANY] * 2 + [VMEM] * 5,
        out_shape=shared + [sds((64, 32, 128), BF16), sds((1, width), F32)],
        scratch_shapes=work + [pltpu.VMEM((512, width), F32)],
        input_output_aliases={6: 0, 7: 1},
        compiler_params=params(56),
        cost_estimate=cost(4 * 10**9, 8 * 10**6),
        name="cross",
    )(scal, before, pull, swapped(pull, 1), push, swapped(push, 1), send, keep, stats, unit,
      inverse, wacc, nrm, dy, gain_row, gain_column, w3, wt, w_out)

    received = lax.all_to_all(pieces, "curve", 0, 0)
    gain_part = gain_part + swapped(gain_part, 1)
    gain_far = swapped(gain_part, 2)

    def whole(*shape):
        return pl.BlockSpec(shape, lambda i: (0,) * len(shape))

    def by_patch(*shape):
        return pl.BlockSpec((1,) + shape, lambda i: (i,) + (0,) * len(shape))

    def by_lanes(*shape):
        return pl.BlockSpec(shape + (patch,), lambda i: (0,) * len(shape) + (i,))

    near, near_stats = swapped(send, 1), swapped(stats, 1)
    send, kept, stats = pl.pallas_call(
        pair_kernel,
        grid=(2,),
        in_specs=[SMEM, by_lanes(2, 128), by_lanes(2, 128), by_lanes(2), by_lanes(2)],
        out_specs=[by_lanes(128), by_lanes(128), by_lanes(2)],
        out_shape=[sds((128, lanes), BF16), sds((128, lanes), BF16), sds((2, lanes), F32)],
        compiler_params=params(16),
        cost_estimate=cost(1000, 1000),
        name="pair",
    )(scal, keep, near, stats, near_stats)
    send, gain_far = lax.optimization_barrier((send, gain_far))
    away, away_stats = swapped(send, 2), swapped(stats, 2)
    branch, back, ahead = pl.pallas_call(
        branch_kernel,
        grid=(2,),
        in_specs=[SMEM, by_lanes(128), by_lanes(128), by_lanes(2), by_lanes(2),
                  by_patch(128, patch), by_patch(8, patch), whole(width, 1)],
        out_specs=[by_patch(128, patch), whole(128, half), whole(128, half)],
        out_shape=[sds((2, 128, patch), BF16), sds((128, half), BF16), sds((128, half), BF16)],
        compiler_params=params(16),
        cost_estimate=cost(10**10, 1000),
        name="branch",
    )(scal, kept, away, stats, away_stats, unit, inverse, gain_column)
    from_before, from_after = passed(ahead, 1), passed(back, -1)

    totals = pl.pallas_call(
        total_kernel,
        in_specs=[SMEM] + [VMEM] * 3,
        out_specs=VMEM,
        out_shape=sds((64, 40, 128), BF16),
        compiler_params=params(16),
        name="total",
    )(scal, received, gain_part, gain_far)
    gathered = lax.all_to_all(totals, "curve", 0, 0)

    grad_points = pl.pallas_call(
        place_kernel,
        grid_spec=pltpu.PrefetchScalarGridSpec(
            num_scalar_prefetch=1,
            grid=(slots,),
            in_specs=[
                pl.BlockSpec((slots, patch), lambda i, s: (0, 0)),
                SMEM,
                pl.BlockSpec((1, patch, 128), lambda i, s: (i, 0, s[1])),
                pl.BlockSpec((2, 128, patch), lambda i, s: (0, 0, 0)),
                pl.BlockSpec((128, half), lambda i, s: (0, 0)),
                pl.BlockSpec((128, half), lambda i, s: (0, 0)),
            ],
            out_specs=pl.BlockSpec((1, patch, 128), lambda i, s: (i, 0, 0)),
            scratch_shapes=[pltpu.VMEM((128, patch), BF16)],
        ),
        out_shape=sds((slots, patch, 128), BF16),
        compiler_params=params(16),
        cost_estimate=cost(10**10, 1000),
        name="place",
    )(scal, order, before, cotangent, branch, from_before, from_after)

    grad_qkv, grad_out, grad_gain = pl.pallas_call(
        finish_kernel,
        in_specs=[VMEM],
        out_specs=[VMEM] * 3,
        out_shape=[sds((3, width, 128), F32), sds((128, width), F32), sds((1, 128), F32)],
        compiler_params=params(16),
        name="finish",
    )(gathered)
    return grad_points, grad_gain.reshape(128), jnp.transpose(grad_qkv, (1, 0, 2)), grad_out


def solution(mesh):
    in_specs = (
        P("curve", None, None),
        P("curve", None),
        P("curve"),
        P("curve", None, None),
        P(),
        P(None, None, "mp"),
        P("mp", None),
    )
    out_specs = (P("curve", None, "mp"), P("mp"), P(None, None, "mp"), P("mp", None))
    return jax.shard_map(shards, mesh=mesh, in_specs=in_specs, out_specs=out_specs, check_vma=False)
```

time: 170 us -> 120 us (0.71)
  Pallas kernels: 68.6 us -> 36 us
  waiting for transfers between devices: 56.8 us -> 36.4 us
  starting transfers between devices: 30.2 us -> 41.2 us
  local copies, waits for them, and re-layouts: 12.1 us -> 3.61 us
    pallas_call x7 -> x6, Pallas kernels: 62.7 us -> 31.4 us  [the longest x1 15.7 us: shards(): pl.pallas_call(functools.partial(cross_kernel, factor), in_specs=[SMEM] *...]
    ppermute x5 -> x8, waiting for transfers between devices: 24.9 us -> 5.02 us  [swapped(): return lax.ppermute(x, 'mp', [(i, i ^ bit) for i in range(4)])]
    all_to_all x1, starting transfers between devices: 5.91 us -> 15.4 us  [shards(): received = lax.all_to_all(pieces, 'curve', 0, 0)]
    unnamed x48 -> x26, local copies, waits for them, and re-layouts: 11.5 us -> 2.75 us
    ppermute x2 -> x5, waiting for transfers between devices: 31.9 us -> 23.7 us  [passed(): lax.ppermute(x, 'curve', [(i, (i + by) % curve) for i in range(curve)])]
    all_to_all x1, waiting for transfers between devices: 0.01 us -> 7.68 us  [shards(): received = lax.all_to_all(pieces, 'curve', 0, 0)]
    ppermute x2 -> x5, starting transfers between devices: 10.4 us -> 15.2 us  [passed(): lax.ppermute(x, 'curve', [(i, (i + by) % curve) for i in range(curve)])]
    all_to_all x1, starting transfers between devices: 9.91 us -> 5.36 us  [shards(): gathered = lax.all_to_all(totals, 'curve', 0, 0)]
  transfers between devices with their start and end apart: 9 -> 15, of which waited for: 4 -> 9; matrix products, arithmetic and copies ran while one was open for 0% -> 1% of each run, Pallas kernels for 25% -> 13%
where the time goes in v2:
time: 120 us
  starting transfers between devices  41.2 us (34%)
  waiting for transfers between devices  36.4 us (30%)
  Pallas kernels  36 us (30%)
  local copies, waits for them, and re-layouts  3.61 us (3%)
  between operations  1.47 us (1%)
  other arithmetic  1.31 us (1%)
    ppermute x5, waiting for transfers between devices, passed(): lax.ppermute(x, 'curve', [(i, (i + by) % curve) for i in range(curve)])  23.7 us
    pallas_call x1, Pallas kernels, shards(): pl.pallas_call(functools.partial(cross_kernel, factor), in_specs=[SMEM] *...  15.7 us
    all_to_all x1, starting transfers between devices, shards(): received = lax.all_to_all(pieces, 'curve', 0, 0)  15.4 us
    ppermute x5, starting transfers between devices, passed(): lax.ppermute(x, 'curve', [(i, (i + by) % curve) for i in range(curve)])  15.2 us
    pallas_call x1, Pallas kernels, shards(): pl.pallas_call(local_kernel, in_specs=[SMEM] + [VMEM] * 7, out_specs=[ANY...  8.05 us
    all_to_all x1, waiting for transfers between devices, shards(): received = lax.all_to_all(pieces, 'curve', 0, 0)  7.68 us
    all_to_all x1, starting transfers between devices, shards(): gathered = lax.all_to_all(totals, 'curve', 0, 0)  5.36 us
    ppermute x8, starting transfers between devices, swapped(): return lax.ppermute(x, 'mp', [(i, i ^ bit) for i in range(4)])  5.19 us
  transfers between devices with their start and end apart: 15, of which 9 were waited for; matrix products, arithmetic and copies ran while one was open for 1% of the time, Pallas kernels for 13%

profile of v2, /device:TPU:16, one launch (start us, length us, event | category | flops | bytes accessed | tf_op | source)
XLA Modules:
  0.0 120.0 jit_solution(13343509320718704234)
XLA Ops:
  1.3 0.7 pad_add_fusion.scal
  2.0 4.1 %halo.1 = (bf16[2,256,512]{2,1,0:T(8,128)(2,1)}, bf16[2,256,512]{2,1,0:T(8,128)(2,1)}) custom-call(s32[4]{0:T(128)} %pad_add_fusion.scal, s32[3,1024]{1,0:T(4,128)} %order.5, bf16[3,1024,512]{2,1,0:T(8,128)(2,1)} %points.1, bf16[3,1024,512]{2,1,0:T(8,128)(2,1)} %cotangent.3, bf16[3,1024,512]{2,1,0:T(8,128)(2,1)} %points.1, bf16[3,1024,512]{2,1,0:T(8,128)(2,1)} %cotangent.3), custom_call_target="tpu_custom_call" | custom-call | tf_op jit(solution)/shard_map/halo/pallas_call | solution.py:369
  6.1 1.5 %collective-permute-start = (s32[1]{0:T(128)}, s32[1]{0:T(128)}, u32[]{:S(2)}, u32[]{:S(2)}) collective-permute-start(s32[1]{0:T(128)} %param.9), channel_id=1, source_target_pairs={{0,4},{4,8},{8,12},{12,16},{16,20},{20,24},{24,28},{28,32},{32,36}... | collective-permute-start | bytes 20 | tf_op jit(solution)/shard_map/ppermute | solution.py:361
  7.6 7.4 %collective-permute-start.1 = (bf16[2,256,512]{2,1,0:T(8,128)(2,1)}, bf16[2,256,512]{2,1,0:T(8,128)(2,1)S(1)}, u32[]{:S(2)}, u32[]{:S(2)}) collective-permute-start(bf16[2,256,512]{2,1,0:T(8,128)(2,1)} %get-tuple-element.43), channel_id=1, source_target_pairs={{0,252},{4,0},{8,4},{12,8},{16,12},{20,16},{24,20},{28,24},{32,28}... | collective-permute-start | bytes 1572872 | tf_op jit(solution)/shard_map/ppermute | solution.py:361
  14.9 0.0 collective-permute-start.2
  14.9 0.9 copy.13.gain_column
  15.8 0.8 collective-permute-done.before
  16.6 8.1 %local.1 = (bf16[2,128,2048]{2,1,0:T(8,128)(2,1)}, bf16[2,128,2048]{2,1,0:T(8,128)(2,1)}, f32[2,2048]{1,0:T(2,128)}, bf16[2,128,1024]{2,1,0:T(8,128)(2,1)}, f32[...) custom-call(s32[4]{0:T(128)} %pad_add_fusion.scal, ...), custom_call_target="tpu_custom_call" | custom-call | flops 16000000000 | bytes 16000000 | tf_op jit(solution)/shard_map/local/pallas_call | solution.py:406
  24.7 1.8 %collective-permute-done.1.pull = bf16[2,256,512]{2,1,0:T(8,128)(2,1)S(1)} collective-permute-done((bf16[2,256,512]{2,1,0:T(8,128)(2,1)}, bf16[2,256,512]{2,1,0:T(8,128)(2,1)S(1)}, u32[]{:S(2)}, u32[]{:S(2)}) %collective-permute-start.1) | collective-permute-done | bytes 524320 | tf_op jit(solution)/shard_map/ppermute | solution.py:361
  26.4 6.3 %collective-permute-done.2.push = bf16[2,256,512]{2,1,0:T(8,128)(2,1)S(1)} collective-permute-done((bf16[2,256,512]{2,1,0:T(8,128)(2,1)}, bf16[2,256,512]{2,1,0:T(8,128)(2,1)S(1)}, u32[]{:S(2)}, u32[]{:S(2)}) %collective-permute-start.2) | collective-permute-done | bytes 524320 | tf_op jit(solution)/shard_map/ppermute | solution.py:361
  32.7 0.0 collective-permute-start.3
  32.7 0.5 collective-permute-start.4
  33.3 1.4 %collective-permute-done.3.pull_other = bf16[2,256,512]{2,1,0:T(8,128)(2,1)S(1)} collective-permute-done((bf16[2,256,512]{2,1,0:T(8,128)(2,1)S(1)}, bf16[2,256,512]{2,1,0:T(8,128)(2,1)S(1)}, u32[]{:S(2)}, u32[]{:S(2)}) %collective-permute-start.3) | collective-permute-done | bytes 524320 | tf_op jit(solution)/shard_map/ppermute | solution.py:364
  34.7 0.7 collective-permute-done.4.push_other
  35.4 0.0 copy-done.11
  35.4 0.7 copy-done.12
  36.2 15.7 %cross.1 = (bf16[2,128,2048]{2,1,0:T(8,128)(2,1)}, bf16[2,128,2048]{2,1,0:T(8,128)(2,1)}, f32[2,2048]{1,0:T(2,128)}, bf16[2,128,1024]{2,1,0:T(8,128)(2,1)}, f32[...) custom-call(s32[4]{0:T(128)} %pad_add_fusion.scal, ...), custom_call_target="tpu_custom_call", output_to_operand_aliasing={{0}: (6, {}), {1}: (7, {})} | custom-call | flops 4000000000 | bytes 8000000 | tf_op jit(solution)/shard_map/cross/pallas_call | solution.py:424
  51.9 0.0 copy-start.2
  51.9 0.2 collective-permute-start.5
  52.2 15.4 %all-to-all-start = ((bf16[64,32,128]{2,1,0:T(8,128)(2,1)}), bf16[64,32,128]{2,1,0:T(8,128)(2,1)S(1)}, u32[]{:S(2)}, u32[]{:S(2)}) async-start(bf16[64,32,128]{2,1,0:T(8,128)(2,1)} %get-tuple-element.71), calls=%async_computation | async-start | bytes 1048576 | tf_op jit(solution)/shard_map/all_to_all | solution.py:437
  67.6 0.1 collective-permute-start.6
  67.7 0.5 collective-permute-start.7
  68.2 1.0 collective-permute-done.7
  69.2 0.6 add.9.gain
  69.9 0.3 collective-permute-start.8
  70.2 0.0 collective-permute-done.6.stats_received
  70.2 0.0 collective-permute-done.5.received
  70.2 1.2 %copy-done.1 = bf16[2,128,2048]{2,1,0:T(8,128)(2,1)S(1)} copy-done((bf16[2,128,2048]{2,1,0:T(8,128)(2,1)S(1)}, bf16[2,128,2048]{2,1,0:T(8,128)(2,1)}, u32[]{:S(2)}) %copy-start.1) | copy-done | bytes 1048600
  71.4 0.7 copy-done.4
  72.2 1.0 pair.1
  73.1 1.8 %collective-permute-done.8.gain_received = f32[1,512]{1,0:T(1,128)S(1)} collective-permute-done((f32[1,512]{1,0:T(1,128)S(1)}, f32[1,512]{1,0:T(1,128)S(1)}, u32[]{:S(2)}, u32[]{:S(2)}) %collective-permute-start.8) | collective-permute-done | bytes 2080 | tf_op jit(solution)/shard_map/ppermute | solution.py:364
  75.0 1.5 %collective-permute-start.9 = (bf16[128,2048]{1,0:T(8,128)(2,1)S(1)}, bf16[128,2048]{1,0:T(8,128)(2,1)S(1)}, u32[]{:S(2)}, u32[]{:S(2)}) collective-permute-start(bf16[128,2048]{1,0:T(8,128)(2,1)S(1)} %get-tuple-element.64), channel_id=1, source_target_pairs={{0,2},{1,3},{2,0},{3,1},{4,6},{5,7},{6,4},{7,5},{8,10},{9,11},{10,... | collective-permute-start | bytes 1572872 | tf_op jit(solution)/shard_map/ppermute | solution.py:364
  76.5 2.1 %collective-permute-start.10 = (f32[2,2048]{1,0:T(2,128)S(1)}, f32[2,2048]{1,0:T(2,128)S(1)}, u32[]{:S(2)}, u32[]{:S(2)}) collective-permute-start(f32[2,2048]{1,0:T(2,128)S(1)} %get-tuple-element.65.stats), channel_id=1, source_target_pairs={{0,2},{1,3},{2,0},{3,1},{4,6},{5,7},{6,4},{7,5},{8,10},{9,11},{10,... | collective-permute-start | bytes 49160 | tf_op jit(solution)/shard_map/ppermute | solution.py:364
  78.5 7.7 %all-to-all-done.received = bf16[64,32,128]{2,1,0:T(8,128)(2,1)S(1)} async-done(((bf16[64,32,128]{2,1,0:T(8,128)(2,1)}), bf16[64,32,128]{2,1,0:T(8,128)(2,1)S(1)}, u32[]{:S(2)}, u32[]{:S(2)}) %all-to-all-start) | async-done | bytes 524320 | tf_op jit(solution)/shard_map/all_to_all | solution.py:437
  86.2 1.5 %total.1 = bf16[64,40,128]{2,1,0:T(8,128)(2,1)} custom-call(s32[4]{0:T(128)S(1)} %copy-done.5, bf16[64,32,128]{2,1,0:T(8,128)(2,1)S(1)} %all-to-all-done.received, f32[1,512]{1,0:T(1,128)S(1)} %add.9.gain, f32[1,512]{1,0:T(1,128)S(1)} %collective-permute-done.8.gain_received), custom_call_target="tpu_custom_call" | custom-call | tf_op jit(solution)/shard_map/total/pallas_call | solution.py:476
  87.7 5.4 %all-to-all-start.1 = ((bf16[64,40,128]{2,1,0:T(8,128)(2,1)}), bf16[64,40,128]{2,1,0:T(8,128)(2,1)S(1)}, u32[]{:S(2)}, u32[]{:S(2)}) async-start(bf16[64,40,128]{2,1,0:T(8,128)(2,1)} %total.1), calls=%async_computation.1 | async-start | bytes 1310720 | tf_op jit(solution)/shard_map/all_to_all | solution.py:484
  93.1 0.0 collective-permute-done.10.stats_received
  93.1 0.0 collective-permute-done.9.received
  93.2 0.0 copy-start
  93.2 0.0 copy-start.3
  93.2 1.0 branch.1
  94.2 1.6 %collective-permute-start.11 = (bf16[128,512]{1,0:T(8,128)(2,1)S(1)}, bf16[128,512]{1,0:T(8,128)(2,1)S(1)}, u32[]{:S(2)}, u32[]{:S(2)}) collective-permute-start(bf16[128,512]{1,0:T(8,128)(2,1)S(1)} %get-tuple-element.69), channel_id=1, source_target_pairs={{0,4},{4,8},{8,12},{12,16},{16,20},{20,24},{24,28},{28,32},{32,36}... | collective-permute-start | bytes 393224 | tf_op jit(solution)/shard_map/ppermute | solution.py:361
  95.9 4.7 %collective-permute-start.12 = (bf16[128,512]{1,0:T(8,128)(2,1)S(1)}, bf16[128,512]{1,0:T(8,128)(2,1)S(1)}, u32[]{:S(2)}, u32[]{:S(2)}) collective-permute-start(bf16[128,512]{1,0:T(8,128)(2,1)S(1)} %get-tuple-element.70), channel_id=1, source_target_pairs={{0,252},{4,0},{8,4},{12,8},{16,12},{20,16},{24,20},{28,24},{32,28}... | collective-permute-start | bytes 393224 | tf_op jit(solution)/shard_map/ppermute | solution.py:361
  100.5 14.8 %collective-permute-done.11.from_before = bf16[128,512]{1,0:T(8,128)(2,1)S(1)} collective-permute-done((bf16[128,512]{1,0:T(8,128)(2,1)S(1)}, bf16[128,512]{1,0:T(8,128)(2,1)S(1)}, u32[]{:S(2)}, u32[]{:S(2)}) %collective-permute-start.11) | collective-permute-done | bytes 131104 | tf_op jit(solution)/shard_map/ppermute | solution.py:361
  115.4 0.0 collective-permute-done.12.from_after
  115.4 3.5 %place.1 = bf16[3,1024,128]{2,1,0:T(8,128)(2,1)} custom-call(s32[4]{0:T(128)S(1)} %copy-done.5, s32[3,1024]{1,0:T(4,128)S(1)} %copy-done.3, s32[1]{0:T(128)} %collective-permute-done.before, bf16[3,1024,512]{2,1,0:T(8,128)(2,1)S(1)} %copy-done, bf16[2,128,1024]{2,1,0:T(8,128)(2,1)S(1)} %get-tuple-element.68.branch, ...), custom_call_target="tpu_custom_call" | custom-call | flops 10000000000 | bytes 1000 | tf_op jit(solution)/shard_map/place/pallas_call | solution.py:486
  118.9 0.0 all-to-all-done.1.received
  118.9 1.1 finish.1
  (19 shorter events, 0.0 us)
Async XLA Ops:
  2.0 13.0 %copy-start.8 = (f32[512]{0:T(512)S(1)}, f32[512]{0:T(512)}, u32[]{:S(2)}) copy-start(f32[512]{0:T(512)} %param.11) | copy-start | bytes 6148
  6.1 10.5 %collective-permute-start = (s32[1]{0:T(128)}, s32[1]{0:T(128)}, u32[]{:S(2)}, u32[]{:S(2)}) collective-permute-start(s32[1]{0:T(128)} %param.9), channel_id=1, source_target_pairs={{0,4},{4,8},{8,12},{12,16},{16,20},{20,24},{24,28},{28,32},{32,36}... | collective-permute-start | bytes 20 | tf_op jit(solution)/shard_map/ppermute | solution.py:361
  7.6 18.9 %collective-permute-start.1 = (bf16[2,256,512]{2,1,0:T(8,128)(2,1)}, bf16[2,256,512]{2,1,0:T(8,128)(2,1)S(1)}, u32[]{:S(2)}, u32[]{:S(2)}) collective-permute-start(bf16[2,256,512]{2,1,0:T(8,128)(2,1)} %get-tuple-element.43), channel_id=1, source_target_pairs={{0,252},{4,0},{8,4},{12,8},{16,12},{20,16},{24,20},{28,24},{32,28}... | collective-permute-start | bytes 1572872 | tf_op jit(solution)/shard_map/ppermute | solution.py:361
  14.9 17.8 %collective-permute-start.2 = (bf16[2,256,512]{2,1,0:T(8,128)(2,1)}, bf16[2,256,512]{2,1,0:T(8,128)(2,1)S(1)}, u32[]{:S(2)}, u32[]{:S(2)}) collective-permute-start(bf16[2,256,512]{2,1,0:T(8,128)(2,1)} %get-tuple-element.44), channel_id=1, source_target_pairs={{0,4},{4,8},{8,12},{12,16},{16,20},{20,24},{24,28},{28,32},{32,36}... | collective-permute-start | bytes 1572872 | tf_op jit(solution)/shard_map/ppermute | solution.py:361
  26.4 9.0 %copy-start.9 = (bf16[2,256,512]{2,1,0:T(8,128)(2,1)}, bf16[2,256,512]{2,1,0:T(8,128)(2,1)S(1)}, u32[]{:S(2)}) copy-start(bf16[2,256,512]{2,1,0:T(8,128)(2,1)S(1)} %collective-permute-done.1.pull) | copy-start | bytes 1572868
  32.7 2.7 %copy-start.10 = (bf16[2,256,512]{2,1,0:T(8,128)(2,1)}, bf16[2,256,512]{2,1,0:T(8,128)(2,1)S(1)}, u32[]{:S(2)}) copy-start(bf16[2,256,512]{2,1,0:T(8,128)(2,1)S(1)} %collective-permute-done.2.push) | copy-start | bytes 1572868
  32.7 1.9 %collective-permute-start.3 = (bf16[2,256,512]{2,1,0:T(8,128)(2,1)S(1)}, bf16[2,256,512]{2,1,0:T(8,128)(2,1)S(1)}, u32[]{:S(2)}, u32[]{:S(2)}) collective-permute-start(bf16[2,256,512]{2,1,0:T(8,128)(2,1)S(1)} %collective-permute-done.1.pull), channel_id=1, source_target_pairs={{0,1},{1,0},{2,3},{3,2},{4,5},{5,4},{6,7},{7,6},{8,9},{9,8},{10,11... | collective-permute-start | bytes 1572872 | tf_op jit(solution)/shard_map/ppermute | solution.py:364
  32.7 2.7 %collective-permute-start.4 = (bf16[2,256,512]{2,1,0:T(8,128)(2,1)S(1)}, bf16[2,256,512]{2,1,0:T(8,128)(2,1)S(1)}, u32[]{:S(2)}, u32[]{:S(2)}) collective-permute-start(bf16[2,256,512]{2,1,0:T(8,128)(2,1)S(1)} %collective-permute-done.2.push), channel_id=1, source_target_pairs={{0,1},{1,0},{2,3},{3,2},{4,5},{5,4},{6,7},{7,6},{8,9},{9,8},{10,11... | collective-permute-start | bytes 1572872 | tf_op jit(solution)/shard_map/ppermute | solution.py:364
  34.7 0.8 copy-start.11
  35.4 0.8 copy-start.12
  36.2 34.0 %copy-start.5 = (s32[4]{0:T(128)S(1)}, s32[4]{0:T(128)}, u32[]{:S(2)}) copy-start(s32[4]{0:T(128)} %pad_add_fusion.scal) | copy-start | bytes 52
  51.9 41.2 %copy-start.2 = (f32[512,1]{1,0:T(8,128)S(1)}, f32[512,1]{1,0:T(8,128)}, u32[]{:S(2)}) copy-start(f32[512,1]{1,0:T(8,128)} %copy.13.gain_column) | copy-start | bytes 6148
  51.9 41.2 %copy-start.6 = (bf16[2,128,1024]{2,1,0:T(8,128)(2,1)S(1)}, bf16[2,128,1024]{2,1,0:T(8,128)(2,1)}, u32[]{:S(2)}) copy-start(bf16[2,128,1024]{2,1,0:T(8,128)(2,1)} %get-tuple-element.66.unit) | copy-start | bytes 1572868
  51.9 41.2 %copy-start.7 = (f32[2,8,1024]{2,1,0:T(8,128)S(1)}, f32[2,8,1024]{2,1,0:T(8,128)}, u32[]{:S(2)}) copy-start(f32[2,8,1024]{2,1,0:T(8,128)} %get-tuple-element.67.stat) | copy-start | bytes 196612
  51.9 18.3 %collective-permute-start.5 = (bf16[2,128,2048]{2,1,0:T(8,128)(2,1)}, bf16[2,128,2048]{2,1,0:T(8,128)(2,1)S(1)}, u32[]{:S(2)}, u32[]{:S(2)}) collective-permute-start(bf16[2,128,2048]{2,1,0:T(8,128)(2,1)} %get-tuple-element.59), channel_id=1, source_target_pairs={{0,1},{1,0},{2,3},{3,2},{4,5},{5,4},{6,7},{7,6},{8,9},{9,8},{10,11... | collective-permute-start | bytes 3145736 | tf_op jit(solution)/shard_map/ppermute | solution.py:364
  52.2 34.0 %all-to-all-start = ((bf16[64,32,128]{2,1,0:T(8,128)(2,1)}), bf16[64,32,128]{2,1,0:T(8,128)(2,1)S(1)}, u32[]{:S(2)}, u32[]{:S(2)}) async-start(bf16[64,32,128]{2,1,0:T(8,128)(2,1)} %get-tuple-element.71), calls=%async_computation | async-start | bytes 1048576 | tf_op jit(solution)/shard_map/all_to_all | solution.py:437
  67.6 2.6 %collective-permute-start.6 = (f32[2,2048]{1,0:T(2,128)}, f32[2,2048]{1,0:T(2,128)S(1)}, u32[]{:S(2)}, u32[]{:S(2)}) collective-permute-start(f32[2,2048]{1,0:T(2,128)} %get-tuple-element.60.stats), channel_id=1, source_target_pairs={{0,1},{1,0},{2,3},{3,2},{4,5},{5,4},{6,7},{7,6},{8,9},{9,8},{10,11... | collective-permute-start | bytes 49160 | tf_op jit(solution)/shard_map/ppermute | solution.py:364
  67.7 1.5 %collective-permute-start.7 = (f32[1,512]{1,0:T(1,128)}, f32[1,512]{1,0:T(1,128)S(1)}, u32[]{:S(2)}, u32[]{:S(2)}) collective-permute-start(f32[1,512]{1,0:T(1,128)} %get-tuple-element.63), channel_id=1, source_target_pairs={{0,1},{1,0},{2,3},{3,2},{4,5},{5,4},{6,7},{7,6},{8,9},{9,8},{10,11... | collective-permute-start | bytes 6152 | tf_op jit(solution)/shard_map/ppermute | solution.py:364
  69.9 5.1 %collective-permute-start.8 = (f32[1,512]{1,0:T(1,128)S(1)}, f32[1,512]{1,0:T(1,128)S(1)}, u32[]{:S(2)}, u32[]{:S(2)}) collective-permute-start(f32[1,512]{1,0:T(1,128)S(1)} %add.9.gain), channel_id=1, source_target_pairs={{0,2},{1,3},{2,0},{3,1},{4,6},{5,7},{6,4},{7,5},{8,10},{9,11},{10,... | collective-permute-start | bytes 6152 | tf_op jit(solution)/shard_map/ppermute | solution.py:364
  70.2 1.2 %copy-start.1 = (bf16[2,128,2048]{2,1,0:T(8,128)(2,1)S(1)}, bf16[2,128,2048]{2,1,0:T(8,128)(2,1)}, u32[]{:S(2)}) copy-start(bf16[2,128,2048]{2,1,0:T(8,128)(2,1)} %get-tuple-element.58.keep) | copy-start | bytes 3145732
  71.4 0.7 copy-start.4
  75.0 18.1 %collective-permute-start.9 = (bf16[128,2048]{1,0:T(8,128)(2,1)S(1)}, bf16[128,2048]{1,0:T(8,128)(2,1)S(1)}, u32[]{:S(2)}, u32[]{:S(2)}) collective-permute-start(bf16[128,2048]{1,0:T(8,128)(2,1)S(1)} %get-tuple-element.64), channel_id=1, source_target_pairs={{0,2},{1,3},{2,0},{3,1},{4,6},{5,7},{6,4},{7,5},{8,10},{9,11},{10,... | collective-permute-start | bytes 1572872 | tf_op jit(solution)/shard_map/ppermute | solution.py:364
  76.5 16.7 %collective-permute-start.10 = (f32[2,2048]{1,0:T(2,128)S(1)}, f32[2,2048]{1,0:T(2,128)S(1)}, u32[]{:S(2)}, u32[]{:S(2)}) collective-permute-start(f32[2,2048]{1,0:T(2,128)S(1)} %get-tuple-element.65.stats), channel_id=1, source_target_pairs={{0,2},{1,3},{2,0},{3,1},{4,6},{5,7},{6,4},{7,5},{8,10},{9,11},{10,... | collective-permute-start | bytes 49160 | tf_op jit(solution)/shard_map/ppermute | solution.py:364
  87.7 31.1 %all-to-all-start.1 = ((bf16[64,40,128]{2,1,0:T(8,128)(2,1)}), bf16[64,40,128]{2,1,0:T(8,128)(2,1)S(1)}, u32[]{:S(2)}, u32[]{:S(2)}) async-start(bf16[64,40,128]{2,1,0:T(8,128)(2,1)} %total.1), calls=%async_computation.1 | async-start | bytes 1310720 | tf_op jit(solution)/shard_map/all_to_all | solution.py:484
  93.2 22.2 %copy-start = (bf16[3,1024,512]{2,1,0:T(8,128)(2,1)S(1)}, bf16[3,1024,512]{2,1,0:T(8,128)(2,1)}, u32[]{:S(2)}) copy-start(bf16[3,1024,512]{2,1,0:T(8,128)(2,1)} %cotangent.3) | copy-start | bytes 9437188
  93.2 22.2 %copy-start.3 = (s32[3,1024]{1,0:T(4,128)S(1)}, s32[3,1024]{1,0:T(4,128)}, u32[]{:S(2)}) copy-start(s32[3,1024]{1,0:T(4,128)} %order.5) | copy-start | bytes 36868
  94.2 21.2 %collective-permute-start.11 = (bf16[128,512]{1,0:T(8,128)(2,1)S(1)}, bf16[128,512]{1,0:T(8,128)(2,1)S(1)}, u32[]{:S(2)}, u32[]{:S(2)}) collective-permute-start(bf16[128,512]{1,0:T(8,128)(2,1)S(1)} %get-tuple-element.69), channel_id=1, source_target_pairs={{0,4},{4,8},{8,12},{12,16},{16,20},{20,24},{24,28},{28,32},{32,36}... | collective-permute-start | bytes 393224 | tf_op jit(solution)/shard_map/ppermute | solution.py:361
  95.9 19.5 %collective-permute-start.12 = (bf16[128,512]{1,0:T(8,128)(2,1)S(1)}, bf16[128,512]{1,0:T(8,128)(2,1)S(1)}, u32[]{:S(2)}, u32[]{:S(2)}) collective-permute-start(bf16[128,512]{1,0:T(8,128)(2,1)S(1)} %get-tuple-element.70), channel_id=1, source_target_pairs={{0,252},{4,0},{8,4},{12,8},{16,12},{20,16},{24,20},{28,24},{32,28}... | collective-permute-start | bytes 393224 | tf_op jit(solution)/shard_map/ppermute | solution.py:361

commit v3 on v2

--- a/solution.py
+++ b/solution.py
@@ -47,20 +47,25 @@
     )
 
 
-def halo_kernel(scal, order, first_x, first_dy, last_x, last_dy, pull, push, chosen):
+def halo_kernel(scal, order, points, cotangent, pull, push, held, done):
     rows = pull.shape[1]
-    patch = first_x.shape[1]
-
-    @pl.when(pl.program_id(0) == 0)
-    def _():
-        for k, slot, base in ((0, 0, 0), (1, order.shape[0] - 1, patch // 2)):
-            at = pl.ds(pl.multiple_of(base + scal[0] * rows, rows), rows)
-            chosen[k] = one_hot_rows(order[slot:slot + 1, at], patch)
-
-    pull[0] = mm(chosen[0], first_x[0]).astype(BF16)
-    pull[1] = mm(chosen[0], first_dy[0]).astype(BF16)
-    push[0] = mm(chosen[1], last_x[0]).astype(BF16)
-    push[1] = mm(chosen[1], last_dy[0]).astype(BF16)
+    patch = points.shape[1]
+    last = points.shape[0] - 1
+    copies = []
+    for slot in (last, 0):
+        for source in (points, cotangent):
+            k = len(copies)
+            copies.append(pltpu.make_async_copy(source.at[slot], held.at[k], done.at[k]))
+            copies[-1].start()
+    count = jnp.zeros((16, push.shape[2]), F32) + scal[2].astype(F32)
+    for k, (slot, base, out) in enumerate(((last, patch // 2, push), (0, 0, pull))):
+        at = pl.ds(pl.multiple_of(base + scal[0] * rows, rows), rows)
+        chosen = one_hot_rows(order[slot:slot + 1, at], patch)
+        for j in range(2):
+            copies[2 * k + j].wait()
+            out[j, 0:rows, :] = mm(chosen, held[2 * k + j]).astype(BF16)
+    push[0, rows:, :] = count.astype(BF16)
+    push[1, rows:, :] = count.astype(BF16)
 
 
 def norm_half(x, gain, own):
@@ -74,57 +79,99 @@
     return normed, unit, inverse_row
 
 
-def project(nrm, dy, w3, wt, wo, prj, kr, vr, dat):
+def project(nrm, dy, weights, wt, wo, prj, kr, vr, dat):
     prj[0:128, :] = (mm_nt(wt[0:128, :], nrm[...]) * SCALE).astype(BF16)
     prj[128:384, :] = mm_nt(wt[128:384, :], nrm[...]).astype(BF16)
-    kr[...] = mm(nrm[...], w3[1]).astype(BF16)
-    vr[...] = mm(nrm[...], w3[2]).astype(BF16)
+    both = mm(nrm[...], weights[0:D, 128:384]).astype(BF16)
+    kr[...] = both[:, 0:128]
+    vr[...] = both[:, 128:256]
     dat[...] = mm_nt(wo[...], dy[...]).astype(BF16)
 
 
-def attend(prj, kr, vr, dat, gp, att):
-    zeros = jnp.zeros((HEAD, prj.shape[1]), BF16)
+def attend(prj, kr, vr, dat, gp, att, scores, lows):
+    patch = prj.shape[1]
+    chunk = 256
+    blocks = [slice(c, c + chunk) for c in range(0, patch, chunk)]
+    zeros = jnp.zeros((HEAD, patch), BF16)
+    state = [{}, {}]
 
     def pad(x, h):
         return jnp.concatenate([x, zeros] if h == 0 else [zeros, x], axis=0)
 
-    def soft(scores):
-        expos = jnp.exp2(scores - jnp.max(scores, axis=0, keepdims=True))
-        recip = 1.0 / jnp.sum(expos, axis=0, keepdims=True)
-        return expos, expos.astype(BF16), recip
-
-    def middle(lo, expos, low, recip):
-        attended = mm(prj[256 + lo:256 + lo + HEAD, :], low) * recip
-        att[lo:lo + HEAD, :] = attended.astype(BF16)
-        grad = dat[lo:lo + HEAD, :].astype(F32) * recip
-        inner = jnp.sum(grad * attended, axis=0, keepdims=True)
-        grad = grad.astype(BF16)
-        grad_probs = mm(vr[...], pad(grad, lo // HEAD))
-        return grad, (expos * (grad_probs - inner)).astype(BF16)
-
-    def end(lo, low, grad, grad_scores):
-        dq = mm(prj[128 + lo:128 + lo + HEAD, :], grad_scores) * (HEAD ** (-0.5))
-        gp[lo:lo + HEAD, :] = dq.astype(BF16)
+    def fold(x, op):
+        return op(x.reshape(chunk // 8, 8, patch), axis=0)
+
+    def score(h, keys):
+        here, lo = state[h], h * HEAD
+        block = mm(kr[keys, :], pad(prj[lo:lo + HEAD, :], h))
+        scores[h, keys, :] = block
+        high = fold(block, jnp.max)
+        here["high"] = jnp.maximum(here["high"], high) if "high" in here else high
+        if keys.stop == patch:
+            here["high"] = jnp.max(here["high"], axis=0, keepdims=True)
+
+    def soften(h, keys):
+        here, lo = state[h], h * HEAD
+        expos = jnp.exp2(scores[h, keys, :] - here["high"])
+        scores[h, keys, :] = expos
+        lows[h, keys, :] = expos.astype(BF16)
+        total = fold(expos, jnp.sum)
+        here["total"] = here["total"] + total if "total" in here else total
+        if keys.stop == patch:
+            recip = 1.0 / jnp.sum(here["total"], axis=0, keepdims=True)
+            attended = mm(prj[256 + lo:256 + lo + HEAD, :], lows[h]) * recip
+            att[lo:lo + HEAD, :] = attended.astype(BF16)
+            grad = dat[lo:lo + HEAD, :].astype(F32) * recip
+            here["inner"] = jnp.sum(grad * attended, axis=0, keepdims=True)
+            here["grad"] = grad.astype(BF16)
+
+    def back(h, keys):
+        here, lo = state[h], h * HEAD
+        grad_probs = mm(vr[keys, :], pad(here["grad"], h))
+        grad_scores = (scores[h, keys, :] * (grad_probs - here["inner"])).astype(BF16)
         dk = mm_nt(prj[lo:lo + HEAD, :], grad_scores) * (HEAD ** (-0.5) / SCALE)
-        gp[128 + lo:128 + lo + HEAD, :] = dk.astype(BF16)
-        gp[256 + lo:256 + lo + HEAD, :] = mm_nt(grad, low).astype(BF16)
-
-    heads = (0, HEAD)
-    scores = [mm(kr[...], pad(prj[lo:lo + HEAD, :], lo // HEAD)) for lo in heads]
-    softs = [soft(x) for x in scores]
-    middles = [middle(lo, *x) for lo, x in zip(heads, softs)]
-    for lo, x, y in zip(heads, softs, middles):
-        end(lo, x[1], *y)
-
-
-def patch_core(core, p, nrm, dy, w3, wt, wo, gain_column, send, keep, stats,
-               prj, kr, vr, dat, att, wacc, gp, grads, done):
-    project(nrm, dy, w3, wt, wo, prj, kr, vr, dat)
-    attend(prj, kr, vr, dat, gp, att)
+        gp[128 + lo:128 + lo + HEAD, keys] = dk.astype(BF16)
+        gp[256 + lo:256 + lo + HEAD, keys] = mm_nt(here["grad"], lows[h, keys, :]).astype(BF16)
+        lows[h, keys, :] = grad_scores
+        if keys.stop == patch:
+            dq = mm(prj[128 + lo:128 + lo + HEAD, :], lows[h]) * (HEAD ** (-0.5))
+            gp[lo:lo + HEAD, :] = dq.astype(BF16)
+
+    for keys in blocks:
+        score(0, keys)
+    for keys in blocks:
+        score(1, keys)
+        soften(0, keys)
+    for keys in blocks:
+        back(0, keys)
+        soften(1, keys)
+    for keys in blocks:
+        back(1, keys)
+
+
+def split3(x):
+    first = x.astype(BF16)
+    rest = x - first.astype(F32)
+    second = rest.astype(BF16)
+    third = (rest - second.astype(F32)).astype(BF16)
+    none = jnp.zeros((13, x.shape[1]), BF16)
+    return jnp.concatenate([first, second, third, none], axis=0)
+
+
+def load_weights(w3, wt, gain, weights):
+    for t in range(3):
+        weights[0:D, 128 * t:128 * t + 128] = w3[t]
+    sums = jnp.sum(mm_nt(split3(gain[...]), wt[...]), axis=0, keepdims=True)
+    weights[D:D + 16, :] = split3(sums)
+
+
+def patch_core(core, p, nrm, dy, wt, wo, send, keep, stats, wacc,
+               prj, kr, vr, dat, att, gp, grads, scores, lows, weights, done):
+    project(nrm, dy, weights, wt, wo, prj, kr, vr, dat)
+    attend(prj, kr, vr, dat, gp, att, scores, lows)
     patch = gp.shape[1]
     cols = pl.ds(pl.multiple_of(p * patch, patch), patch)
-    weights = jnp.concatenate([w3[0], w3[1], w3[2]], axis=1)
-    grads[...] = mm(weights, gp[...]).astype(BF16)
+    grads[...] = mm(weights[0:D, :], gp[...]).astype(BF16)
     copies = []
     for j in range(2):
         for k, (block, into) in enumerate(((2 * j + 1 - core, send), (2 * j + core, keep))):
@@ -135,7 +182,7 @@
             copies[-1].start()
     wacc[0:384] += mm(gp[...], nrm[...])
     wacc[384:512] += mm(att[...], dy[...])
-    stats[0:1, cols] = jnp.sum(grads[...].astype(F32) * gain_column[...], axis=0, keepdims=True)
+    stats[0:1, cols] = jnp.sum(mm(weights[D:D + 16, :], gp[...]), axis=0, keepdims=True)
     stats[1:2, cols] = second_stat(gp, prj)
     for copy in copies:
         copy.wait()
@@ -160,80 +207,110 @@
     return unit, inverse
 
 
-def local_kernel(scal, order, points, cotangent, gain, gain_column, w3, wo,
+def local_kernel(scal, order, points, cotangent, gain, w3, wo,
                  send, keep, stats, unit_o, inv_o, wacc, wt, nrm_o, dy_o,
                  nrm, dy, own, *work):
     half = points.shape[1] // 2
     for t in range(3):
         wt[128 * t:128 * t + 128, :] = w3[t].astype(F32).T.astype(BF16)
     wacc[...] = jnp.zeros_like(wacc)
-
-    def interior(p, carry):
+    load_weights(w3, wt, gain, work[-2])
+
+    whole = scal[2] > 1
+
+    def step(p, carry):
         for side in range(2):
             rows = slice(half * side, half * side + half)
-            unit, inverse = gather_rows(scal, order, points, cotangent, gain, own, p + side,
-                                        1 - side, nrm.at[rows], dy.at[rows])
-            unit_o[p, :, rows] = unit
-            inv_o[p, :, rows] = inverse
-        patch_core(scal[0], p, nrm, dy, w3, wt, wo, gain_column, send, keep, stats,
-                   *work[:5], wacc, *work[5:])
+
+            @pl.when(jnp.logical_or(whole, p == side))
+            def _():
+                slot = jnp.where(whole, p + side, 0)
+                unit, inverse = gather_rows(scal, order, points, cotangent, gain, own, slot,
+                                            1 - side, nrm.at[rows], dy.at[rows])
+                unit_o[p, :, rows] = unit
+                inv_o[p, :, rows] = inverse
+
+        @pl.when(whole)
+        def _():
+            patch_core(scal[0], p, nrm, dy, wt, wo, send, keep, stats, wacc, *work)
+
+        @pl.when(jnp.logical_not(whole))
+        def _():
+            here = pl.ds(pl.multiple_of(half * p, half), half)
+            nrm_o[p] = nrm[here, :]
+            dy_o[p] = dy[here, :]
+
         return carry
 
-    lax.fori_loop(0, scal[2] - 1, interior, 0)
-
-    @pl.when(scal[2] == 1)
-    def _():
-        for p in range(2):
-            rows = slice(half * p, half * p + half)
-            unit, inverse = gather_rows(scal, order, points, cotangent, gain, own, 0, 1 - p,
-                                        nrm_o.at[p], dy_o.at[p])
-            unit_o[p, :, rows] = unit
-            inv_o[p, :, rows] = inverse
-
-
-def cross_kernel(factor, scal, before, pull, pull_other, push, push_other, send_i, keep_i, stats_i,
-                 unit_i, inv_i, wacc_i, nrm_i, dy_i, gain, gain_column, w3, wt, wo,
-                 send, keep, stats, unit_o, inv_o, pieces, gain_o,
-                 nrm, dy, own, *work_wacc):
+    lax.fori_loop(0, 2, step, 0)
+
+
+def cross_kernel(factor, scal, pull, pull_other, push, push_other, send_i, keep_i, wacc_i, nrm_i,
+                 dy_i, stats_i, unit_i, inv_i, gain, w3, wt, wo,
+                 send, keep, stats, unit_o, inv_o, pieces, gain_o, pushed,
+                 flag, nrm_2, dy_2, own_2, arrived, *work_wacc):
     wacc, work = work_wacc[-1], work_wacc[:-1]
     half = nrm_i.shape[1]
     part = half // 2
     first = pl.multiple_of(scal[1] * 128, 128)
     light = scal[2] == 1
+    told = pltpu.make_async_copy(push.at[0, part:part + 16], flag, arrived.at[2, 0])
+    told.start()
+    copies = []
+    for p, one, other in ((0, pull, pull_other), (1, push, push_other)):
+        here, there = half * p, half * (1 - p)
+        moves = [(nrm_i.at[p], nrm_2.at[p, here:here + half]),
+                 (dy_i.at[p], dy_2.at[p, here:here + half])]
+        for source, core in ((one, scal[0]), (other, 1 - scal[0])):
+            at = pl.multiple_of(core * part, part)
+            moves.append((source.at[0, 0:part], own_2.at[p, pl.ds(at, part)]))
+            moves.append((source.at[1, 0:part],
+                          dy_2.at[p, pl.ds(pl.multiple_of(there + at, part), part)]))
+        copies.append([pltpu.make_async_copy(source, into, arrived.at[p, k])
+                       for k, (source, into) in enumerate(moves)])
+        for copy in copies[-1]:
+            copy.start()
     stats[...] = stats_i[...]
     unit_o[...] = unit_i[...]
     inv_o[...] = inv_i[...]
-    wacc[...] = wacc_i[...]
+    load_weights(w3, wt, gain, work[-2])
+
+    @pl.when(light)
+    def _():
+        wacc[...] = jnp.zeros_like(wacc)
+
+    @pl.when(jnp.logical_not(light))
+    def _():
+        copy = pltpu.make_async_copy(wacc_i, wacc, work[-1].at[0])
+        copy.start()
+        copy.wait()
+
+    told.wait()
+    before = jnp.max(flag[...].astype(F32)).astype(jnp.int32)
+    pushed[0] = before
+    patches = jnp.where(light, jnp.where(before > 1, 2, 1), 0)
 
     def cross(p, carry):
-        here = pl.multiple_of(half * p, half)
-        there = pl.multiple_of(half * (1 - p), half)
-        nrm[pl.ds(here, half), :] = nrm_i[p]
-        dy[pl.ds(here, half), :] = dy_i[p]
-
-        def take(one, other):
-            for source, core in ((one, scal[0]), (other, 1 - scal[0])):
-                at = pl.multiple_of(core * part, part)
-                own[pl.ds(at, part), :] = source[0]
-                dy[pl.ds(pl.multiple_of(there + at, part), part), :] = source[1]
-
-        @pl.when(p == 0)
-        def _():
-            take(pull, pull_other)
-
-        @pl.when(p == 1)
-        def _():
-            take(push, push_other)
-
-        normed, unit, inverse = norm_half(own[...], gain[...], own[:, pl.ds(first, 128)])
-        nrm[pl.ds(there, half), :] = normed
-        unit_o[p, :, pl.ds(there, half)] = unit
-        inv_o[p, :, pl.ds(there, half)] = inverse
-        patch_core(scal[0], p, nrm, dy, w3, wt, wo, gain_column, send, keep, stats,
-                   *work[:5], wacc, *work[5:])
+        for q in range(2):
+            @pl.when(p == q)
+            def _():
+                for copy in copies[q]:
+                    copy.wait()
+
+        @pl.when(p < patches)
+        def _():
+            there = pl.multiple_of(half * (1 - p), half)
+            own = own_2.at[p]
+            nrm = nrm_2.at[p]
+            normed, unit, inverse = norm_half(own[...], gain[...], own[:, pl.ds(first, 128)])
+            nrm[pl.ds(there, half), :] = normed
+            unit_o[p, :, pl.ds(there, half)] = unit
+            inv_o[p, :, pl.ds(there, half)] = inverse
+            patch_core(scal[0], p, nrm, dy_2.at[p], wt, wo, send, keep, stats, wacc, *work)
+
         return carry
 
-    lax.fori_loop(0, jnp.where(light, jnp.where(before[0] > 1, 2, 1), 0), cross, 0)
+    lax.fori_loop(0, 2, cross, 0)
     total = wacc[0:384] * factor
     gain_o[...] = jnp.sum(total * wt[...].astype(F32), axis=0, keepdims=True) / gain[...]
     for r in range(16):
@@ -249,10 +326,11 @@
     stats_o[...] = stats[...] + stats_received[...]
 
 
-def branch_kernel(scal, kept, received, stats, stats_received, unit, stat, gain_column,
+def branch_kernel(scal, kept, received, stats, stats_received, unit, stat, gain,
                   branch, back, ahead):
     half = branch.shape[2] // 2
-    own_gain = gain_column[pl.ds(pl.multiple_of(scal[1] * 128, 128), 128), :]
+    own_gain = gain[:, pl.ds(pl.multiple_of(scal[1] * 128, 128), 128)]
+    own_gain = jnp.broadcast_to(own_gain, (128, 128)).T[:, 0:1]
     scaled = (kept[...].astype(F32) + received[...].astype(F32)) * own_gain
     mean = (stats[0:1, :] + stats_received[0:1, :]) * (1.0 / D)
     slope = (stats[1:2, :] + stats_received[1:2, :]) * (1.0 / D)
@@ -353,7 +431,6 @@
     far = model_part // 2
     scal = jnp.stack([core, model_part, counts[0], far]).astype(jnp.int32)
     gain_row = norm_gain.reshape(1, width)
-    gain_column = norm_gain.reshape(width, 1)
     w3 = jnp.transpose(w_qkv, (1, 0, 2))
     sds = jax.ShapeDtypeStruct
 
@@ -363,29 +440,30 @@
     def swapped(x, bit):
         return lax.ppermute(x, "mp", [(i, i ^ bit) for i in range(4)])
 
-    first_block = pl.BlockSpec((1, patch, width // 2), lambda i: (0, 0, i))
-    last_block = pl.BlockSpec((1, patch, width // 2), lambda i: (slots - 1, 0, i))
-    part_block = pl.BlockSpec((2, half // 2, width // 2), lambda i: (0, 0, i))
     pull, push = pl.pallas_call(
         halo_kernel,
-        grid=(2,),
-        in_specs=[SMEM, pl.BlockSpec((slots, patch), lambda i: (0, 0)),
-                  first_block, first_block, last_block, last_block],
-        out_specs=[part_block] * 2,
-        out_shape=[sds((2, half // 2, width), BF16)] * 2,
-        scratch_shapes=[pltpu.VMEM((2, half // 2, patch), BF16)],
+        in_specs=[SMEM, VMEM, ANY, ANY],
+        out_specs=[VMEM] * 2,
+        out_shape=[sds((2, half // 2, width), BF16), sds((2, half // 2 + 16, width), BF16)],
+        scratch_shapes=[pltpu.VMEM((4, patch, width), BF16), pltpu.SemaphoreType.DMA((4,))],
         compiler_params=params(60),
         name="halo",
-    )(scal, order, points, cotangent, points, cotangent)
-    counts, pull = lax.optimization_barrier((counts, pull))
-    before = passed(counts, 1)
+    )(scal, order, points, cotangent)
     pull, push = passed(pull, -1), passed(push, 1)
-    scal_local, before = lax.optimization_barrier((scal, before))
-
-    work = [
+
+    rows = [
         pltpu.VMEM((patch, width), BF16),
         pltpu.VMEM((patch, width), BF16),
         pltpu.VMEM((half, width), BF16),
+    ]
+    rows_2 = [
+        pltpu.VMEM((16, width), BF16),
+        pltpu.VMEM((2, patch, width), BF16),
+        pltpu.VMEM((2, patch, width), BF16),
+        pltpu.VMEM((2, half, width), BF16),
+        pltpu.SemaphoreType.DMA((3, 6)),
+    ]
+    work = [
         pltpu.VMEM((384, patch), BF16),
         pltpu.VMEM((patch, 128), BF16),
         pltpu.VMEM((patch, 128), BF16),
@@ -393,6 +471,9 @@
         pltpu.VMEM((128, patch), BF16),
         pltpu.VMEM((384, patch), BF16),
         pltpu.VMEM((width, patch), BF16),
+        pltpu.VMEM((2, patch, patch), F32),
+        pltpu.VMEM((2, patch, patch), BF16),
+        pltpu.VMEM((width + 16, 384), BF16),
         pltpu.SemaphoreType.DMA((4,)),
     ]
     lanes = 2 * patch
@@ -405,7 +486,7 @@
     ]
     send, keep, stats, unit, inverse, wacc, wt, nrm, dy = pl.pallas_call(
         local_kernel,
-        in_specs=[SMEM] + [VMEM] * 7,
+        in_specs=[SMEM] + [VMEM] * 6,
         out_specs=[ANY] * 2 + [VMEM] * 7,
         out_shape=shared + [
             sds((512, width), F32),
@@ -413,26 +494,28 @@
             sds((2, half, width), BF16),
             sds((2, half, width), BF16),
         ],
-        scratch_shapes=work,
+        scratch_shapes=rows + work,
         compiler_params=params(60),
         cost_estimate=cost(16 * 10**9, 16 * 10**6),
         name="local",
-    )(scal_local, order, points, cotangent, gain_row, gain_column, w3, w_out)
+    )(scal, order, points, cotangent, gain_row, w3, w_out)
     pull, push, wacc = lax.optimization_barrier((pull, push, wacc))
 
     factor = 1.0 / math.sqrt(curve * slots * patch)
-    send, keep, stats, unit, inverse, pieces, gain_part = pl.pallas_call(
+    send, keep, stats, unit, inverse, pieces, gain_part, before = pl.pallas_call(
         functools.partial(cross_kernel, factor),
-        in_specs=[SMEM] * 2 + [VMEM] * 4 + [ANY] * 2 + [VMEM] * 11,
-        out_specs=[ANY] * 2 + [VMEM] * 5,
-        out_shape=shared + [sds((64, 32, 128), BF16), sds((1, width), F32)],
-        scratch_shapes=work + [pltpu.VMEM((512, width), F32)],
-        input_output_aliases={6: 0, 7: 1},
-        compiler_params=params(56),
+        in_specs=[SMEM] + [ANY] * 9 + [VMEM] * 7,
+        out_specs=[ANY] * 2 + [VMEM] * 5 + [SMEM],
+        out_shape=shared + [
+            sds((64, 32, 128), BF16), sds((1, width), F32), sds((1,), jnp.int32)
+        ],
+        scratch_shapes=rows_2 + work + [pltpu.VMEM((512, width), F32)],
+        input_output_aliases={5: 0, 6: 1},
+        compiler_params=params(60),
         cost_estimate=cost(4 * 10**9, 8 * 10**6),
         name="cross",
-    )(scal, before, pull, swapped(pull, 1), push, swapped(push, 1), send, keep, stats, unit,
-      inverse, wacc, nrm, dy, gain_row, gain_column, w3, wt, w_out)
+    )(scal, pull, swapped(pull, 1), push, swapped(push, 1), send, keep, wacc, nrm, dy, stats, unit,
+      inverse, gain_row, w3, wt, w_out)
 
     received = lax.all_to_all(pieces, "curve", 0, 0)
     gain_part = gain_part + swapped(gain_part, 1)
@@ -464,13 +547,13 @@
         branch_kernel,
         grid=(2,),
         in_specs=[SMEM, by_lanes(128), by_lanes(128), by_lanes(2), by_lanes(2),
-                  by_patch(128, patch), by_patch(8, patch), whole(width, 1)],
+                  by_patch(128, patch), by_patch(8, patch), whole(1, width)],
         out_specs=[by_patch(128, patch), whole(128, half), whole(128, half)],
         out_shape=[sds((2, 128, patch), BF16), sds((128, half), BF16), sds((128, half), BF16)],
         compiler_params=params(16),
         cost_estimate=cost(10**10, 1000),
         name="branch",
-    )(scal, kept, away, stats, away_stats, unit, inverse, gain_column)
+    )(scal, kept, away, stats, away_stats, unit, inverse, gain_row)
     from_before, from_after = passed(ahead, 1), passed(back, -1)
 
     totals = pl.pallas_call(

time: 120 us -> 117 us (0.975)
  starting transfers between devices: 41.2 us -> 37.3 us
    all_to_all x1, starting transfers between devices: 15.4 us -> 11.2 us  [shards(): received = lax.all_to_all(pieces, 'curve', 0, 0)]
    ppermute x5 -> x4, waiting for transfers between devices: 23.7 us -> 24.8 us  [passed(): lax.ppermute(x, 'curve', [(i, (i + by) % curve) for i in range(curve)])]
    unnamed x26 -> x24, local copies, waits for them, and re-layouts: 2.75 us -> 2.93 us
    ppermute x5 -> x4, starting transfers between devices: 15.2 us -> 15.2 us  [passed(): lax.ppermute(x, 'curve', [(i, (i + by) % curve) for i in range(curve)])]
  transfers between devices with their start and end apart: 15 -> 14, of which waited for: 9 -> 7; matrix products, arithmetic and copies ran while one was open for 1% -> 1% of each run, Pallas kernels for 13% -> 13%
where the time goes in v3:
time: 117 us; the launch traced here: 116 us
  starting transfers between devices  37.3 us (32%)
  waiting for transfers between devices  37.2 us (32%)
  Pallas kernels  35.9 us (31%)
  local copies, waits for them, and re-layouts  2.93 us (3%)
  between operations  1.47 us (1%)
  other arithmetic  1.31 us (1%)
    ppermute x4, waiting for transfers between devices, passed(): lax.ppermute(x, 'curve', [(i, (i + by) % curve) for i in range(curve)])  24.8 us
    ppermute x4, starting transfers between devices, passed(): lax.ppermute(x, 'curve', [(i, (i + by) % curve) for i in range(curve)])  15.2 us
    pallas_call x1, Pallas kernels, shards(): pl.pallas_call(functools.partial(cross_kernel, factor), in_specs=[SMEM] +...  14.7 us
    all_to_all x1, starting transfers between devices, shards(): received = lax.all_to_all(pieces, 'curve', 0, 0)  11.2 us
    pallas_call x1, Pallas kernels, shards(): pl.pallas_call(local_kernel, in_specs=[SMEM] + [VMEM] * 6, out_specs=[ANY...  8.42 us
    all_to_all x1, waiting for transfers between devices, shards(): received = lax.all_to_all(pieces, 'curve', 0, 0)  7.65 us
    all_to_all x1, starting transfers between devices, shards(): gathered = lax.all_to_all(totals, 'curve', 0, 0)  5.48 us
    ppermute x8, starting transfers between devices, swapped(): return lax.ppermute(x, 'mp', [(i, i ^ bit) for i in range(4)])  5.47 us
  transfers between devices with their start and end apart: 14, of which 7 were waited for; matrix products, arithmetic and copies ran while one was open for 1% of the time, Pallas kernels for 13%

profile of v3, /device:TPU:16, one launch (start us, length us, event | category | flops | bytes accessed | tf_op | source)
XLA Modules:
  0.0 116.2 jit_solution(11116303461329864128)
XLA Ops:
  1.3 0.6 pad_add_fusion.scal
  1.9 4.6 %halo.1 = (bf16[2,256,512]{2,1,0:T(8,128)(2,1)}, bf16[2,272,512]{2,1,0:T(8,128)(2,1)}) custom-call(s32[4]{0:T(128)} %pad_add_fusion.scal, s32[3,1024]{1,0:T(4,128)} %order.5, bf16[3,1024,512]{2,1,0:T(8,128)(2,1)} %points.3, bf16[3,1024,512]{2,1,0:T(8,128)(2,1)} %cotangent.5), custom_call_target="tpu_custom_call" | custom-call | tf_op jit(solution)/shard_map/halo/pallas_call | solution.py:443
  6.5 8.8 %collective-permute-start = (bf16[2,256,512]{2,1,0:T(8,128)(2,1)}, bf16[2,256,512]{2,1,0:T(8,128)(2,1)S(1)}, u32[]{:S(2)}, u32[]{:S(2)}) collective-permute-start(bf16[2,256,512]{2,1,0:T(8,128)(2,1)} %get-tuple-element.37), channel_id=1, source_target_pairs={{0,252},{4,0},{8,4},{12,8},{16,12},{20,16},{24,20},{28,24},{32,28}... | collective-permute-start | bytes 1572872 | tf_op jit(solution)/shard_map/ppermute | solution.py:438
  15.3 0.0 collective-permute-start.1
  15.3 8.4 %local.1 = (bf16[2,128,2048]{2,1,0:T(8,128)(2,1)}, bf16[2,128,2048]{2,1,0:T(8,128)(2,1)}, f32[2,2048]{1,0:T(2,128)}, bf16[2,128,1024]{2,1,0:T(8,128)(2,1)}, f32[...) custom-call(s32[4]{0:T(128)} %pad_add_fusion.scal, ...), custom_call_target="tpu_custom_call" | custom-call | flops 16000000000 | bytes 16000000 | tf_op jit(solution)/shard_map/local/pallas_call | solution.py:487
  23.8 3.1 %collective-permute-done.pull = bf16[2,256,512]{2,1,0:T(8,128)(2,1)S(1)} collective-permute-done((bf16[2,256,512]{2,1,0:T(8,128)(2,1)}, bf16[2,256,512]{2,1,0:T(8,128)(2,1)S(1)}, u32[]{:S(2)}, u32[]{:S(2)}) %collective-permute-start) | collective-permute-done | bytes 524320 | tf_op jit(solution)/shard_map/ppermute | solution.py:438
  26.8 7.0 %collective-permute-done.1.push = bf16[2,272,512]{2,1,0:T(8,128)(2,1)S(1)} collective-permute-done((bf16[2,272,512]{2,1,0:T(8,128)(2,1)}, bf16[2,272,512]{2,1,0:T(8,128)(2,1)S(1)}, u32[]{:S(2)}, u32[]{:S(2)}) %collective-permute-start.1) | collective-permute-done | bytes 557088 | tf_op jit(solution)/shard_map/ppermute | solution.py:438
  33.9 0.0 collective-permute-start.3
  33.9 0.5 collective-permute-start.2
  34.4 2.2 %collective-permute-done.2.pull_other = bf16[2,256,512]{2,1,0:T(8,128)(2,1)S(1)} collective-permute-done((bf16[2,256,512]{2,1,0:T(8,128)(2,1)S(1)}, bf16[2,256,512]{2,1,0:T(8,128)(2,1)S(1)}, u32[]{:S(2)}, u32[]{:S(2)}) %collective-permute-start.2) | collective-permute-done | bytes 524320 | tf_op jit(solution)/shard_map/ppermute | solution.py:441
  36.6 0.0 collective-permute-done.3.push_other
  36.6 0.0 copy-done.10
  36.6 0.0 copy-done.8
  36.6 0.8 copy-done.11
  37.3 0.2 copy-done.9
  37.5 14.7 %cross.1 = (bf16[2,128,2048]{2,1,0:T(8,128)(2,1)}, bf16[2,128,2048]{2,1,0:T(8,128)(2,1)}, f32[2,2048]{1,0:T(2,128)}, bf16[2,128,1024]{2,1,0:T(8,128)(2,1)}, f32[...) custom-call(s32[4]{0:T(128)} %pad_add_fusion.scal, ...), custom_call_target="tpu_custom_call", output_to_operand_aliasing={{0}: (5, {}), {1}: (6, {})} | custom-call | flops 4000000000 | bytes 8000000 | tf_op jit(solution)/shard_map/cross/pallas_call | solution.py:505
  52.2 0.0 copy-start.5
  52.3 0.2 collective-permute-start.4
  52.5 11.2 %all-to-all-start = ((bf16[64,32,128]{2,1,0:T(8,128)(2,1)}), bf16[64,32,128]{2,1,0:T(8,128)(2,1)S(1)}, u32[]{:S(2)}, u32[]{:S(2)}) async-start(bf16[64,32,128]{2,1,0:T(8,128)(2,1)} %get-tuple-element.65), calls=%async_computation | async-start | bytes 1048576 | tf_op jit(solution)/shard_map/all_to_all | solution.py:520
  63.7 0.2 collective-permute-start.5
  63.8 0.4 collective-permute-start.6
  64.3 1.0 collective-permute-done.6
  65.3 0.7 add.9.gain
  66.0 0.6 collective-permute-start.7
  66.6 0.0 collective-permute-done.5.stats_received
  66.6 0.0 collective-permute-done.4.received
  66.6 1.2 %copy-done.1 = bf16[2,128,2048]{2,1,0:T(8,128)(2,1)S(1)} copy-done((bf16[2,128,2048]{2,1,0:T(8,128)(2,1)S(1)}, bf16[2,128,2048]{2,1,0:T(8,128)(2,1)}, u32[]{:S(2)}) %copy-start.1) | copy-done | bytes 1048600
  67.8 0.7 copy-done.3
  68.5 1.0 pair.1
  69.5 1.5 %collective-permute-done.7.gain_received = f32[1,512]{1,0:T(1,128)S(1)} collective-permute-done((f32[1,512]{1,0:T(1,128)S(1)}, f32[1,512]{1,0:T(1,128)S(1)}, u32[]{:S(2)}, u32[]{:S(2)}) %collective-permute-start.7) | collective-permute-done | bytes 2080 | tf_op jit(solution)/shard_map/ppermute | solution.py:441
  71.1 1.7 %collective-permute-start.8 = (bf16[128,2048]{1,0:T(8,128)(2,1)S(1)}, bf16[128,2048]{1,0:T(8,128)(2,1)S(1)}, u32[]{:S(2)}, u32[]{:S(2)}) collective-permute-start(bf16[128,2048]{1,0:T(8,128)(2,1)S(1)} %get-tuple-element.58), channel_id=1, source_target_pairs={{0,2},{1,3},{2,0},{3,1},{4,6},{5,7},{6,4},{7,5},{8,10},{9,11},{10,... | collective-permute-start | bytes 1572872 | tf_op jit(solution)/shard_map/ppermute | solution.py:441
  72.8 1.8 %collective-permute-start.9 = (f32[2,2048]{1,0:T(2,128)S(1)}, f32[2,2048]{1,0:T(2,128)S(1)}, u32[]{:S(2)}, u32[]{:S(2)}) collective-permute-start(f32[2,2048]{1,0:T(2,128)S(1)} %get-tuple-element.59.stats), channel_id=1, source_target_pairs={{0,2},{1,3},{2,0},{3,1},{4,6},{5,7},{6,4},{7,5},{8,10},{9,11},{10,... | collective-permute-start | bytes 49160 | tf_op jit(solution)/shard_map/ppermute | solution.py:441
  74.6 7.6 %all-to-all-done.received = bf16[64,32,128]{2,1,0:T(8,128)(2,1)S(1)} async-done(((bf16[64,32,128]{2,1,0:T(8,128)(2,1)}), bf16[64,32,128]{2,1,0:T(8,128)(2,1)S(1)}, u32[]{:S(2)}, u32[]{:S(2)}) %all-to-all-start) | async-done | bytes 524320 | tf_op jit(solution)/shard_map/all_to_all | solution.py:520
  82.2 1.5 %total.1 = bf16[64,40,128]{2,1,0:T(8,128)(2,1)} custom-call(s32[4]{0:T(128)S(1)} %copy-done.4, bf16[64,32,128]{2,1,0:T(8,128)(2,1)S(1)} %all-to-all-done.received, f32[1,512]{1,0:T(1,128)S(1)} %add.9.gain, f32[1,512]{1,0:T(1,128)S(1)} %collective-permute-done.7.gain_received), custom_call_target="tpu_custom_call" | custom-call | tf_op jit(solution)/shard_map/total/pallas_call | solution.py:559
  83.8 5.5 %all-to-all-start.1 = ((bf16[64,40,128]{2,1,0:T(8,128)(2,1)}), bf16[64,40,128]{2,1,0:T(8,128)(2,1)S(1)}, u32[]{:S(2)}, u32[]{:S(2)}) async-start(bf16[64,40,128]{2,1,0:T(8,128)(2,1)} %total.1), calls=%async_computation.1 | async-start | bytes 1310720 | tf_op jit(solution)/shard_map/all_to_all | solution.py:567
  89.3 0.0 collective-permute-done.9.stats_received
  89.3 0.0 collective-permute-done.8.received
  89.3 0.0 copy-start
  89.3 0.0 copy-start.2
  89.3 1.2 branch.1
  90.5 1.6 %collective-permute-start.10 = (bf16[128,512]{1,0:T(8,128)(2,1)S(1)}, bf16[128,512]{1,0:T(8,128)(2,1)S(1)}, u32[]{:S(2)}, u32[]{:S(2)}) collective-permute-start(bf16[128,512]{1,0:T(8,128)(2,1)S(1)} %get-tuple-element.63), channel_id=1, source_target_pairs={{0,4},{4,8},{8,12},{12,16},{16,20},{20,24},{24,28},{28,32},{32,36}... | collective-permute-start | bytes 393224 | tf_op jit(solution)/shard_map/ppermute | solution.py:438
  92.1 4.7 %collective-permute-start.11 = (bf16[128,512]{1,0:T(8,128)(2,1)S(1)}, bf16[128,512]{1,0:T(8,128)(2,1)S(1)}, u32[]{:S(2)}, u32[]{:S(2)}) collective-permute-start(bf16[128,512]{1,0:T(8,128)(2,1)S(1)} %get-tuple-element.64), channel_id=1, source_target_pairs={{0,252},{4,0},{8,4},{12,8},{16,12},{20,16},{24,20},{28,24},{32,28}... | collective-permute-start | bytes 393224 | tf_op jit(solution)/shard_map/ppermute | solution.py:438
  96.8 14.7 %collective-permute-done.10.from_before = bf16[128,512]{1,0:T(8,128)(2,1)S(1)} collective-permute-done((bf16[128,512]{1,0:T(8,128)(2,1)S(1)}, bf16[128,512]{1,0:T(8,128)(2,1)S(1)}, u32[]{:S(2)}, u32[]{:S(2)}) %collective-permute-start.10) | collective-permute-done | bytes 131104 | tf_op jit(solution)/shard_map/ppermute | solution.py:438
  111.5 0.0 collective-permute-done.11.from_after
  111.5 0.0 copy-done
  111.6 3.5 %place.1 = bf16[3,1024,128]{2,1,0:T(8,128)(2,1)} custom-call(s32[4]{0:T(128)S(1)} %copy-done.4, s32[3,1024]{1,0:T(4,128)S(1)} %copy-done.2, s32[1]{0:T(128)} %get-tuple-element.51.before, bf16[3,1024,512]{2,1,0:T(8,128)(2,1)S(1)} %copy-done, bf16[2,128,1024]{2,1,0:T(8,128)(2,1)S(1)} %get-tuple-element.62.branch, ...), custom_call_target="tpu_custom_call" | custom-call | flops 10000000000 | bytes 1000 | tf_op jit(solution)/shard_map/place/pallas_call | solution.py:569
  115.1 0.0 all-to-all-done.1.received
  115.1 1.1 finish.1
  (14 shorter events, 0.0 us)
Async XLA Ops:
  6.5 20.3 %collective-permute-start = (bf16[2,256,512]{2,1,0:T(8,128)(2,1)}, bf16[2,256,512]{2,1,0:T(8,128)(2,1)S(1)}, u32[]{:S(2)}, u32[]{:S(2)}) collective-permute-start(bf16[2,256,512]{2,1,0:T(8,128)(2,1)} %get-tuple-element.37), channel_id=1, source_target_pairs={{0,252},{4,0},{8,4},{12,8},{16,12},{20,16},{24,20},{28,24},{32,28}... | collective-permute-start | bytes 1572872 | tf_op jit(solution)/shard_map/ppermute | solution.py:438
  15.3 18.5 %collective-permute-start.1 = (bf16[2,272,512]{2,1,0:T(8,128)(2,1)}, bf16[2,272,512]{2,1,0:T(8,128)(2,1)S(1)}, u32[]{:S(2)}, u32[]{:S(2)}) collective-permute-start(bf16[2,272,512]{2,1,0:T(8,128)(2,1)} %get-tuple-element.38), channel_id=1, source_target_pairs={{0,4},{4,8},{8,12},{12,16},{16,20},{20,24},{24,28},{28,32},{32,36}... | collective-permute-start | bytes 1671176 | tf_op jit(solution)/shard_map/ppermute | solution.py:438
  26.8 9.7 %copy-start.10 = (bf16[2,256,512]{2,1,0:T(8,128)(2,1)}, bf16[2,256,512]{2,1,0:T(8,128)(2,1)S(1)}, u32[]{:S(2)}) copy-start(bf16[2,256,512]{2,1,0:T(8,128)(2,1)S(1)} %collective-permute-done.pull) | copy-start | bytes 1572868
  33.9 2.7 %copy-start.8 = (bf16[2,272,512]{2,1,0:T(8,128)(2,1)}, bf16[2,272,512]{2,1,0:T(8,128)(2,1)S(1)}, u32[]{:S(2)}) copy-start(bf16[2,272,512]{2,1,0:T(8,128)(2,1)S(1)} %collective-permute-done.1.push) | copy-start | bytes 1671172
  33.9 2.7 %collective-permute-start.3 = (bf16[2,272,512]{2,1,0:T(8,128)(2,1)S(1)}, bf16[2,272,512]{2,1,0:T(8,128)(2,1)S(1)}, u32[]{:S(2)}, u32[]{:S(2)}) collective-permute-start(bf16[2,272,512]{2,1,0:T(8,128)(2,1)S(1)} %collective-permute-done.1.push), channel_id=1, source_target_pairs={{0,1},{1,0},{2,3},{3,2},{4,5},{5,4},{6,7},{7,6},{8,9},{9,8},{10,11... | collective-permute-start | bytes 1671176 | tf_op jit(solution)/shard_map/ppermute | solution.py:441
  33.9 2.7 %collective-permute-start.2 = (bf16[2,256,512]{2,1,0:T(8,128)(2,1)S(1)}, bf16[2,256,512]{2,1,0:T(8,128)(2,1)S(1)}, u32[]{:S(2)}, u32[]{:S(2)}) collective-permute-start(bf16[2,256,512]{2,1,0:T(8,128)(2,1)S(1)} %collective-permute-done.pull), channel_id=1, source_target_pairs={{0,1},{1,0},{2,3},{3,2},{4,5},{5,4},{6,7},{7,6},{8,9},{9,8},{10,11... | collective-permute-start | bytes 1572872 | tf_op jit(solution)/shard_map/ppermute | solution.py:441
  36.6 0.8 copy-start.11
  36.6 1.0 copy-start.9
  37.5 29.0 %copy-start.4 = (s32[4]{0:T(128)S(1)}, s32[4]{0:T(128)}, u32[]{:S(2)}) copy-start(s32[4]{0:T(128)} %pad_add_fusion.scal) | copy-start | bytes 52
  52.2 37.1 %copy-start.5 = (f32[512]{0:T(512)S(1)}, f32[512]{0:T(512)}, u32[]{:S(2)}) copy-start(f32[512]{0:T(512)} %param.11) | copy-start | bytes 6148
  52.2 37.1 %copy-start.6 = (bf16[2,128,1024]{2,1,0:T(8,128)(2,1)S(1)}, bf16[2,128,1024]{2,1,0:T(8,128)(2,1)}, u32[]{:S(2)}) copy-start(bf16[2,128,1024]{2,1,0:T(8,128)(2,1)} %get-tuple-element.60.unit) | copy-start | bytes 1572868
  52.3 37.1 %copy-start.7 = (f32[2,8,1024]{2,1,0:T(8,128)S(1)}, f32[2,8,1024]{2,1,0:T(8,128)}, u32[]{:S(2)}) copy-start(f32[2,8,1024]{2,1,0:T(8,128)} %get-tuple-element.61.stat) | copy-start | bytes 196612
  52.3 14.3 %collective-permute-start.4 = (bf16[2,128,2048]{2,1,0:T(8,128)(2,1)}, bf16[2,128,2048]{2,1,0:T(8,128)(2,1)S(1)}, u32[]{:S(2)}, u32[]{:S(2)}) collective-permute-start(bf16[2,128,2048]{2,1,0:T(8,128)(2,1)} %get-tuple-element.53), channel_id=1, source_target_pairs={{0,1},{1,0},{2,3},{3,2},{4,5},{5,4},{6,7},{7,6},{8,9},{9,8},{10,11... | collective-permute-start | bytes 3145736 | tf_op jit(solution)/shard_map/ppermute | solution.py:441
  52.5 29.7 %all-to-all-start = ((bf16[64,32,128]{2,1,0:T(8,128)(2,1)}), bf16[64,32,128]{2,1,0:T(8,128)(2,1)S(1)}, u32[]{:S(2)}, u32[]{:S(2)}) async-start(bf16[64,32,128]{2,1,0:T(8,128)(2,1)} %get-tuple-element.65), calls=%async_computation | async-start | bytes 1048576 | tf_op jit(solution)/shard_map/all_to_all | solution.py:520
  63.7 2.9 %collective-permute-start.5 = (f32[2,2048]{1,0:T(2,128)}, f32[2,2048]{1,0:T(2,128)S(1)}, u32[]{:S(2)}, u32[]{:S(2)}) collective-permute-start(f32[2,2048]{1,0:T(2,128)} %get-tuple-element.54.stats), channel_id=1, source_target_pairs={{0,1},{1,0},{2,3},{3,2},{4,5},{5,4},{6,7},{7,6},{8,9},{9,8},{10,11... | collective-permute-start | bytes 49160 | tf_op jit(solution)/shard_map/ppermute | solution.py:441
  63.8 1.5 %collective-permute-start.6 = (f32[1,512]{1,0:T(1,128)}, f32[1,512]{1,0:T(1,128)S(1)}, u32[]{:S(2)}, u32[]{:S(2)}) collective-permute-start(f32[1,512]{1,0:T(1,128)} %get-tuple-element.57), channel_id=1, source_target_pairs={{0,1},{1,0},{2,3},{3,2},{4,5},{5,4},{6,7},{7,6},{8,9},{9,8},{10,11... | collective-permute-start | bytes 6152 | tf_op jit(solution)/shard_map/ppermute | solution.py:441
  66.0 5.1 %collective-permute-start.7 = (f32[1,512]{1,0:T(1,128)S(1)}, f32[1,512]{1,0:T(1,128)S(1)}, u32[]{:S(2)}, u32[]{:S(2)}) collective-permute-start(f32[1,512]{1,0:T(1,128)S(1)} %add.9.gain), channel_id=1, source_target_pairs={{0,2},{1,3},{2,0},{3,1},{4,6},{5,7},{6,4},{7,5},{8,10},{9,11},{10,... | collective-permute-start | bytes 6152 | tf_op jit(solution)/shard_map/ppermute | solution.py:441
  66.6 1.2 %copy-start.1 = (bf16[2,128,2048]{2,1,0:T(8,128)(2,1)S(1)}, bf16[2,128,2048]{2,1,0:T(8,128)(2,1)}, u32[]{:S(2)}) copy-start(bf16[2,128,2048]{2,1,0:T(8,128)(2,1)} %get-tuple-element.52.keep) | copy-start | bytes 3145732
  67.8 0.7 copy-start.3
  71.1 18.2 %collective-permute-start.8 = (bf16[128,2048]{1,0:T(8,128)(2,1)S(1)}, bf16[128,2048]{1,0:T(8,128)(2,1)S(1)}, u32[]{:S(2)}, u32[]{:S(2)}) collective-permute-start(bf16[128,2048]{1,0:T(8,128)(2,1)S(1)} %get-tuple-element.58), channel_id=1, source_target_pairs={{0,2},{1,3},{2,0},{3,1},{4,6},{5,7},{6,4},{7,5},{8,10},{9,11},{10,... | collective-permute-start | bytes 1572872 | tf_op jit(solution)/shard_map/ppermute | solution.py:441
  72.8 16.5 %collective-permute-start.9 = (f32[2,2048]{1,0:T(2,128)S(1)}, f32[2,2048]{1,0:T(2,128)S(1)}, u32[]{:S(2)}, u32[]{:S(2)}) collective-permute-start(f32[2,2048]{1,0:T(2,128)S(1)} %get-tuple-element.59.stats), channel_id=1, source_target_pairs={{0,2},{1,3},{2,0},{3,1},{4,6},{5,7},{6,4},{7,5},{8,10},{9,11},{10,... | collective-permute-start | bytes 49160 | tf_op jit(solution)/shard_map/ppermute | solution.py:441
  83.8 31.3 %all-to-all-start.1 = ((bf16[64,40,128]{2,1,0:T(8,128)(2,1)}), bf16[64,40,128]{2,1,0:T(8,128)(2,1)S(1)}, u32[]{:S(2)}, u32[]{:S(2)}) async-start(bf16[64,40,128]{2,1,0:T(8,128)(2,1)} %total.1), calls=%async_computation.1 | async-start | bytes 1310720 | tf_op jit(solution)/shard_map/all_to_all | solution.py:567
  89.3 22.2 %copy-start = (bf16[3,1024,512]{2,1,0:T(8,128)(2,1)S(1)}, bf16[3,1024,512]{2,1,0:T(8,128)(2,1)}, u32[]{:S(2)}) copy-start(bf16[3,1024,512]{2,1,0:T(8,128)(2,1)} %cotangent.5) | copy-start | bytes 9437188
  89.3 22.2 %copy-start.2 = (s32[3,1024]{1,0:T(4,128)S(1)}, s32[3,1024]{1,0:T(4,128)}, u32[]{:S(2)}) copy-start(s32[3,1024]{1,0:T(4,128)} %order.5) | copy-start | bytes 36868
  90.5 21.0 %collective-permute-start.10 = (bf16[128,512]{1,0:T(8,128)(2,1)S(1)}, bf16[128,512]{1,0:T(8,128)(2,1)S(1)}, u32[]{:S(2)}, u32[]{:S(2)}) collective-permute-start(bf16[128,512]{1,0:T(8,128)(2,1)S(1)} %get-tuple-element.63), channel_id=1, source_target_pairs={{0,4},{4,8},{8,12},{12,16},{16,20},{20,24},{24,28},{28,32},{32,36}... | collective-permute-start | bytes 393224 | tf_op jit(solution)/shard_map/ppermute | solution.py:438
  92.1 19.4 %collective-permute-start.11 = (bf16[128,512]{1,0:T(8,128)(2,1)S(1)}, bf16[128,512]{1,0:T(8,128)(2,1)S(1)}, u32[]{:S(2)}, u32[]{:S(2)}) collective-permute-start(bf16[128,512]{1,0:T(8,128)(2,1)S(1)} %get-tuple-element.64), channel_id=1, source_target_pairs={{0,252},{4,0},{8,4},{12,8},{16,12},{20,16},{24,20},{28,24},{32,28}... | collective-permute-start | bytes 393224 | tf_op jit(solution)/shard_map/ppermute | solution.py:438

commit v4 on v3

--- a/solution.py
+++ b/solution.py
@@ -20,6 +20,7 @@
 VMEM = pl.BlockSpec(memory_space=pltpu.VMEM)
 SMEM = pl.BlockSpec(memory_space=pltpu.SMEM)
 ANY = pl.BlockSpec(memory_space=pl.ANY)
+HBM = pl.BlockSpec(memory_space=pltpu.HBM)
 
 
 def mm(a, b):
@@ -47,25 +48,29 @@
     )
 
 
-def halo_kernel(scal, order, points, cotangent, pull, push, held, done):
+def halo_kernel(counts, order_i, points, cotangent, pull, push, order, held, done):
     rows = pull.shape[1]
     patch = points.shape[1]
     last = points.shape[0] - 1
+    core = lax.axis_index("mp") % 2
+    places = pltpu.make_async_copy(order_i, order, done.at[4])
+    places.start()
     copies = []
     for slot in (last, 0):
         for source in (points, cotangent):
             k = len(copies)
             copies.append(pltpu.make_async_copy(source.at[slot], held.at[k], done.at[k]))
             copies[-1].start()
-    count = jnp.zeros((16, push.shape[2]), F32) + scal[2].astype(F32)
+    count = jnp.zeros((16, push.shape[2]), F32) + counts[0].astype(F32)
+    push[0, rows:, :] = count.astype(BF16)
+    push[1, rows:, :] = count.astype(BF16)
+    places.wait()
     for k, (slot, base, out) in enumerate(((last, patch // 2, push), (0, 0, pull))):
-        at = pl.ds(pl.multiple_of(base + scal[0] * rows, rows), rows)
+        at = pl.ds(pl.multiple_of(base + core * rows, rows), rows)
         chosen = one_hot_rows(order[slot:slot + 1, at], patch)
         for j in range(2):
             copies[2 * k + j].wait()
             out[j, 0:rows, :] = mm(chosen, held[2 * k + j]).astype(BF16)
-    push[0, rows:, :] = count.astype(BF16)
-    push[1, rows:, :] = count.astype(BF16)
 
 
 def norm_half(x, gain, own):
@@ -165,8 +170,8 @@
     weights[D:D + 16, :] = split3(sums)
 
 
-def patch_core(core, p, nrm, dy, wt, wo, send, keep, stats, wacc,
-               prj, kr, vr, dat, att, gp, grads, scores, lows, weights, done):
+def patch_core(core, p, nrm, dy, weights, wt, wo, send, keep, stats, wacc,
+               prj, kr, vr, dat, att, gp, grads, scores, lows, done):
     project(nrm, dy, weights, wt, wo, prj, kr, vr, dat)
     attend(prj, kr, vr, dat, gp, att, scores, lows)
     patch = gp.shape[1]
@@ -208,13 +213,13 @@
 
 
 def local_kernel(scal, order, points, cotangent, gain, w3, wo,
-                 send, keep, stats, unit_o, inv_o, wacc, wt, nrm_o, dy_o,
+                 send, keep, stats, unit_o, inv_o, wacc, weights, wt, nrm_o, dy_o,
                  nrm, dy, own, *work):
     half = points.shape[1] // 2
     for t in range(3):
         wt[128 * t:128 * t + 128, :] = w3[t].astype(F32).T.astype(BF16)
     wacc[...] = jnp.zeros_like(wacc)
-    load_weights(w3, wt, gain, work[-2])
+    load_weights(w3, wt, gain, weights)
 
     whole = scal[2] > 1
 
@@ -232,7 +237,7 @@
 
         @pl.when(whole)
         def _():
-            patch_core(scal[0], p, nrm, dy, wt, wo, send, keep, stats, wacc, *work)
+            patch_core(scal[0], p, nrm, dy, weights, wt, wo, send, keep, stats, wacc, *work)
 
         @pl.when(jnp.logical_not(whole))
         def _():
@@ -246,9 +251,9 @@
 
 
 def cross_kernel(factor, scal, pull, pull_other, push, push_other, send_i, keep_i, wacc_i, nrm_i,
-                 dy_i, stats_i, unit_i, inv_i, gain, w3, wt, wo,
+                 dy_i, stats_i, unit_i, inv_i, weights_i, wt_i, wo_i, gain,
                  send, keep, stats, unit_o, inv_o, pieces, gain_o, pushed,
-                 flag, nrm_2, dy_2, own_2, arrived, *work_wacc):
+                 flag, nrm_2, dy_2, own_2, weights, wt, wo, arrived, *work_wacc):
     wacc, work = work_wacc[-1], work_wacc[:-1]
     half = nrm_i.shape[1]
     part = half // 2
@@ -257,6 +262,10 @@
     told = pltpu.make_async_copy(push.at[0, part:part + 16], flag, arrived.at[2, 0])
     told.start()
     copies = []
+    common = ((stats_i, stats), (unit_i, unit_o), (inv_i, inv_o), (weights_i, weights), (wt_i, wt),
+              (wo_i, wo))
+    common = [pltpu.make_async_copy(source, into, arrived.at[2, k + 1])
+              for k, (source, into) in enumerate(common)]
     for p, one, other in ((0, pull, pull_other), (1, push, push_other)):
         here, there = half * p, half * (1 - p)
         moves = [(nrm_i.at[p], nrm_2.at[p, here:here + half]),
@@ -270,11 +279,9 @@
                        for k, (source, into) in enumerate(moves)])
         for copy in copies[-1]:
             copy.start()
-    stats[...] = stats_i[...]
-    unit_o[...] = unit_i[...]
-    inv_o[...] = inv_i[...]
-    load_weights(w3, wt, gain, work[-2])
-
+        if p == 0:
+            for copy in common:
+                copy.start()
     @pl.when(light)
     def _():
         wacc[...] = jnp.zeros_like(wacc)
@@ -286,6 +293,8 @@
         copy.wait()
 
     told.wait()
+    for copy in common:
+        copy.wait()
     before = jnp.max(flag[...].astype(F32)).astype(jnp.int32)
     pushed[0] = before
     patches = jnp.where(light, jnp.where(before > 1, 2, 1), 0)
@@ -306,7 +315,8 @@
             nrm[pl.ds(there, half), :] = normed
             unit_o[p, :, pl.ds(there, half)] = unit
             inv_o[p, :, pl.ds(there, half)] = inverse
-            patch_core(scal[0], p, nrm, dy_2.at[p], wt, wo, send, keep, stats, wacc, *work)
+            patch_core(scal[0], p, nrm, dy_2.at[p], weights, wt, wo, send, keep, stats, wacc,
+                       *work)
 
         return carry
 
@@ -442,13 +452,17 @@
 
     pull, push = pl.pallas_call(
         halo_kernel,
-        in_specs=[SMEM, VMEM, ANY, ANY],
+        in_specs=[SMEM, ANY, ANY, ANY],
         out_specs=[VMEM] * 2,
         out_shape=[sds((2, half // 2, width), BF16), sds((2, half // 2 + 16, width), BF16)],
-        scratch_shapes=[pltpu.VMEM((4, patch, width), BF16), pltpu.SemaphoreType.DMA((4,))],
+        scratch_shapes=[
+            pltpu.VMEM((slots, patch), jnp.int32),
+            pltpu.VMEM((4, patch, width), BF16),
+            pltpu.SemaphoreType.DMA((5,)),
+        ],
         compiler_params=params(60),
         name="halo",
-    )(scal, order, points, cotangent)
+    )(counts, order, points, cotangent)
     pull, push = passed(pull, -1), passed(push, 1)
 
     rows = [
@@ -461,7 +475,10 @@
         pltpu.VMEM((2, patch, width), BF16),
         pltpu.VMEM((2, patch, width), BF16),
         pltpu.VMEM((2, half, width), BF16),
-        pltpu.SemaphoreType.DMA((3, 6)),
+        pltpu.VMEM((width + 16, 384), BF16),
+        pltpu.VMEM((384, width), BF16),
+        pltpu.VMEM((128, width), BF16),
+        pltpu.SemaphoreType.DMA((3, 7)),
     ]
     work = [
         pltpu.VMEM((384, patch), BF16),
@@ -473,7 +490,6 @@
         pltpu.VMEM((width, patch), BF16),
         pltpu.VMEM((2, patch, patch), F32),
         pltpu.VMEM((2, patch, patch), BF16),
-        pltpu.VMEM((width + 16, 384), BF16),
         pltpu.SemaphoreType.DMA((4,)),
     ]
     lanes = 2 * patch
@@ -484,12 +500,13 @@
         sds((2, 128, patch), BF16),
         sds((2, 8, patch), F32),
     ]
-    send, keep, stats, unit, inverse, wacc, wt, nrm, dy = pl.pallas_call(
+    send, keep, stats, unit, inverse, wacc, weights, wt, nrm, dy = pl.pallas_call(
         local_kernel,
         in_specs=[SMEM] + [VMEM] * 6,
-        out_specs=[ANY] * 2 + [VMEM] * 7,
+        out_specs=[ANY] * 2 + [VMEM] * 8,
         out_shape=shared + [
             sds((512, width), F32),
+            sds((width + 16, 384), BF16),
             sds((384, width), BF16),
             sds((2, half, width), BF16),
             sds((2, half, width), BF16),
@@ -504,7 +521,7 @@
     factor = 1.0 / math.sqrt(curve * slots * patch)
     send, keep, stats, unit, inverse, pieces, gain_part, before = pl.pallas_call(
         functools.partial(cross_kernel, factor),
-        in_specs=[SMEM] + [ANY] * 9 + [VMEM] * 7,
+        in_specs=[SMEM] + [ANY] * 4 + [HBM] * 11 + [VMEM],
         out_specs=[ANY] * 2 + [VMEM] * 5 + [SMEM],
         out_shape=shared + [
             sds((64, 32, 128), BF16), sds((1, width), F32), sds((1,), jnp.int32)
@@ -515,7 +532,7 @@
         cost_estimate=cost(4 * 10**9, 8 * 10**6),
         name="cross",
     )(scal, pull, swapped(pull, 1), push, swapped(push, 1), send, keep, wacc, nrm, dy, stats, unit,
-      inverse, gain_row, w3, wt, w_out)
+      inverse, weights, wt, w_out, gain_row)
 
     received = lax.all_to_all(pieces, "curve", 0, 0)
     gain_part = gain_part + swapped(gain_part, 1)

time: 117 us -> 117 us (level)
  Pallas kernels: 35.9 us -> 48.7 us
  waiting for transfers between devices: 37.2 us -> 27.4 us
  starting transfers between devices: 37.3 us -> 33.7 us
    pallas_call x1, Pallas kernels: 8.42 us -> 30.3 us  [shards(): pl.pallas_call(local_kernel, in_specs=[SMEM] + [VMEM] * 6, out_specs=[ANY...]
    ppermute x4, waiting for transfers between devices: 24.8 us -> 14.7 us  [passed(): lax.ppermute(x, 'curve', [(i, (i + by) % curve) for i in range(curve)])]
    pallas_call x1, Pallas kernels: 14.7 us -> 5.37 us  [shards(): pl.pallas_call(functools.partial(cross_kernel, factor), in_specs=[SMEM] +...]
    all_to_all x1, starting transfers between devices: 11.2 us -> 7.72 us  [shards(): received = lax.all_to_all(pieces, 'curve', 0, 0)]
  transfers between devices with their start and end apart: 14 -> 14, of which waited for: 7 -> 5; matrix products, arithmetic and copies ran while one was open for 1% -> 1% of each run, Pallas kernels for 13% -> 33%
where the time goes in v4:
time: 117 us; the launch traced here: 115 us
  Pallas kernels  48.7 us (42%)
  starting transfers between devices  33.7 us (29%)
  waiting for transfers between devices  27.4 us (23%)
  local copies, waits for them, and re-layouts  2.93 us (3%)
  between operations  1.5 us (1%)
  other arithmetic  1.22 us (1%)
    pallas_call x1, Pallas kernels, shards(): pl.pallas_call(local_kernel, in_specs=[SMEM] + [VMEM] * 6, out_specs=[ANY...  30.3 us
    ppermute x4, starting transfers between devices, passed(): lax.ppermute(x, 'curve', [(i, (i + by) % curve) for i in range(curve)])  15.2 us
    ppermute x4, waiting for transfers between devices, passed(): lax.ppermute(x, 'curve', [(i, (i + by) % curve) for i in range(curve)])  14.7 us
    all_to_all x1, starting transfers between devices, shards(): received = lax.all_to_all(pieces, 'curve', 0, 0)  7.72 us
    all_to_all x1, waiting for transfers between devices, shards(): received = lax.all_to_all(pieces, 'curve', 0, 0)  7.69 us
    all_to_all x1, starting transfers between devices, shards(): gathered = lax.all_to_all(totals, 'curve', 0, 0)  5.48 us
    pallas_call x1, Pallas kernels, shards(): pl.pallas_call(functools.partial(cross_kernel, factor), in_specs=[SMEM] +...  5.37 us
    ppermute x8, starting transfers between devices, swapped(): return lax.ppermute(x, 'mp', [(i, i ^ bit) for i in range(4)])  5.32 us
  transfers between devices with their start and end apart: 14, of which 5 were waited for; matrix products, arithmetic and copies ran while one was open for 1% of the time, Pallas kernels for 33%

profile of v4, /device:TPU:16, one launch (start us, length us, event | category | flops | bytes accessed | tf_op | source)
XLA Modules:
  0.0 115.5 jit_solution(2122126205466065009)
XLA Ops:
  1.3 3.9 %halo.1 = (bf16[2,256,512]{2,1,0:T(8,128)(2,1)}, bf16[2,272,512]{2,1,0:T(8,128)(2,1)}) custom-call(s32[1]{0:T(128)S(6)} %copy.15.counts, s32[3,1024]{1,0:T(4,128)} %order.3, bf16[3,1024,512]{2,1,0:T(8,128)(2,1)} %points.3, bf16[3,1024,512]{2,1,0:T(8,128)(2,1)} %cotangent.5), custom_call_target="tpu_custom_call" | custom-call | tf_op jit(solution)/shard_map/halo/pallas_call | solution.py:453
  5.1 8.8 %collective-permute-start = (bf16[2,256,512]{2,1,0:T(8,128)(2,1)}, bf16[2,256,512]{2,1,0:T(8,128)(2,1)S(1)}, u32[]{:S(2)}, u32[]{:S(2)}) collective-permute-start(bf16[2,256,512]{2,1,0:T(8,128)(2,1)} %get-tuple-element.38), channel_id=1, source_target_pairs={{0,252},{4,0},{8,4},{12,8},{16,12},{20,16},{24,20},{28,24},{32,28}... | collective-permute-start | bytes 1572872 | tf_op jit(solution)/shard_map/ppermute | solution.py:448
  14.0 0.0 collective-permute-start.1
  14.0 0.6 pad_add_fusion.scal
  14.6 30.3 %local.1 = (bf16[2,128,2048]{2,1,0:T(8,128)(2,1)}, bf16[2,128,2048]{2,1,0:T(8,128)(2,1)}, f32[2,2048]{1,0:T(2,128)}, bf16[2,128,1024]{2,1,0:T(8,128)(2,1)}, f32[...) custom-call(s32[4]{0:T(128)} %pad_add_fusion.scal, ...), custom_call_target="tpu_custom_call" | custom-call | flops 16000000000 | bytes 16000000 | tf_op jit(solution)/shard_map/local/pallas_call | solution.py:503
  44.9 0.0 collective-permute-done.pull
  44.9 0.0 copy-start.10
  44.9 0.0 collective-permute-done.1.push
  44.9 0.0 copy-start.8
  45.0 0.1 collective-permute-start.3
  45.1 0.5 collective-permute-start.2
  45.6 2.2 %collective-permute-done.2.pull_other = bf16[2,256,512]{2,1,0:T(8,128)(2,1)S(1)} collective-permute-done((bf16[2,256,512]{2,1,0:T(8,128)(2,1)S(1)}, bf16[2,256,512]{2,1,0:T(8,128)(2,1)S(1)}, u32[]{:S(2)}, u32[]{:S(2)}) %collective-permute-start.2) | collective-permute-done | bytes 524320 | tf_op jit(solution)/shard_map/ppermute | solution.py:451
  47.8 0.0 collective-permute-done.3.push_other
  47.8 0.8 copy-done.11
  48.5 0.2 copy-done.9
  48.7 5.4 %cross.1 = (bf16[2,128,2048]{2,1,0:T(8,128)(2,1)}, bf16[2,128,2048]{2,1,0:T(8,128)(2,1)}, f32[2,2048]{1,0:T(2,128)}, bf16[2,128,1024]{2,1,0:T(8,128)(2,1)}, f32[...) custom-call(s32[4]{0:T(128)} %pad_add_fusion.scal, ...), custom_call_target="tpu_custom_call", output_to_operand_aliasing={{0}: (5, {}), {1}: (6, {})} | custom-call | flops 4000000000 | bytes 8000000 | tf_op jit(solution)/shard_map/cross/pallas_call | solution.py:522
  54.1 0.0 copy-start.5
  54.1 0.2 collective-permute-start.4
  54.4 7.7 %all-to-all-start = ((bf16[64,32,128]{2,1,0:T(8,128)(2,1)}), bf16[64,32,128]{2,1,0:T(8,128)(2,1)S(1)}, u32[]{:S(2)}, u32[]{:S(2)}) async-start(bf16[64,32,128]{2,1,0:T(8,128)(2,1)} %get-tuple-element.67), calls=%async_computation | async-start | bytes 1048576 | tf_op jit(solution)/shard_map/all_to_all | solution.py:537
  62.1 0.2 collective-permute-start.5
  62.3 0.4 collective-permute-start.6
  62.7 1.0 collective-permute-done.6
  63.7 0.6 add.9.gain
  64.3 0.4 collective-permute-start.7
  64.7 0.0 collective-permute-done.5.stats_received
  64.7 0.0 collective-permute-done.4.received
  64.7 1.2 %copy-done.1 = bf16[2,128,2048]{2,1,0:T(8,128)(2,1)S(1)} copy-done((bf16[2,128,2048]{2,1,0:T(8,128)(2,1)S(1)}, bf16[2,128,2048]{2,1,0:T(8,128)(2,1)}, u32[]{:S(2)}) %copy-start.1) | copy-done | bytes 1048600
  66.0 0.7 copy-done.3
  66.7 1.0 pair.1
  67.7 1.8 %collective-permute-done.7.gain_received = f32[1,512]{1,0:T(1,128)S(1)} collective-permute-done((f32[1,512]{1,0:T(1,128)S(1)}, f32[1,512]{1,0:T(1,128)S(1)}, u32[]{:S(2)}, u32[]{:S(2)}) %collective-permute-start.7) | collective-permute-done | bytes 2080 | tf_op jit(solution)/shard_map/ppermute | solution.py:451
  69.4 1.7 %collective-permute-start.8 = (bf16[128,2048]{1,0:T(8,128)(2,1)S(1)}, bf16[128,2048]{1,0:T(8,128)(2,1)S(1)}, u32[]{:S(2)}, u32[]{:S(2)}) collective-permute-start(bf16[128,2048]{1,0:T(8,128)(2,1)S(1)} %get-tuple-element.60), channel_id=1, source_target_pairs={{0,2},{1,3},{2,0},{3,1},{4,6},{5,7},{6,4},{7,5},{8,10},{9,11},{10,... | collective-permute-start | bytes 1572872 | tf_op jit(solution)/shard_map/ppermute | solution.py:451
  71.2 1.8 %collective-permute-start.9 = (f32[2,2048]{1,0:T(2,128)S(1)}, f32[2,2048]{1,0:T(2,128)S(1)}, u32[]{:S(2)}, u32[]{:S(2)}) collective-permute-start(f32[2,2048]{1,0:T(2,128)S(1)} %get-tuple-element.61.stats), channel_id=1, source_target_pairs={{0,2},{1,3},{2,0},{3,1},{4,6},{5,7},{6,4},{7,5},{8,10},{9,11},{10,... | collective-permute-start | bytes 49160 | tf_op jit(solution)/shard_map/ppermute | solution.py:451
  73.0 7.7 %all-to-all-done.received = bf16[64,32,128]{2,1,0:T(8,128)(2,1)S(1)} async-done(((bf16[64,32,128]{2,1,0:T(8,128)(2,1)}), bf16[64,32,128]{2,1,0:T(8,128)(2,1)S(1)}, u32[]{:S(2)}, u32[]{:S(2)}) %all-to-all-start) | async-done | bytes 524320 | tf_op jit(solution)/shard_map/all_to_all | solution.py:537
  80.7 1.5 %total.1 = bf16[64,40,128]{2,1,0:T(8,128)(2,1)} custom-call(s32[4]{0:T(128)S(1)} %copy-done.4, bf16[64,32,128]{2,1,0:T(8,128)(2,1)S(1)} %all-to-all-done.received, f32[1,512]{1,0:T(1,128)S(1)} %add.9.gain, f32[1,512]{1,0:T(1,128)S(1)} %collective-permute-done.7.gain_received), custom_call_target="tpu_custom_call" | custom-call | tf_op jit(solution)/shard_map/total/pallas_call | solution.py:576
  82.2 5.5 %all-to-all-start.1 = ((bf16[64,40,128]{2,1,0:T(8,128)(2,1)}), bf16[64,40,128]{2,1,0:T(8,128)(2,1)S(1)}, u32[]{:S(2)}, u32[]{:S(2)}) async-start(bf16[64,40,128]{2,1,0:T(8,128)(2,1)} %total.1), calls=%async_computation.1 | async-start | bytes 1310720 | tf_op jit(solution)/shard_map/all_to_all | solution.py:584
  87.7 0.0 collective-permute-done.9.stats_received
  87.7 0.0 collective-permute-done.8.received
  87.7 0.0 copy-start
  87.8 0.0 copy-start.2
  87.8 1.2 branch.1
  88.9 1.6 %collective-permute-start.10 = (bf16[128,512]{1,0:T(8,128)(2,1)S(1)}, bf16[128,512]{1,0:T(8,128)(2,1)S(1)}, u32[]{:S(2)}, u32[]{:S(2)}) collective-permute-start(bf16[128,512]{1,0:T(8,128)(2,1)S(1)} %get-tuple-element.65), channel_id=1, source_target_pairs={{0,4},{4,8},{8,12},{12,16},{16,20},{20,24},{24,28},{28,32},{32,36}... | collective-permute-start | bytes 393224 | tf_op jit(solution)/shard_map/ppermute | solution.py:448
  90.6 4.7 %collective-permute-start.11 = (bf16[128,512]{1,0:T(8,128)(2,1)S(1)}, bf16[128,512]{1,0:T(8,128)(2,1)S(1)}, u32[]{:S(2)}, u32[]{:S(2)}) collective-permute-start(bf16[128,512]{1,0:T(8,128)(2,1)S(1)} %get-tuple-element.66), channel_id=1, source_target_pairs={{0,252},{4,0},{8,4},{12,8},{16,12},{20,16},{24,20},{28,24},{32,28}... | collective-permute-start | bytes 393224 | tf_op jit(solution)/shard_map/ppermute | solution.py:448
  95.2 14.7 %collective-permute-done.10.from_before = bf16[128,512]{1,0:T(8,128)(2,1)S(1)} collective-permute-done((bf16[128,512]{1,0:T(8,128)(2,1)S(1)}, bf16[128,512]{1,0:T(8,128)(2,1)S(1)}, u32[]{:S(2)}, u32[]{:S(2)}) %collective-permute-start.10) | collective-permute-done | bytes 131104 | tf_op jit(solution)/shard_map/ppermute | solution.py:448
  110.0 0.0 collective-permute-done.11.from_after
  110.0 0.0 copy-done
  110.0 4.4 %place.1 = bf16[3,1024,128]{2,1,0:T(8,128)(2,1)} custom-call(s32[4]{0:T(128)S(1)} %copy-done.4, s32[3,1024]{1,0:T(4,128)S(1)} %copy-done.2, s32[1]{0:T(128)} %get-tuple-element.53.before, bf16[3,1024,512]{2,1,0:T(8,128)(2,1)S(1)} %copy-done, bf16[2,128,1024]{2,1,0:T(8,128)(2,1)S(1)} %get-tuple-element.64.branch, ...), custom_call_target="tpu_custom_call" | custom-call | flops 10000000000 | bytes 1000 | tf_op jit(solution)/shard_map/place/pallas_call | solution.py:586
  114.4 0.0 all-to-all-done.1.received
  114.4 1.1 finish.1
  (14 shorter events, 0.0 us)
Async XLA Ops:
  5.1 39.8 %collective-permute-start = (bf16[2,256,512]{2,1,0:T(8,128)(2,1)}, bf16[2,256,512]{2,1,0:T(8,128)(2,1)S(1)}, u32[]{:S(2)}, u32[]{:S(2)}) collective-permute-start(bf16[2,256,512]{2,1,0:T(8,128)(2,1)} %get-tuple-element.38), channel_id=1, source_target_pairs={{0,252},{4,0},{8,4},{12,8},{16,12},{20,16},{24,20},{28,24},{32,28}... | collective-permute-start | bytes 1572872 | tf_op jit(solution)/shard_map/ppermute | solution.py:448
  14.0 30.9 %collective-permute-start.1 = (bf16[2,272,512]{2,1,0:T(8,128)(2,1)}, bf16[2,272,512]{2,1,0:T(8,128)(2,1)S(1)}, u32[]{:S(2)}, u32[]{:S(2)}) collective-permute-start(bf16[2,272,512]{2,1,0:T(8,128)(2,1)} %get-tuple-element.39), channel_id=1, source_target_pairs={{0,4},{4,8},{8,12},{12,16},{16,20},{20,24},{24,28},{28,32},{32,36}... | collective-permute-start | bytes 1671176 | tf_op jit(solution)/shard_map/ppermute | solution.py:448
  44.9 2.8 %copy-start.10 = (bf16[2,256,512]{2,1,0:T(8,128)(2,1)}, bf16[2,256,512]{2,1,0:T(8,128)(2,1)S(1)}, u32[]{:S(2)}) copy-start(bf16[2,256,512]{2,1,0:T(8,128)(2,1)S(1)} %collective-permute-done.pull) | copy-start | bytes 1572868
  44.9 2.8 %copy-start.8 = (bf16[2,272,512]{2,1,0:T(8,128)(2,1)}, bf16[2,272,512]{2,1,0:T(8,128)(2,1)S(1)}, u32[]{:S(2)}) copy-start(bf16[2,272,512]{2,1,0:T(8,128)(2,1)S(1)} %collective-permute-done.1.push) | copy-start | bytes 1671172
  45.0 2.8 %collective-permute-start.3 = (bf16[2,272,512]{2,1,0:T(8,128)(2,1)S(1)}, bf16[2,272,512]{2,1,0:T(8,128)(2,1)S(1)}, u32[]{:S(2)}, u32[]{:S(2)}) collective-permute-start(bf16[2,272,512]{2,1,0:T(8,128)(2,1)S(1)} %collective-permute-done.1.push), channel_id=1, source_target_pairs={{0,1},{1,0},{2,3},{3,2},{4,5},{5,4},{6,7},{7,6},{8,9},{9,8},{10,11... | collective-permute-start | bytes 1671176 | tf_op jit(solution)/shard_map/ppermute | solution.py:451
  45.1 2.7 %collective-permute-start.2 = (bf16[2,256,512]{2,1,0:T(8,128)(2,1)S(1)}, bf16[2,256,512]{2,1,0:T(8,128)(2,1)S(1)}, u32[]{:S(2)}, u32[]{:S(2)}) collective-permute-start(bf16[2,256,512]{2,1,0:T(8,128)(2,1)S(1)} %collective-permute-done.pull), channel_id=1, source_target_pairs={{0,1},{1,0},{2,3},{3,2},{4,5},{5,4},{6,7},{7,6},{8,9},{9,8},{10,11... | collective-permute-start | bytes 1572872 | tf_op jit(solution)/shard_map/ppermute | solution.py:451
  47.7 0.8 copy-start.11
  47.8 1.0 copy-start.9
  48.7 16.0 %copy-start.4 = (s32[4]{0:T(128)S(1)}, s32[4]{0:T(128)}, u32[]{:S(2)}) copy-start(s32[4]{0:T(128)} %pad_add_fusion.scal) | copy-start | bytes 52
  54.1 33.6 %copy-start.5 = (f32[512]{0:T(512)S(1)}, f32[512]{0:T(512)}, u32[]{:S(2)}) copy-start(f32[512]{0:T(512)} %param.11) | copy-start | bytes 6148
  54.1 33.6 %copy-start.6 = (bf16[2,128,1024]{2,1,0:T(8,128)(2,1)S(1)}, bf16[2,128,1024]{2,1,0:T(8,128)(2,1)}, u32[]{:S(2)}) copy-start(bf16[2,128,1024]{2,1,0:T(8,128)(2,1)} %get-tuple-element.62.unit) | copy-start | bytes 1572868
  54.1 33.6 %copy-start.7 = (f32[2,8,1024]{2,1,0:T(8,128)S(1)}, f32[2,8,1024]{2,1,0:T(8,128)}, u32[]{:S(2)}) copy-start(f32[2,8,1024]{2,1,0:T(8,128)} %get-tuple-element.63.stat) | copy-start | bytes 196612
  54.1 10.6 %collective-permute-start.4 = (bf16[2,128,2048]{2,1,0:T(8,128)(2,1)}, bf16[2,128,2048]{2,1,0:T(8,128)(2,1)S(1)}, u32[]{:S(2)}, u32[]{:S(2)}) collective-permute-start(bf16[2,128,2048]{2,1,0:T(8,128)(2,1)} %get-tuple-element.55), channel_id=1, source_target_pairs={{0,1},{1,0},{2,3},{3,2},{4,5},{5,4},{6,7},{7,6},{8,9},{9,8},{10,11... | collective-permute-start | bytes 3145736 | tf_op jit(solution)/shard_map/ppermute | solution.py:451
  54.4 26.3 %all-to-all-start = ((bf16[64,32,128]{2,1,0:T(8,128)(2,1)}), bf16[64,32,128]{2,1,0:T(8,128)(2,1)S(1)}, u32[]{:S(2)}, u32[]{:S(2)}) async-start(bf16[64,32,128]{2,1,0:T(8,128)(2,1)} %get-tuple-element.67), calls=%async_computation | async-start | bytes 1048576 | tf_op jit(solution)/shard_map/all_to_all | solution.py:537
  62.1 2.6 %collective-permute-start.5 = (f32[2,2048]{1,0:T(2,128)}, f32[2,2048]{1,0:T(2,128)S(1)}, u32[]{:S(2)}, u32[]{:S(2)}) collective-permute-start(f32[2,2048]{1,0:T(2,128)} %get-tuple-element.56.stats), channel_id=1, source_target_pairs={{0,1},{1,0},{2,3},{3,2},{4,5},{5,4},{6,7},{7,6},{8,9},{9,8},{10,11... | collective-permute-start | bytes 49160 | tf_op jit(solution)/shard_map/ppermute | solution.py:451
  62.3 1.5 %collective-permute-start.6 = (f32[1,512]{1,0:T(1,128)}, f32[1,512]{1,0:T(1,128)S(1)}, u32[]{:S(2)}, u32[]{:S(2)}) collective-permute-start(f32[1,512]{1,0:T(1,128)} %get-tuple-element.59), channel_id=1, source_target_pairs={{0,1},{1,0},{2,3},{3,2},{4,5},{5,4},{6,7},{7,6},{8,9},{9,8},{10,11... | collective-permute-start | bytes 6152 | tf_op jit(solution)/shard_map/ppermute | solution.py:451
  64.3 5.1 %collective-permute-start.7 = (f32[1,512]{1,0:T(1,128)S(1)}, f32[1,512]{1,0:T(1,128)S(1)}, u32[]{:S(2)}, u32[]{:S(2)}) collective-permute-start(f32[1,512]{1,0:T(1,128)S(1)} %add.9.gain), channel_id=1, source_target_pairs={{0,2},{1,3},{2,0},{3,1},{4,6},{5,7},{6,4},{7,5},{8,10},{9,11},{10,... | collective-permute-start | bytes 6152 | tf_op jit(solution)/shard_map/ppermute | solution.py:451
  64.7 1.2 %copy-start.1 = (bf16[2,128,2048]{2,1,0:T(8,128)(2,1)S(1)}, bf16[2,128,2048]{2,1,0:T(8,128)(2,1)}, u32[]{:S(2)}) copy-start(bf16[2,128,2048]{2,1,0:T(8,128)(2,1)} %get-tuple-element.54.keep) | copy-start | bytes 3145732
  66.0 0.7 copy-start.3
  69.4 18.3 %collective-permute-start.8 = (bf16[128,2048]{1,0:T(8,128)(2,1)S(1)}, bf16[128,2048]{1,0:T(8,128)(2,1)S(1)}, u32[]{:S(2)}, u32[]{:S(2)}) collective-permute-start(bf16[128,2048]{1,0:T(8,128)(2,1)S(1)} %get-tuple-element.60), channel_id=1, source_target_pairs={{0,2},{1,3},{2,0},{3,1},{4,6},{5,7},{6,4},{7,5},{8,10},{9,11},{10,... | collective-permute-start | bytes 1572872 | tf_op jit(solution)/shard_map/ppermute | solution.py:451
  71.2 16.5 %collective-permute-start.9 = (f32[2,2048]{1,0:T(2,128)S(1)}, f32[2,2048]{1,0:T(2,128)S(1)}, u32[]{:S(2)}, u32[]{:S(2)}) collective-permute-start(f32[2,2048]{1,0:T(2,128)S(1)} %get-tuple-element.61.stats), channel_id=1, source_target_pairs={{0,2},{1,3},{2,0},{3,1},{4,6},{5,7},{6,4},{7,5},{8,10},{9,11},{10,... | collective-permute-start | bytes 49160 | tf_op jit(solution)/shard_map/ppermute | solution.py:451
  82.2 32.2 %all-to-all-start.1 = ((bf16[64,40,128]{2,1,0:T(8,128)(2,1)}), bf16[64,40,128]{2,1,0:T(8,128)(2,1)S(1)}, u32[]{:S(2)}, u32[]{:S(2)}) async-start(bf16[64,40,128]{2,1,0:T(8,128)(2,1)} %total.1), calls=%async_computation.1 | async-start | bytes 1310720 | tf_op jit(solution)/shard_map/all_to_all | solution.py:584
  87.7 22.2 %copy-start = (bf16[3,1024,512]{2,1,0:T(8,128)(2,1)S(1)}, bf16[3,1024,512]{2,1,0:T(8,128)(2,1)}, u32[]{:S(2)}) copy-start(bf16[3,1024,512]{2,1,0:T(8,128)(2,1)} %cotangent.5) | copy-start | bytes 9437188
  87.8 22.2 %copy-start.2 = (s32[3,1024]{1,0:T(4,128)S(1)}, s32[3,1024]{1,0:T(4,128)}, u32[]{:S(2)}) copy-start(s32[3,1024]{1,0:T(4,128)} %order.3) | copy-start | bytes 36868
  88.9 21.0 %collective-permute-start.10 = (bf16[128,512]{1,0:T(8,128)(2,1)S(1)}, bf16[128,512]{1,0:T(8,128)(2,1)S(1)}, u32[]{:S(2)}, u32[]{:S(2)}) collective-permute-start(bf16[128,512]{1,0:T(8,128)(2,1)S(1)} %get-tuple-element.65), channel_id=1, source_target_pairs={{0,4},{4,8},{8,12},{12,16},{16,20},{20,24},{24,28},{28,32},{32,36}... | collective-permute-start | bytes 393224 | tf_op jit(solution)/shard_map/ppermute | solution.py:448
  90.6 19.4 %collective-permute-start.11 = (bf16[128,512]{1,0:T(8,128)(2,1)S(1)}, bf16[128,512]{1,0:T(8,128)(2,1)S(1)}, u32[]{:S(2)}, u32[]{:S(2)}) collective-permute-start(bf16[128,512]{1,0:T(8,128)(2,1)S(1)} %get-tuple-element.66), channel_id=1, source_target_pairs={{0,252},{4,0},{8,4},{12,8},{16,12},{20,16},{24,20},{28,24},{32,28}... | collective-permute-start | bytes 393224 | tf_op jit(solution)/shard_map/ppermute | solution.py:448

commit v5 on v4

--- a/solution.py
+++ b/solution.py
@@ -170,27 +170,32 @@
     weights[D:D + 16, :] = split3(sums)
 
 
+def block_copies(core, p, send, keep, grads, done):
+    patch = grads.shape[2]
+    cols = pl.ds(pl.multiple_of(p * patch, patch), patch)
+    copies = []
+    for j in range(2):
+        for k, (block, into) in enumerate(((2 * j + 1 - core, send), (2 * j + core, keep))):
+            rows = pl.ds(pl.multiple_of(block * 128, 128), 128)
+            copies.append(pltpu.make_async_copy(
+                grads.at[p, rows], into.at[j, :, cols], done.at[p, 2 * j + k]
+            ))
+    return copies
+
+
 def patch_core(core, p, nrm, dy, weights, wt, wo, send, keep, stats, wacc,
                prj, kr, vr, dat, att, gp, grads, scores, lows, done):
     project(nrm, dy, weights, wt, wo, prj, kr, vr, dat)
     attend(prj, kr, vr, dat, gp, att, scores, lows)
     patch = gp.shape[1]
     cols = pl.ds(pl.multiple_of(p * patch, patch), patch)
-    grads[...] = mm(weights[0:D, :], gp[...]).astype(BF16)
-    copies = []
-    for j in range(2):
-        for k, (block, into) in enumerate(((2 * j + 1 - core, send), (2 * j + core, keep))):
-            rows = pl.ds(pl.multiple_of(block * 128, 128), 128)
-            copies.append(
-                pltpu.make_async_copy(grads.at[rows], into.at[j, :, cols], done.at[2 * j + k])
-            )
-            copies[-1].start()
+    grads[p] = mm(weights[0:D, :], gp[...]).astype(BF16)
+    for copy in block_copies(core, p, send, keep, grads, done):
+        copy.start()
     wacc[0:384] += mm(gp[...], nrm[...])
     wacc[384:512] += mm(att[...], dy[...])
     stats[0:1, cols] = jnp.sum(mm(weights[D:D + 16, :], gp[...]), axis=0, keepdims=True)
     stats[1:2, cols] = second_stat(gp, prj)
-    for copy in copies:
-        copy.wait()
 
 
 def second_stat(gp, prj):
@@ -248,6 +253,12 @@
         return carry
 
     lax.fori_loop(0, 2, step, 0)
+
+    @pl.when(whole)
+    def _():
+        for p in range(2):
+            for copy in block_copies(scal[0], p, send, keep, work[-4], work[-1]):
+                copy.wait()
 
 
 def cross_kernel(factor, scal, pull, pull_other, push, push_other, send_i, keep_i, wacc_i, nrm_i,
@@ -288,7 +299,7 @@
 
     @pl.when(jnp.logical_not(light))
     def _():
-        copy = pltpu.make_async_copy(wacc_i, wacc, work[-1].at[0])
+        copy = pltpu.make_async_copy(wacc_i, wacc, arrived.at[3, 0])
         copy.start()
         copy.wait()
 
@@ -327,6 +338,11 @@
         for c in range(4):
             block = wacc[32 * r:32 * r + 32, 128 * c:128 * c + 128]
             pieces[4 * r + c] = (block * factor).astype(BF16)
+    for p in range(2):
+        @pl.when(p < patches)
+        def _():
+            for copy in block_copies(scal[0], p, send, keep, work[-4], work[-1]):
+                copy.wait()
 
 
 def pair_kernel(scal, keep, received, stats, stats_received, send, kept, stats_o):
@@ -478,7 +494,7 @@
         pltpu.VMEM((width + 16, 384), BF16),
         pltpu.VMEM((384, width), BF16),
         pltpu.VMEM((128, width), BF16),
-        pltpu.SemaphoreType.DMA((3, 7)),
+        pltpu.SemaphoreType.DMA((4, 7)),
     ]
     work = [
         pltpu.VMEM((384, patch), BF16),
@@ -487,10 +503,10 @@
         pltpu.VMEM((128, patch), BF16),
         pltpu.VMEM((128, patch), BF16),
         pltpu.VMEM((384, patch), BF16),
-        pltpu.VMEM((width, patch), BF16),
+        pltpu.VMEM((2, width, patch), BF16),
         pltpu.VMEM((2, patch, patch), F32),
         pltpu.VMEM((2, patch, patch), BF16),
-        pltpu.SemaphoreType.DMA((4,)),
+        pltpu.SemaphoreType.DMA((2, 4)),
     ]
     lanes = 2 * patch
     shared = [
@@ -521,7 +537,7 @@
     factor = 1.0 / math.sqrt(curve * slots * patch)
     send, keep, stats, unit, inverse, pieces, gain_part, before = pl.pallas_call(
         functools.partial(cross_kernel, factor),
-        in_specs=[SMEM] + [ANY] * 4 + [HBM] * 11 + [VMEM],
+        in_specs=[SMEM] + [HBM] * 15 + [VMEM],
         out_specs=[ANY] * 2 + [VMEM] * 5 + [SMEM],
         out_shape=shared + [
             sds((64, 32, 128), BF16), sds((1, width), F32), sds((1,), jnp.int32)

time: 117 us -> 116 us (level)
  no operation moved by 1% of the time
where the time goes in v5:
time: 116 us; the launch traced here: 115 us
  Pallas kernels  48.6 us (42%)
  starting transfers between devices  34 us (29%)
  waiting for transfers between devices  27.2 us (23%)
  local copies, waits for them, and re-layouts  2.93 us (3%)
  between operations  1.5 us (1%)
  other arithmetic  1.22 us (1%)
    pallas_call x1, Pallas kernels, shards(): pl.pallas_call(local_kernel, in_specs=[SMEM] + [VMEM] * 6, out_specs=[ANY...  30 us
    ppermute x4, starting transfers between devices, passed(): lax.ppermute(x, 'curve', [(i, (i + by) % curve) for i in range(curve)])  15.2 us
    ppermute x4, waiting for transfers between devices, passed(): lax.ppermute(x, 'curve', [(i, (i + by) % curve) for i in range(curve)])  14.7 us
    all_to_all x1, starting transfers between devices, shards(): received = lax.all_to_all(pieces, 'curve', 0, 0)  7.74 us
    all_to_all x1, waiting for transfers between devices, shards(): received = lax.all_to_all(pieces, 'curve', 0, 0)  7.69 us
    pallas_call x1, Pallas kernels, shards(): pl.pallas_call(functools.partial(cross_kernel, factor), in_specs=[SMEM] +...  5.63 us
    ppermute x8, starting transfers between devices, swapped(): return lax.ppermute(x, 'mp', [(i, i ^ bit) for i in range(4)])  5.57 us
    all_to_all x1, starting transfers between devices, shards(): gathered = lax.all_to_all(totals, 'curve', 0, 0)  5.48 us
  transfers between devices with their start and end apart: 14, of which 5 were waited for; matrix products, arithmetic and copies ran while one was open for 1% of the time, Pallas kernels for 33%

profile of v5, /device:TPU:16, one launch (start us, length us, event | category | flops | bytes accessed | tf_op | source)
XLA Modules:
  0.0 115.4 jit_solution(14527458191529675912)
XLA Ops:
  1.3 3.9 %halo.1 = (bf16[2,256,512]{2,1,0:T(8,128)(2,1)}, bf16[2,272,512]{2,1,0:T(8,128)(2,1)}) custom-call(s32[1]{0:T(128)S(6)} %copy.15.counts, s32[3,1024]{1,0:T(4,128)} %order.3, bf16[3,1024,512]{2,1,0:T(8,128)(2,1)} %points.3, bf16[3,1024,512]{2,1,0:T(8,128)(2,1)} %cotangent.5), custom_call_target="tpu_custom_call" | custom-call | tf_op jit(solution)/shard_map/halo/pallas_call | solution.py:469
  5.1 8.8 %collective-permute-start = (bf16[2,256,512]{2,1,0:T(8,128)(2,1)}, bf16[2,256,512]{2,1,0:T(8,128)(2,1)S(1)}, u32[]{:S(2)}, u32[]{:S(2)}) collective-permute-start(bf16[2,256,512]{2,1,0:T(8,128)(2,1)} %get-tuple-element.38), channel_id=1, source_target_pairs={{0,252},{4,0},{8,4},{12,8},{16,12},{20,16},{24,20},{28,24},{32,28}... | collective-permute-start | bytes 1572872 | tf_op jit(solution)/shard_map/ppermute | solution.py:464
  14.0 0.0 collective-permute-start.1
  14.0 0.6 pad_add_fusion.scal
  14.6 30.0 %local.1 = (bf16[2,128,2048]{2,1,0:T(8,128)(2,1)}, bf16[2,128,2048]{2,1,0:T(8,128)(2,1)}, f32[2,2048]{1,0:T(2,128)}, bf16[2,128,1024]{2,1,0:T(8,128)(2,1)}, f32[...) custom-call(s32[4]{0:T(128)} %pad_add_fusion.scal, ...), custom_call_target="tpu_custom_call" | custom-call | flops 16000000000 | bytes 16000000 | tf_op jit(solution)/shard_map/local/pallas_call | solution.py:519
  44.6 0.0 collective-permute-done.pull
  44.6 0.0 copy-start.10
  44.6 0.0 collective-permute-done.1.push
  44.6 0.0 copy-start.8
  44.6 0.1 collective-permute-start.3
  44.7 0.5 collective-permute-start.2
  45.2 2.2 %collective-permute-done.2.pull_other = bf16[2,256,512]{2,1,0:T(8,128)(2,1)S(1)} collective-permute-done((bf16[2,256,512]{2,1,0:T(8,128)(2,1)S(1)}, bf16[2,256,512]{2,1,0:T(8,128)(2,1)S(1)}, u32[]{:S(2)}, u32[]{:S(2)}) %collective-permute-start.2) | collective-permute-done | bytes 524320 | tf_op jit(solution)/shard_map/ppermute | solution.py:467
  47.4 0.0 collective-permute-done.3.push_other
  47.5 0.0 copy-done.10
  47.5 0.8 copy-done.11
  48.2 0.2 copy-done.9
  48.4 5.6 %cross.1 = (bf16[2,128,2048]{2,1,0:T(8,128)(2,1)}, bf16[2,128,2048]{2,1,0:T(8,128)(2,1)}, f32[2,2048]{1,0:T(2,128)}, bf16[2,128,1024]{2,1,0:T(8,128)(2,1)}, f32[...) custom-call(s32[4]{0:T(128)} %pad_add_fusion.scal, ...), custom_call_target="tpu_custom_call", output_to_operand_aliasing={{0}: (5, {}), {1}: (6, {})} | custom-call | flops 4000000000 | bytes 8000000 | tf_op jit(solution)/shard_map/cross/pallas_call | solution.py:538
  54.1 0.0 copy-start.5
  54.1 0.2 collective-permute-start.4
  54.3 7.7 %all-to-all-start = ((bf16[64,32,128]{2,1,0:T(8,128)(2,1)}), bf16[64,32,128]{2,1,0:T(8,128)(2,1)S(1)}, u32[]{:S(2)}, u32[]{:S(2)}) async-start(bf16[64,32,128]{2,1,0:T(8,128)(2,1)} %get-tuple-element.67), calls=%async_computation | async-start | bytes 1048576 | tf_op jit(solution)/shard_map/all_to_all | solution.py:553
  62.1 0.2 collective-permute-start.5
  62.2 0.4 collective-permute-start.6
  62.7 1.0 collective-permute-done.6
  63.7 0.6 add.9.gain
  64.3 0.6 collective-permute-start.7
  64.9 0.0 collective-permute-done.5.stats_received
  64.9 0.0 collective-permute-done.4.received
  65.0 1.2 %copy-done.1 = bf16[2,128,2048]{2,1,0:T(8,128)(2,1)S(1)} copy-done((bf16[2,128,2048]{2,1,0:T(8,128)(2,1)S(1)}, bf16[2,128,2048]{2,1,0:T(8,128)(2,1)}, u32[]{:S(2)}) %copy-start.1) | copy-done | bytes 1048600
  66.2 0.7 copy-done.3
  66.9 1.0 pair.1
  67.9 1.5 %collective-permute-done.7.gain_received = f32[1,512]{1,0:T(1,128)S(1)} collective-permute-done((f32[1,512]{1,0:T(1,128)S(1)}, f32[1,512]{1,0:T(1,128)S(1)}, u32[]{:S(2)}, u32[]{:S(2)}) %collective-permute-start.7) | collective-permute-done | bytes 2080 | tf_op jit(solution)/shard_map/ppermute | solution.py:467
  69.4 1.7 %collective-permute-start.8 = (bf16[128,2048]{1,0:T(8,128)(2,1)S(1)}, bf16[128,2048]{1,0:T(8,128)(2,1)S(1)}, u32[]{:S(2)}, u32[]{:S(2)}) collective-permute-start(bf16[128,2048]{1,0:T(8,128)(2,1)S(1)} %get-tuple-element.60), channel_id=1, source_target_pairs={{0,2},{1,3},{2,0},{3,1},{4,6},{5,7},{6,4},{7,5},{8,10},{9,11},{10,... | collective-permute-start | bytes 1572872 | tf_op jit(solution)/shard_map/ppermute | solution.py:467
  71.1 1.8 %collective-permute-start.9 = (f32[2,2048]{1,0:T(2,128)S(1)}, f32[2,2048]{1,0:T(2,128)S(1)}, u32[]{:S(2)}, u32[]{:S(2)}) collective-permute-start(f32[2,2048]{1,0:T(2,128)S(1)} %get-tuple-element.61.stats), channel_id=1, source_target_pairs={{0,2},{1,3},{2,0},{3,1},{4,6},{5,7},{6,4},{7,5},{8,10},{9,11},{10,... | collective-permute-start | bytes 49160 | tf_op jit(solution)/shard_map/ppermute | solution.py:467
  72.9 7.7 %all-to-all-done.received = bf16[64,32,128]{2,1,0:T(8,128)(2,1)S(1)} async-done(((bf16[64,32,128]{2,1,0:T(8,128)(2,1)}), bf16[64,32,128]{2,1,0:T(8,128)(2,1)S(1)}, u32[]{:S(2)}, u32[]{:S(2)}) %all-to-all-start) | async-done | bytes 524320 | tf_op jit(solution)/shard_map/all_to_all | solution.py:553
  80.6 1.5 %total.1 = bf16[64,40,128]{2,1,0:T(8,128)(2,1)} custom-call(s32[4]{0:T(128)S(1)} %copy-done.4, bf16[64,32,128]{2,1,0:T(8,128)(2,1)S(1)} %all-to-all-done.received, f32[1,512]{1,0:T(1,128)S(1)} %add.9.gain, f32[1,512]{1,0:T(1,128)S(1)} %collective-permute-done.7.gain_received), custom_call_target="tpu_custom_call" | custom-call | tf_op jit(solution)/shard_map/total/pallas_call | solution.py:592
  82.2 5.5 %all-to-all-start.1 = ((bf16[64,40,128]{2,1,0:T(8,128)(2,1)}), bf16[64,40,128]{2,1,0:T(8,128)(2,1)S(1)}, u32[]{:S(2)}, u32[]{:S(2)}) async-start(bf16[64,40,128]{2,1,0:T(8,128)(2,1)} %total.1), calls=%async_computation.1 | async-start | bytes 1310720 | tf_op jit(solution)/shard_map/all_to_all | solution.py:600
  87.7 0.0 collective-permute-done.9.stats_received
  87.7 0.0 collective-permute-done.8.received
  87.7 0.0 copy-start
  87.7 0.0 copy-start.2
  87.7 1.2 branch.1
  88.9 1.6 %collective-permute-start.10 = (bf16[128,512]{1,0:T(8,128)(2,1)S(1)}, bf16[128,512]{1,0:T(8,128)(2,1)S(1)}, u32[]{:S(2)}, u32[]{:S(2)}) collective-permute-start(bf16[128,512]{1,0:T(8,128)(2,1)S(1)} %get-tuple-element.65), channel_id=1, source_target_pairs={{0,4},{4,8},{8,12},{12,16},{16,20},{20,24},{24,28},{28,32},{32,36}... | collective-permute-start | bytes 393224 | tf_op jit(solution)/shard_map/ppermute | solution.py:464
  90.5 4.7 %collective-permute-start.11 = (bf16[128,512]{1,0:T(8,128)(2,1)S(1)}, bf16[128,512]{1,0:T(8,128)(2,1)S(1)}, u32[]{:S(2)}, u32[]{:S(2)}) collective-permute-start(bf16[128,512]{1,0:T(8,128)(2,1)S(1)} %get-tuple-element.66), channel_id=1, source_target_pairs={{0,252},{4,0},{8,4},{12,8},{16,12},{20,16},{24,20},{28,24},{32,28}... | collective-permute-start | bytes 393224 | tf_op jit(solution)/shard_map/ppermute | solution.py:464
  95.2 14.7 %collective-permute-done.10.from_before = bf16[128,512]{1,0:T(8,128)(2,1)S(1)} collective-permute-done((bf16[128,512]{1,0:T(8,128)(2,1)S(1)}, bf16[128,512]{1,0:T(8,128)(2,1)S(1)}, u32[]{:S(2)}, u32[]{:S(2)}) %collective-permute-start.10) | collective-permute-done | bytes 131104 | tf_op jit(solution)/shard_map/ppermute | solution.py:464
  109.9 0.0 collective-permute-done.11.from_after
  110.0 4.4 %place.1 = bf16[3,1024,128]{2,1,0:T(8,128)(2,1)} custom-call(s32[4]{0:T(128)S(1)} %copy-done.4, s32[3,1024]{1,0:T(4,128)S(1)} %copy-done.2, s32[1]{0:T(128)} %get-tuple-element.53.before, bf16[3,1024,512]{2,1,0:T(8,128)(2,1)S(1)} %copy-done, bf16[2,128,1024]{2,1,0:T(8,128)(2,1)S(1)} %get-tuple-element.64.branch, ...), custom_call_target="tpu_custom_call" | custom-call | flops 10000000000 | bytes 1000 | tf_op jit(solution)/shard_map/place/pallas_call | solution.py:602
  114.3 0.0 all-to-all-done.1.received
  114.3 1.1 finish.1
  (14 shorter events, 0.0 us)
Async XLA Ops:
  5.1 39.5 %collective-permute-start = (bf16[2,256,512]{2,1,0:T(8,128)(2,1)}, bf16[2,256,512]{2,1,0:T(8,128)(2,1)S(1)}, u32[]{:S(2)}, u32[]{:S(2)}) collective-permute-start(bf16[2,256,512]{2,1,0:T(8,128)(2,1)} %get-tuple-element.38), channel_id=1, source_target_pairs={{0,252},{4,0},{8,4},{12,8},{16,12},{20,16},{24,20},{28,24},{32,28}... | collective-permute-start | bytes 1572872 | tf_op jit(solution)/shard_map/ppermute | solution.py:464
  14.0 30.6 %collective-permute-start.1 = (bf16[2,272,512]{2,1,0:T(8,128)(2,1)}, bf16[2,272,512]{2,1,0:T(8,128)(2,1)S(1)}, u32[]{:S(2)}, u32[]{:S(2)}) collective-permute-start(bf16[2,272,512]{2,1,0:T(8,128)(2,1)} %get-tuple-element.39), channel_id=1, source_target_pairs={{0,4},{4,8},{8,12},{12,16},{16,20},{20,24},{24,28},{28,32},{32,36}... | collective-permute-start | bytes 1671176 | tf_op jit(solution)/shard_map/ppermute | solution.py:464
  44.6 2.8 %copy-start.10 = (bf16[2,256,512]{2,1,0:T(8,128)(2,1)}, bf16[2,256,512]{2,1,0:T(8,128)(2,1)S(1)}, u32[]{:S(2)}) copy-start(bf16[2,256,512]{2,1,0:T(8,128)(2,1)S(1)} %collective-permute-done.pull) | copy-start | bytes 1572868
  44.6 2.8 %copy-start.8 = (bf16[2,272,512]{2,1,0:T(8,128)(2,1)}, bf16[2,272,512]{2,1,0:T(8,128)(2,1)S(1)}, u32[]{:S(2)}) copy-start(bf16[2,272,512]{2,1,0:T(8,128)(2,1)S(1)} %collective-permute-done.1.push) | copy-start | bytes 1671172
  44.6 2.8 %collective-permute-start.3 = (bf16[2,272,512]{2,1,0:T(8,128)(2,1)S(1)}, bf16[2,272,512]{2,1,0:T(8,128)(2,1)S(1)}, u32[]{:S(2)}, u32[]{:S(2)}) collective-permute-start(bf16[2,272,512]{2,1,0:T(8,128)(2,1)S(1)} %collective-permute-done.1.push), channel_id=1, source_target_pairs={{0,1},{1,0},{2,3},{3,2},{4,5},{5,4},{6,7},{7,6},{8,9},{9,8},{10,11... | collective-permute-start | bytes 1671176 | tf_op jit(solution)/shard_map/ppermute | solution.py:467
  44.7 2.7 %collective-permute-start.2 = (bf16[2,256,512]{2,1,0:T(8,128)(2,1)S(1)}, bf16[2,256,512]{2,1,0:T(8,128)(2,1)S(1)}, u32[]{:S(2)}, u32[]{:S(2)}) collective-permute-start(bf16[2,256,512]{2,1,0:T(8,128)(2,1)S(1)} %collective-permute-done.pull), channel_id=1, source_target_pairs={{0,1},{1,0},{2,3},{3,2},{4,5},{5,4},{6,7},{7,6},{8,9},{9,8},{10,11... | collective-permute-start | bytes 1572872 | tf_op jit(solution)/shard_map/ppermute | solution.py:467
  47.4 0.8 copy-start.11
  47.4 1.0 copy-start.9
  48.4 16.5 %copy-start.4 = (s32[4]{0:T(128)S(1)}, s32[4]{0:T(128)}, u32[]{:S(2)}) copy-start(s32[4]{0:T(128)} %pad_add_fusion.scal) | copy-start | bytes 52
  54.1 33.6 %copy-start.5 = (f32[512]{0:T(512)S(1)}, f32[512]{0:T(512)}, u32[]{:S(2)}) copy-start(f32[512]{0:T(512)} %param.11) | copy-start | bytes 6148
  54.1 33.6 %copy-start.6 = (bf16[2,128,1024]{2,1,0:T(8,128)(2,1)S(1)}, bf16[2,128,1024]{2,1,0:T(8,128)(2,1)}, u32[]{:S(2)}) copy-start(bf16[2,128,1024]{2,1,0:T(8,128)(2,1)} %get-tuple-element.62.unit) | copy-start | bytes 1572868
  54.1 33.6 %copy-start.7 = (f32[2,8,1024]{2,1,0:T(8,128)S(1)}, f32[2,8,1024]{2,1,0:T(8,128)}, u32[]{:S(2)}) copy-start(f32[2,8,1024]{2,1,0:T(8,128)} %get-tuple-element.63.stat) | copy-start | bytes 196612
  54.1 10.9 %collective-permute-start.4 = (bf16[2,128,2048]{2,1,0:T(8,128)(2,1)}, bf16[2,128,2048]{2,1,0:T(8,128)(2,1)S(1)}, u32[]{:S(2)}, u32[]{:S(2)}) collective-permute-start(bf16[2,128,2048]{2,1,0:T(8,128)(2,1)} %get-tuple-element.55), channel_id=1, source_target_pairs={{0,1},{1,0},{2,3},{3,2},{4,5},{5,4},{6,7},{7,6},{8,9},{9,8},{10,11... | collective-permute-start | bytes 3145736 | tf_op jit(solution)/shard_map/ppermute | solution.py:467
  54.3 26.3 %all-to-all-start = ((bf16[64,32,128]{2,1,0:T(8,128)(2,1)}), bf16[64,32,128]{2,1,0:T(8,128)(2,1)S(1)}, u32[]{:S(2)}, u32[]{:S(2)}) async-start(bf16[64,32,128]{2,1,0:T(8,128)(2,1)} %get-tuple-element.67), calls=%async_computation | async-start | bytes 1048576 | tf_op jit(solution)/shard_map/all_to_all | solution.py:553
  62.1 2.9 %collective-permute-start.5 = (f32[2,2048]{1,0:T(2,128)}, f32[2,2048]{1,0:T(2,128)S(1)}, u32[]{:S(2)}, u32[]{:S(2)}) collective-permute-start(f32[2,2048]{1,0:T(2,128)} %get-tuple-element.56.stats), channel_id=1, source_target_pairs={{0,1},{1,0},{2,3},{3,2},{4,5},{5,4},{6,7},{7,6},{8,9},{9,8},{10,11... | collective-permute-start | bytes 49160 | tf_op jit(solution)/shard_map/ppermute | solution.py:467
  62.2 1.5 %collective-permute-start.6 = (f32[1,512]{1,0:T(1,128)}, f32[1,512]{1,0:T(1,128)S(1)}, u32[]{:S(2)}, u32[]{:S(2)}) collective-permute-start(f32[1,512]{1,0:T(1,128)} %get-tuple-element.59), channel_id=1, source_target_pairs={{0,1},{1,0},{2,3},{3,2},{4,5},{5,4},{6,7},{7,6},{8,9},{9,8},{10,11... | collective-permute-start | bytes 6152 | tf_op jit(solution)/shard_map/ppermute | solution.py:467
  64.3 5.1 %collective-permute-start.7 = (f32[1,512]{1,0:T(1,128)S(1)}, f32[1,512]{1,0:T(1,128)S(1)}, u32[]{:S(2)}, u32[]{:S(2)}) collective-permute-start(f32[1,512]{1,0:T(1,128)S(1)} %add.9.gain), channel_id=1, source_target_pairs={{0,2},{1,3},{2,0},{3,1},{4,6},{5,7},{6,4},{7,5},{8,10},{9,11},{10,... | collective-permute-start | bytes 6152 | tf_op jit(solution)/shard_map/ppermute | solution.py:467
  65.0 1.2 %copy-start.1 = (bf16[2,128,2048]{2,1,0:T(8,128)(2,1)S(1)}, bf16[2,128,2048]{2,1,0:T(8,128)(2,1)}, u32[]{:S(2)}) copy-start(bf16[2,128,2048]{2,1,0:T(8,128)(2,1)} %get-tuple-element.54.keep) | copy-start | bytes 3145732
  66.2 0.7 copy-start.3
  69.4 18.3 %collective-permute-start.8 = (bf16[128,2048]{1,0:T(8,128)(2,1)S(1)}, bf16[128,2048]{1,0:T(8,128)(2,1)S(1)}, u32[]{:S(2)}, u32[]{:S(2)}) collective-permute-start(bf16[128,2048]{1,0:T(8,128)(2,1)S(1)} %get-tuple-element.60), channel_id=1, source_target_pairs={{0,2},{1,3},{2,0},{3,1},{4,6},{5,7},{6,4},{7,5},{8,10},{9,11},{10,... | collective-permute-start | bytes 1572872 | tf_op jit(solution)/shard_map/ppermute | solution.py:467
  71.1 16.5 %collective-permute-start.9 = (f32[2,2048]{1,0:T(2,128)S(1)}, f32[2,2048]{1,0:T(2,128)S(1)}, u32[]{:S(2)}, u32[]{:S(2)}) collective-permute-start(f32[2,2048]{1,0:T(2,128)S(1)} %get-tuple-element.61.stats), channel_id=1, source_target_pairs={{0,2},{1,3},{2,0},{3,1},{4,6},{5,7},{6,4},{7,5},{8,10},{9,11},{10,... | collective-permute-start | bytes 49160 | tf_op jit(solution)/shard_map/ppermute | solution.py:467
  82.2 32.2 %all-to-all-start.1 = ((bf16[64,40,128]{2,1,0:T(8,128)(2,1)}), bf16[64,40,128]{2,1,0:T(8,128)(2,1)S(1)}, u32[]{:S(2)}, u32[]{:S(2)}) async-start(bf16[64,40,128]{2,1,0:T(8,128)(2,1)} %total.1), calls=%async_computation.1 | async-start | bytes 1310720 | tf_op jit(solution)/shard_map/all_to_all | solution.py:600
  87.7 22.2 %copy-start = (bf16[3,1024,512]{2,1,0:T(8,128)(2,1)S(1)}, bf16[3,1024,512]{2,1,0:T(8,128)(2,1)}, u32[]{:S(2)}) copy-start(bf16[3,1024,512]{2,1,0:T(8,128)(2,1)} %cotangent.5) | copy-start | bytes 9437188
  87.7 22.2 %copy-start.2 = (s32[3,1024]{1,0:T(4,128)S(1)}, s32[3,1024]{1,0:T(4,128)}, u32[]{:S(2)}) copy-start(s32[3,1024]{1,0:T(4,128)} %order.3) | copy-start | bytes 36868
  88.9 21.0 %collective-permute-start.10 = (bf16[128,512]{1,0:T(8,128)(2,1)S(1)}, bf16[128,512]{1,0:T(8,128)(2,1)S(1)}, u32[]{:S(2)}, u32[]{:S(2)}) collective-permute-start(bf16[128,512]{1,0:T(8,128)(2,1)S(1)} %get-tuple-element.65), channel_id=1, source_target_pairs={{0,4},{4,8},{8,12},{12,16},{16,20},{20,24},{24,28},{28,32},{32,36}... | collective-permute-start | bytes 393224 | tf_op jit(solution)/shard_map/ppermute | solution.py:464
  90.5 19.4 %collective-permute-start.11 = (bf16[128,512]{1,0:T(8,128)(2,1)S(1)}, bf16[128,512]{1,0:T(8,128)(2,1)S(1)}, u32[]{:S(2)}, u32[]{:S(2)}) collective-permute-start(bf16[128,512]{1,0:T(8,128)(2,1)S(1)} %get-tuple-element.66), channel_id=1, source_target_pairs={{0,252},{4,0},{8,4},{12,8},{16,12},{20,16},{24,20},{28,24},{32,28}... | collective-permute-start | bytes 393224 | tf_op jit(solution)/shard_map/ppermute | solution.py:464

commit v6 on v5

--- a/solution.py
+++ b/solution.py
@@ -532,7 +532,10 @@
         cost_estimate=cost(16 * 10**9, 16 * 10**6),
         name="local",
     )(scal, order, points, cotangent, gain_row, w3, w_out)
-    pull, push, wacc = lax.optimization_barrier((pull, push, wacc))
+    pull, wacc = lax.optimization_barrier((pull, wacc))
+    pull_other = swapped(pull, 1)
+    push, pull_other = lax.optimization_barrier((push, pull_other))
+    push_other = swapped(push, 1)
 
     factor = 1.0 / math.sqrt(curve * slots * patch)
     send, keep, stats, unit, inverse, pieces, gain_part, before = pl.pallas_call(
@@ -547,7 +550,7 @@
         compiler_params=params(60),
         cost_estimate=cost(4 * 10**9, 8 * 10**6),
         name="cross",
-    )(scal, pull, swapped(pull, 1), push, swapped(push, 1), send, keep, wacc, nrm, dy, stats, unit,
+    )(scal, pull, pull_other, push, push_other, send, keep, wacc, nrm, dy, stats, unit,
       inverse, weights, wt, w_out, gain_row)
 
     received = lax.all_to_all(pieces, "curve", 0, 0)

time: 116 us -> 117 us (level)
  Pallas kernels: 48.6 us -> 35.3 us
  waiting for transfers between devices: 27.2 us -> 36.3 us
  starting transfers between devices: 34 us -> 38.4 us
    pallas_call x1, Pallas kernels: 30 us -> 8.53 us  [shards(): pl.pallas_call(local_kernel, in_specs=[SMEM] + [VMEM] * 6, out_specs=[ANY...]
    ppermute x4, waiting for transfers between devices: 14.7 us -> 24.1 us  [passed(): lax.ppermute(x, 'curve', [(i, (i + by) % curve) for i in range(curve)])]
    pallas_call x1, Pallas kernels: 5.63 us -> 14.7 us  [shards(): pl.pallas_call(functools.partial(cross_kernel, factor), in_specs=[SMEM] +...]
    all_to_all x1, starting transfers between devices: 7.74 us -> 12.7 us  [shards(): received = lax.all_to_all(pieces, 'curve', 0, 0)]
  transfers between devices with their start and end apart: 14 -> 14, of which waited for: 5 -> 7; matrix products, arithmetic and copies ran while one was open for 1% -> 1% of each run, Pallas kernels for 33% -> 14%
where the time goes in v6:
time: 117 us; the launch traced here: 115 us
  starting transfers between devices  38.4 us (33%)
  waiting for transfers between devices  36.3 us (31%)
  Pallas kernels  35.3 us (30%)
  local copies, waits for them, and re-layouts  2.77 us (2%)
  between operations  1.46 us (1%)
  other arithmetic  1.22 us (1%)
    ppermute x4, waiting for transfers between devices, passed(): lax.ppermute(x, 'curve', [(i, (i + by) % curve) for i in range(curve)])  24.1 us
    ppermute x4, starting transfers between devices, passed(): lax.ppermute(x, 'curve', [(i, (i + by) % curve) for i in range(curve)])  15.2 us
    pallas_call x1, Pallas kernels, shards(): pl.pallas_call(functools.partial(cross_kernel, factor), in_specs=[SMEM] +...  14.7 us
    all_to_all x1, starting transfers between devices, shards(): received = lax.all_to_all(pieces, 'curve', 0, 0)  12.7 us
    pallas_call x1, Pallas kernels, shards(): pl.pallas_call(local_kernel, in_specs=[SMEM] + [VMEM] * 6, out_specs=[ANY...  8.53 us
    all_to_all x1, waiting for transfers between devices, shards(): received = lax.all_to_all(pieces, 'curve', 0, 0)  7.69 us
    all_to_all x1, starting transfers between devices, shards(): gathered = lax.all_to_all(totals, 'curve', 0, 0)  5.49 us
    ppermute x8, starting transfers between devices, swapped(): return lax.ppermute(x, 'mp', [(i, i ^ bit) for i in range(4)])  5.06 us
  transfers between devices with their start and end apart: 14, of which 7 were waited for; matrix products, arithmetic and copies ran while one was open for 1% of the time, Pallas kernels for 14%

profile of v6, /device:TPU:16, one launch (start us, length us, event | category | flops | bytes accessed | tf_op | source)
XLA Modules:
  0.0 115.5 jit_solution(11011746629604149767)
XLA Ops:
  1.3 3.9 %halo.1 = (bf16[2,256,512]{2,1,0:T(8,128)(2,1)}, bf16[2,272,512]{2,1,0:T(8,128)(2,1)}) custom-call(s32[1]{0:T(128)S(6)} %copy.15.counts, s32[3,1024]{1,0:T(4,128)} %order.3, bf16[3,1024,512]{2,1,0:T(8,128)(2,1)} %points.3, bf16[3,1024,512]{2,1,0:T(8,128)(2,1)} %cotangent.5), custom_call_target="tpu_custom_call" | custom-call | tf_op jit(solution)/shard_map/halo/pallas_call | solution.py:469
  5.1 8.8 %collective-permute-start = (bf16[2,256,512]{2,1,0:T(8,128)(2,1)}, bf16[2,256,512]{2,1,0:T(8,128)(2,1)S(1)}, u32[]{:S(2)}, u32[]{:S(2)}) collective-permute-start(bf16[2,256,512]{2,1,0:T(8,128)(2,1)} %get-tuple-element.39), channel_id=1, source_target_pairs={{0,252},{4,0},{8,4},{12,8},{16,12},{20,16},{24,20},{28,24},{32,28}... | collective-permute-start | bytes 1572872 | tf_op jit(solution)/shard_map/ppermute | solution.py:464
  14.0 0.0 collective-permute-start.1
  14.0 0.6 pad_add_fusion.scal
  14.6 8.5 %local.1 = (bf16[2,128,2048]{2,1,0:T(8,128)(2,1)}, bf16[2,128,2048]{2,1,0:T(8,128)(2,1)}, f32[2,2048]{1,0:T(2,128)}, bf16[2,128,1024]{2,1,0:T(8,128)(2,1)}, f32[...) custom-call(s32[4]{0:T(128)} %pad_add_fusion.scal, ...), custom_call_target="tpu_custom_call" | custom-call | flops 16000000000 | bytes 16000000 | tf_op jit(solution)/shard_map/local/pallas_call | solution.py:519
  23.1 2.4 %collective-permute-done.pull = bf16[2,256,512]{2,1,0:T(8,128)(2,1)S(1)} collective-permute-done((bf16[2,256,512]{2,1,0:T(8,128)(2,1)}, bf16[2,256,512]{2,1,0:T(8,128)(2,1)S(1)}, u32[]{:S(2)}, u32[]{:S(2)}) %collective-permute-start) | collective-permute-done | bytes 524320 | tf_op jit(solution)/shard_map/ppermute | solution.py:464
  25.5 0.0 collective-permute-start.2
  25.5 7.0 %collective-permute-done.1.push = bf16[2,272,512]{2,1,0:T(8,128)(2,1)S(1)} collective-permute-done((bf16[2,272,512]{2,1,0:T(8,128)(2,1)}, bf16[2,272,512]{2,1,0:T(8,128)(2,1)S(1)}, u32[]{:S(2)}, u32[]{:S(2)}) %collective-permute-start.1) | collective-permute-done | bytes 557088 | tf_op jit(solution)/shard_map/ppermute | solution.py:464
  32.5 0.0 collective-permute-done.2.pull_other
  32.5 0.1 collective-permute-start.3
  32.6 1.9 %collective-permute-done.3.push_other = bf16[2,272,512]{2,1,0:T(8,128)(2,1)S(1)} collective-permute-done((bf16[2,272,512]{2,1,0:T(8,128)(2,1)S(1)}, bf16[2,272,512]{2,1,0:T(8,128)(2,1)S(1)}, u32[]{:S(2)}, u32[]{:S(2)}) %collective-permute-start.3) | collective-permute-done | bytes 557088 | tf_op jit(solution)/shard_map/ppermute | solution.py:467
  34.6 0.0 copy-done.8
  34.6 0.8 copy-done.9
  35.4 14.7 %cross.1 = (bf16[2,128,2048]{2,1,0:T(8,128)(2,1)}, bf16[2,128,2048]{2,1,0:T(8,128)(2,1)}, f32[2,2048]{1,0:T(2,128)}, bf16[2,128,1024]{2,1,0:T(8,128)(2,1)}, f32[...) custom-call(s32[4]{0:T(128)} %pad_add_fusion.scal, ...), custom_call_target="tpu_custom_call", output_to_operand_aliasing={{0}: (5, {}), {1}: (6, {})} | custom-call | flops 4000000000 | bytes 8000000 | tf_op jit(solution)/shard_map/cross/pallas_call | solution.py:541
  50.1 0.0 copy-start.5
  50.1 0.0 copy-start.6
  50.1 0.0 copy-start.7
  50.1 0.2 collective-permute-start.4
  50.3 12.7 %all-to-all-start = ((bf16[64,32,128]{2,1,0:T(8,128)(2,1)}), bf16[64,32,128]{2,1,0:T(8,128)(2,1)S(1)}, u32[]{:S(2)}, u32[]{:S(2)}) async-start(bf16[64,32,128]{2,1,0:T(8,128)(2,1)} %get-tuple-element.69), calls=%async_computation | async-start | bytes 1048576 | tf_op jit(solution)/shard_map/all_to_all | solution.py:556
  63.0 0.2 collective-permute-start.5
  63.1 0.4 collective-permute-start.6
  63.6 1.0 collective-permute-done.6
  64.6 0.6 add.9.gain
  65.2 0.6 collective-permute-start.7
  65.8 0.0 collective-permute-done.5.stats_received
  65.8 0.0 collective-permute-done.4.received
  65.8 0.0 copy-done.4
  65.9 1.2 %copy-done.1 = bf16[2,128,2048]{2,1,0:T(8,128)(2,1)S(1)} copy-done((bf16[2,128,2048]{2,1,0:T(8,128)(2,1)S(1)}, bf16[2,128,2048]{2,1,0:T(8,128)(2,1)}, u32[]{:S(2)}) %copy-start.1) | copy-done | bytes 1048600
  67.1 0.7 copy-done.3
  67.8 1.0 pair.1
  68.8 1.5 %collective-permute-done.7.gain_received = f32[1,512]{1,0:T(1,128)S(1)} collective-permute-done((f32[1,512]{1,0:T(1,128)S(1)}, f32[1,512]{1,0:T(1,128)S(1)}, u32[]{:S(2)}, u32[]{:S(2)}) %collective-permute-start.7) | collective-permute-done | bytes 2080 | tf_op jit(solution)/shard_map/ppermute | solution.py:467
  70.3 1.7 %collective-permute-start.8 = (bf16[128,2048]{1,0:T(8,128)(2,1)S(1)}, bf16[128,2048]{1,0:T(8,128)(2,1)S(1)}, u32[]{:S(2)}, u32[]{:S(2)}) collective-permute-start(bf16[128,2048]{1,0:T(8,128)(2,1)S(1)} %get-tuple-element.62), channel_id=1, source_target_pairs={{0,2},{1,3},{2,0},{3,1},{4,6},{5,7},{6,4},{7,5},{8,10},{9,11},{10,... | collective-permute-start | bytes 1572872 | tf_op jit(solution)/shard_map/ppermute | solution.py:467
  72.1 1.8 %collective-permute-start.9 = (f32[2,2048]{1,0:T(2,128)S(1)}, f32[2,2048]{1,0:T(2,128)S(1)}, u32[]{:S(2)}, u32[]{:S(2)}) collective-permute-start(f32[2,2048]{1,0:T(2,128)S(1)} %get-tuple-element.63.stats), channel_id=1, source_target_pairs={{0,2},{1,3},{2,0},{3,1},{4,6},{5,7},{6,4},{7,5},{8,10},{9,11},{10,... | collective-permute-start | bytes 49160 | tf_op jit(solution)/shard_map/ppermute | solution.py:467
  73.8 7.7 %all-to-all-done.received = bf16[64,32,128]{2,1,0:T(8,128)(2,1)S(1)} async-done(((bf16[64,32,128]{2,1,0:T(8,128)(2,1)}), bf16[64,32,128]{2,1,0:T(8,128)(2,1)S(1)}, u32[]{:S(2)}, u32[]{:S(2)}) %all-to-all-start) | async-done | bytes 524320 | tf_op jit(solution)/shard_map/all_to_all | solution.py:556
  81.5 1.5 %total.1 = bf16[64,40,128]{2,1,0:T(8,128)(2,1)} custom-call(s32[4]{0:T(128)S(1)} %copy-done.4, bf16[64,32,128]{2,1,0:T(8,128)(2,1)S(1)} %all-to-all-done.received, f32[1,512]{1,0:T(1,128)S(1)} %add.9.gain, f32[1,512]{1,0:T(1,128)S(1)} %collective-permute-done.7.gain_received), custom_call_target="tpu_custom_call" | custom-call | tf_op jit(solution)/shard_map/total/pallas_call | solution.py:595
  83.1 5.5 %all-to-all-start.1 = ((bf16[64,40,128]{2,1,0:T(8,128)(2,1)}), bf16[64,40,128]{2,1,0:T(8,128)(2,1)S(1)}, u32[]{:S(2)}, u32[]{:S(2)}) async-start(bf16[64,40,128]{2,1,0:T(8,128)(2,1)} %total.1), calls=%async_computation.1 | async-start | bytes 1310720 | tf_op jit(solution)/shard_map/all_to_all | solution.py:603
  88.6 0.0 collective-permute-done.9.stats_received
  88.6 0.0 collective-permute-done.8.received
  88.6 0.0 copy-start
  88.6 0.0 copy-start.2
  88.6 1.2 branch.1
  89.8 1.6 %collective-permute-start.10 = (bf16[128,512]{1,0:T(8,128)(2,1)S(1)}, bf16[128,512]{1,0:T(8,128)(2,1)S(1)}, u32[]{:S(2)}, u32[]{:S(2)}) collective-permute-start(bf16[128,512]{1,0:T(8,128)(2,1)S(1)} %get-tuple-element.67), channel_id=1, source_target_pairs={{0,4},{4,8},{8,12},{12,16},{16,20},{20,24},{24,28},{28,32},{32,36}... | collective-permute-start | bytes 393224 | tf_op jit(solution)/shard_map/ppermute | solution.py:464
  91.5 4.7 %collective-permute-start.11 = (bf16[128,512]{1,0:T(8,128)(2,1)S(1)}, bf16[128,512]{1,0:T(8,128)(2,1)S(1)}, u32[]{:S(2)}, u32[]{:S(2)}) collective-permute-start(bf16[128,512]{1,0:T(8,128)(2,1)S(1)} %get-tuple-element.68), channel_id=1, source_target_pairs={{0,252},{4,0},{8,4},{12,8},{16,12},{20,16},{24,20},{28,24},{32,28}... | collective-permute-start | bytes 393224 | tf_op jit(solution)/shard_map/ppermute | solution.py:464
  96.1 14.7 %collective-permute-done.10.from_before = bf16[128,512]{1,0:T(8,128)(2,1)S(1)} collective-permute-done((bf16[128,512]{1,0:T(8,128)(2,1)S(1)}, bf16[128,512]{1,0:T(8,128)(2,1)S(1)}, u32[]{:S(2)}, u32[]{:S(2)}) %collective-permute-start.10) | collective-permute-done | bytes 131104 | tf_op jit(solution)/shard_map/ppermute | solution.py:464
  110.9 0.0 collective-permute-done.11.from_after
  110.9 3.5 %place.1 = bf16[3,1024,128]{2,1,0:T(8,128)(2,1)} custom-call(s32[4]{0:T(128)S(1)} %copy-done.4, s32[3,1024]{1,0:T(4,128)S(1)} %copy-done.2, s32[1]{0:T(128)} %get-tuple-element.55.before, bf16[3,1024,512]{2,1,0:T(8,128)(2,1)S(1)} %copy-done, bf16[2,128,1024]{2,1,0:T(8,128)(2,1)S(1)} %get-tuple-element.66.branch, ...), custom_call_target="tpu_custom_call" | custom-call | flops 10000000000 | bytes 1000 | tf_op jit(solution)/shard_map/place/pallas_call | solution.py:605
  114.4 0.0 all-to-all-done.1.received
  114.4 1.1 finish.1
  (14 shorter events, 0.0 us)
Async XLA Ops:
  5.1 20.3 %collective-permute-start = (bf16[2,256,512]{2,1,0:T(8,128)(2,1)}, bf16[2,256,512]{2,1,0:T(8,128)(2,1)S(1)}, u32[]{:S(2)}, u32[]{:S(2)}) collective-permute-start(bf16[2,256,512]{2,1,0:T(8,128)(2,1)} %get-tuple-element.39), channel_id=1, source_target_pairs={{0,252},{4,0},{8,4},{12,8},{16,12},{20,16},{24,20},{28,24},{32,28}... | collective-permute-start | bytes 1572872 | tf_op jit(solution)/shard_map/ppermute | solution.py:464
  14.0 18.5 %collective-permute-start.1 = (bf16[2,272,512]{2,1,0:T(8,128)(2,1)}, bf16[2,272,512]{2,1,0:T(8,128)(2,1)S(1)}, u32[]{:S(2)}, u32[]{:S(2)}) collective-permute-start(bf16[2,272,512]{2,1,0:T(8,128)(2,1)} %get-tuple-element.42), channel_id=1, source_target_pairs={{0,4},{4,8},{8,12},{12,16},{16,20},{20,24},{24,28},{28,32},{32,36}... | collective-permute-start | bytes 1671176 | tf_op jit(solution)/shard_map/ppermute | solution.py:464
  25.5 9.1 %copy-start.10 = (bf16[2,256,512]{2,1,0:T(8,128)(2,1)}, bf16[2,256,512]{2,1,0:T(8,128)(2,1)S(1)}, u32[]{:S(2)}) copy-start(bf16[2,256,512]{2,1,0:T(8,128)(2,1)S(1)} %collective-permute-done.pull) | copy-start | bytes 1572868
  25.5 7.0 %collective-permute-start.2 = (bf16[2,256,512]{2,1,0:T(8,128)(2,1)S(1)}, bf16[2,256,512]{2,1,0:T(8,128)(2,1)S(1)}, u32[]{:S(2)}, u32[]{:S(2)}) collective-permute-start(bf16[2,256,512]{2,1,0:T(8,128)(2,1)S(1)} %collective-permute-done.pull), channel_id=1, source_target_pairs={{0,1},{1,0},{2,3},{3,2},{4,5},{5,4},{6,7},{7,6},{8,9},{9,8},{10,11... | collective-permute-start | bytes 1572872 | tf_op jit(solution)/shard_map/ppermute | solution.py:467
  32.5 2.1 %copy-start.8 = (bf16[2,272,512]{2,1,0:T(8,128)(2,1)}, bf16[2,272,512]{2,1,0:T(8,128)(2,1)S(1)}, u32[]{:S(2)}) copy-start(bf16[2,272,512]{2,1,0:T(8,128)(2,1)S(1)} %collective-permute-done.1.push) | copy-start | bytes 1671172
  32.5 2.1 %copy-start.11 = (bf16[2,256,512]{2,1,0:T(8,128)(2,1)}, bf16[2,256,512]{2,1,0:T(8,128)(2,1)S(1)}, u32[]{:S(2)}) copy-start(bf16[2,256,512]{2,1,0:T(8,128)(2,1)S(1)} %collective-permute-done.2.pull_other) | copy-start | bytes 1572868
  32.5 2.0 %collective-permute-start.3 = (bf16[2,272,512]{2,1,0:T(8,128)(2,1)S(1)}, bf16[2,272,512]{2,1,0:T(8,128)(2,1)S(1)}, u32[]{:S(2)}, u32[]{:S(2)}) collective-permute-start(bf16[2,272,512]{2,1,0:T(8,128)(2,1)S(1)} %collective-permute-done.1.push), channel_id=1, source_target_pairs={{0,1},{1,0},{2,3},{3,2},{4,5},{5,4},{6,7},{7,6},{8,9},{9,8},{10,11... | collective-permute-start | bytes 1671176 | tf_op jit(solution)/shard_map/ppermute | solution.py:467
  34.6 0.8 copy-start.9
  35.4 30.5 %copy-start.4 = (s32[4]{0:T(128)S(1)}, s32[4]{0:T(128)}, u32[]{:S(2)}) copy-start(s32[4]{0:T(128)} %pad_add_fusion.scal) | copy-start | bytes 52
  50.1 38.5 %copy-start.5 = (f32[512]{0:T(512)S(1)}, f32[512]{0:T(512)}, u32[]{:S(2)}) copy-start(f32[512]{0:T(512)} %param.11) | copy-start | bytes 6148
  50.1 38.5 %copy-start.6 = (bf16[2,128,1024]{2,1,0:T(8,128)(2,1)S(1)}, bf16[2,128,1024]{2,1,0:T(8,128)(2,1)}, u32[]{:S(2)}) copy-start(bf16[2,128,1024]{2,1,0:T(8,128)(2,1)} %get-tuple-element.64.unit) | copy-start | bytes 1572868
  50.1 38.5 %copy-start.7 = (f32[2,8,1024]{2,1,0:T(8,128)S(1)}, f32[2,8,1024]{2,1,0:T(8,128)}, u32[]{:S(2)}) copy-start(f32[2,8,1024]{2,1,0:T(8,128)} %get-tuple-element.65.stat) | copy-start | bytes 196612
  50.1 15.8 %collective-permute-start.4 = (bf16[2,128,2048]{2,1,0:T(8,128)(2,1)}, bf16[2,128,2048]{2,1,0:T(8,128)(2,1)S(1)}, u32[]{:S(2)}, u32[]{:S(2)}) collective-permute-start(bf16[2,128,2048]{2,1,0:T(8,128)(2,1)} %get-tuple-element.57), channel_id=1, source_target_pairs={{0,1},{1,0},{2,3},{3,2},{4,5},{5,4},{6,7},{7,6},{8,9},{9,8},{10,11... | collective-permute-start | bytes 3145736 | tf_op jit(solution)/shard_map/ppermute | solution.py:467
  50.3 31.2 %all-to-all-start = ((bf16[64,32,128]{2,1,0:T(8,128)(2,1)}), bf16[64,32,128]{2,1,0:T(8,128)(2,1)S(1)}, u32[]{:S(2)}, u32[]{:S(2)}) async-start(bf16[64,32,128]{2,1,0:T(8,128)(2,1)} %get-tuple-element.69), calls=%async_computation | async-start | bytes 1048576 | tf_op jit(solution)/shard_map/all_to_all | solution.py:556
  63.0 2.9 %collective-permute-start.5 = (f32[2,2048]{1,0:T(2,128)}, f32[2,2048]{1,0:T(2,128)S(1)}, u32[]{:S(2)}, u32[]{:S(2)}) collective-permute-start(f32[2,2048]{1,0:T(2,128)} %get-tuple-element.58.stats), channel_id=1, source_target_pairs={{0,1},{1,0},{2,3},{3,2},{4,5},{5,4},{6,7},{7,6},{8,9},{9,8},{10,11... | collective-permute-start | bytes 49160 | tf_op jit(solution)/shard_map/ppermute | solution.py:467
  63.1 1.5 %collective-permute-start.6 = (f32[1,512]{1,0:T(1,128)}, f32[1,512]{1,0:T(1,128)S(1)}, u32[]{:S(2)}, u32[]{:S(2)}) collective-permute-start(f32[1,512]{1,0:T(1,128)} %get-tuple-element.61), channel_id=1, source_target_pairs={{0,1},{1,0},{2,3},{3,2},{4,5},{5,4},{6,7},{7,6},{8,9},{9,8},{10,11... | collective-permute-start | bytes 6152 | tf_op jit(solution)/shard_map/ppermute | solution.py:467
  65.2 5.1 %collective-permute-start.7 = (f32[1,512]{1,0:T(1,128)S(1)}, f32[1,512]{1,0:T(1,128)S(1)}, u32[]{:S(2)}, u32[]{:S(2)}) collective-permute-start(f32[1,512]{1,0:T(1,128)S(1)} %add.9.gain), channel_id=1, source_target_pairs={{0,2},{1,3},{2,0},{3,1},{4,6},{5,7},{6,4},{7,5},{8,10},{9,11},{10,... | collective-permute-start | bytes 6152 | tf_op jit(solution)/shard_map/ppermute | solution.py:467
  65.9 1.2 %copy-start.1 = (bf16[2,128,2048]{2,1,0:T(8,128)(2,1)S(1)}, bf16[2,128,2048]{2,1,0:T(8,128)(2,1)}, u32[]{:S(2)}) copy-start(bf16[2,128,2048]{2,1,0:T(8,128)(2,1)} %get-tuple-element.56.keep) | copy-start | bytes 3145732
  67.1 0.7 copy-start.3
  70.3 18.3 %collective-permute-start.8 = (bf16[128,2048]{1,0:T(8,128)(2,1)S(1)}, bf16[128,2048]{1,0:T(8,128)(2,1)S(1)}, u32[]{:S(2)}, u32[]{:S(2)}) collective-permute-start(bf16[128,2048]{1,0:T(8,128)(2,1)S(1)} %get-tuple-element.62), channel_id=1, source_target_pairs={{0,2},{1,3},{2,0},{3,1},{4,6},{5,7},{6,4},{7,5},{8,10},{9,11},{10,... | collective-permute-start | bytes 1572872 | tf_op jit(solution)/shard_map/ppermute | solution.py:467
  72.1 16.5 %collective-permute-start.9 = (f32[2,2048]{1,0:T(2,128)S(1)}, f32[2,2048]{1,0:T(2,128)S(1)}, u32[]{:S(2)}, u32[]{:S(2)}) collective-permute-start(f32[2,2048]{1,0:T(2,128)S(1)} %get-tuple-element.63.stats), channel_id=1, source_target_pairs={{0,2},{1,3},{2,0},{3,1},{4,6},{5,7},{6,4},{7,5},{8,10},{9,11},{10,... | collective-permute-start | bytes 49160 | tf_op jit(solution)/shard_map/ppermute | solution.py:467
  83.1 31.3 %all-to-all-start.1 = ((bf16[64,40,128]{2,1,0:T(8,128)(2,1)}), bf16[64,40,128]{2,1,0:T(8,128)(2,1)S(1)}, u32[]{:S(2)}, u32[]{:S(2)}) async-start(bf16[64,40,128]{2,1,0:T(8,128)(2,1)} %total.1), calls=%async_computation.1 | async-start | bytes 1310720 | tf_op jit(solution)/shard_map/all_to_all | solution.py:603
  88.6 22.2 %copy-start = (bf16[3,1024,512]{2,1,0:T(8,128)(2,1)S(1)}, bf16[3,1024,512]{2,1,0:T(8,128)(2,1)}, u32[]{:S(2)}) copy-start(bf16[3,1024,512]{2,1,0:T(8,128)(2,1)} %cotangent.5) | copy-start | bytes 9437188
  88.6 22.2 %copy-start.2 = (s32[3,1024]{1,0:T(4,128)S(1)}, s32[3,1024]{1,0:T(4,128)}, u32[]{:S(2)}) copy-start(s32[3,1024]{1,0:T(4,128)} %order.3) | copy-start | bytes 36868
  89.8 21.0 %collective-permute-start.10 = (bf16[128,512]{1,0:T(8,128)(2,1)S(1)}, bf16[128,512]{1,0:T(8,128)(2,1)S(1)}, u32[]{:S(2)}, u32[]{:S(2)}) collective-permute-start(bf16[128,512]{1,0:T(8,128)(2,1)S(1)} %get-tuple-element.67), channel_id=1, source_target_pairs={{0,4},{4,8},{8,12},{12,16},{16,20},{20,24},{24,28},{28,32},{32,36}... | collective-permute-start | bytes 393224 | tf_op jit(solution)/shard_map/ppermute | solution.py:464
  91.5 19.4 %collective-permute-start.11 = (bf16[128,512]{1,0:T(8,128)(2,1)S(1)}, bf16[128,512]{1,0:T(8,128)(2,1)S(1)}, u32[]{:S(2)}, u32[]{:S(2)}) collective-permute-start(bf16[128,512]{1,0:T(8,128)(2,1)S(1)} %get-tuple-element.68), channel_id=1, source_target_pairs={{0,252},{4,0},{8,4},{12,8},{16,12},{20,16},{24,20},{28,24},{32,28}... | collective-permute-start | bytes 393224 | tf_op jit(solution)/shard_map/ppermute | solution.py:464

commit v7 on v5

--- a/solution.py
+++ b/solution.py
@@ -247,8 +247,12 @@
         @pl.when(jnp.logical_not(whole))
         def _():
             here = pl.ds(pl.multiple_of(half * p, half), half)
-            nrm_o[p] = nrm[here, :]
-            dy_o[p] = dy[here, :]
+            copies = [pltpu.make_async_copy(nrm.at[here], nrm_o.at[p], work[-1].at[p, 0]),
+                      pltpu.make_async_copy(dy.at[here], dy_o.at[p], work[-1].at[p, 1])]
+            for copy in copies:
+                copy.start()
+            for copy in copies:
+                copy.wait()
 
         return carry
 
@@ -519,7 +523,7 @@
     send, keep, stats, unit, inverse, wacc, weights, wt, nrm, dy = pl.pallas_call(
         local_kernel,
         in_specs=[SMEM] + [VMEM] * 6,
-        out_specs=[ANY] * 2 + [VMEM] * 8,
+        out_specs=[ANY] * 2 + [VMEM] * 6 + [ANY] * 2,
         out_shape=shared + [
             sds((512, width), F32),
             sds((width + 16, 384), BF16),

time: 116 us -> 116 us (level)
  Pallas kernels: 48.6 us -> 36.4 us
  waiting for transfers between devices: 27.2 us -> 35.5 us
  starting transfers between devices: 34 us -> 37.1 us
    pallas_call x1, Pallas kernels: 30 us -> 9.62 us  [shards(): pl.pallas_call(local_kernel, in_specs=[SMEM] + [VMEM] * 6, out_specs=[ANY...]
    pallas_call x1, Pallas kernels: 5.63 us -> 14.7 us  [shards(): pl.pallas_call(functools.partial(cross_kernel, factor), in_specs=[SMEM] +...]
    ppermute x4, waiting for transfers between devices: 14.7 us -> 23 us  [passed(): lax.ppermute(x, 'curve', [(i, (i + by) % curve) for i in range(curve)])]
    all_to_all x1, starting transfers between devices: 7.74 us -> 10.9 us  [shards(): received = lax.all_to_all(pieces, 'curve', 0, 0)]
  transfers between devices with their start and end apart: 14 -> 14, of which waited for: 5 -> 7; matrix products, arithmetic and copies ran while one was open for 1% -> 1% of each run, Pallas kernels for 33% -> 15%
where the time goes in v7:
time: 116 us; the launch traced here: 115 us
  starting transfers between devices  37.1 us (32%)
  Pallas kernels  36.4 us (31%)
  waiting for transfers between devices  35.5 us (31%)
  local copies, waits for them, and re-layouts  2.93 us (3%)
  between operations  1.46 us (1%)
  other arithmetic  1.22 us (1%)
    ppermute x4, waiting for transfers between devices, passed(): lax.ppermute(x, 'curve', [(i, (i + by) % curve) for i in range(curve)])  23 us
    ppermute x4, starting transfers between devices, passed(): lax.ppermute(x, 'curve', [(i, (i + by) % curve) for i in range(curve)])  15.2 us
    pallas_call x1, Pallas kernels, shards(): pl.pallas_call(functools.partial(cross_kernel, factor), in_specs=[SMEM] +...  14.7 us
    all_to_all x1, starting transfers between devices, shards(): received = lax.all_to_all(pieces, 'curve', 0, 0)  10.9 us
    pallas_call x1, Pallas kernels, shards(): pl.pallas_call(local_kernel, in_specs=[SMEM] + [VMEM] * 6, out_specs=[ANY...  9.62 us
    all_to_all x1, waiting for transfers between devices, shards(): received = lax.all_to_all(pieces, 'curve', 0, 0)  7.69 us
    ppermute x8, starting transfers between devices, swapped(): return lax.ppermute(x, 'mp', [(i, i ^ bit) for i in range(4)])  5.5 us
    all_to_all x1, starting transfers between devices, shards(): gathered = lax.all_to_all(totals, 'curve', 0, 0)  5.48 us
  transfers between devices with their start and end apart: 14, of which 7 were waited for; matrix products, arithmetic and copies ran while one was open for 1% of the time, Pallas kernels for 15%

profile of v7, /device:TPU:16, one launch (start us, length us, event | category | flops | bytes accessed | tf_op | source)
XLA Modules:
  0.0 114.6 jit_solution(2121207168470575652)
XLA Ops:
  1.3 3.9 %halo.1 = (bf16[2,256,512]{2,1,0:T(8,128)(2,1)}, bf16[2,272,512]{2,1,0:T(8,128)(2,1)}) custom-call(s32[1]{0:T(128)S(6)} %copy.15.counts, s32[3,1024]{1,0:T(4,128)} %order.3, bf16[3,1024,512]{2,1,0:T(8,128)(2,1)} %points.3, bf16[3,1024,512]{2,1,0:T(8,128)(2,1)} %cotangent.5), custom_call_target="tpu_custom_call" | custom-call | tf_op jit(solution)/shard_map/halo/pallas_call | solution.py:473
  5.1 8.8 %collective-permute-start = (bf16[2,256,512]{2,1,0:T(8,128)(2,1)}, bf16[2,256,512]{2,1,0:T(8,128)(2,1)S(1)}, u32[]{:S(2)}, u32[]{:S(2)}) collective-permute-start(bf16[2,256,512]{2,1,0:T(8,128)(2,1)} %get-tuple-element.38), channel_id=1, source_target_pairs={{0,252},{4,0},{8,4},{12,8},{16,12},{20,16},{24,20},{28,24},{32,28}... | collective-permute-start | bytes 1572872 | tf_op jit(solution)/shard_map/ppermute | solution.py:468
  14.0 0.0 collective-permute-start.1
  14.0 0.6 pad_add_fusion.scal
  14.6 9.6 %local.1 = (bf16[2,128,2048]{2,1,0:T(8,128)(2,1)}, bf16[2,128,2048]{2,1,0:T(8,128)(2,1)}, f32[2,2048]{1,0:T(2,128)}, bf16[2,128,1024]{2,1,0:T(8,128)(2,1)}, f32[...) custom-call(s32[4]{0:T(128)} %pad_add_fusion.scal, ...), custom_call_target="tpu_custom_call" | custom-call | flops 16000000000 | bytes 16000000 | tf_op jit(solution)/shard_map/local/pallas_call | solution.py:523
  24.2 1.3 %collective-permute-done.pull = bf16[2,256,512]{2,1,0:T(8,128)(2,1)S(1)} collective-permute-done((bf16[2,256,512]{2,1,0:T(8,128)(2,1)}, bf16[2,256,512]{2,1,0:T(8,128)(2,1)S(1)}, u32[]{:S(2)}, u32[]{:S(2)}) %collective-permute-start) | collective-permute-done | bytes 524320 | tf_op jit(solution)/shard_map/ppermute | solution.py:468
  25.5 7.0 %collective-permute-done.1.push = bf16[2,272,512]{2,1,0:T(8,128)(2,1)S(1)} collective-permute-done((bf16[2,272,512]{2,1,0:T(8,128)(2,1)}, bf16[2,272,512]{2,1,0:T(8,128)(2,1)S(1)}, u32[]{:S(2)}, u32[]{:S(2)}) %collective-permute-start.1) | collective-permute-done | bytes 557088 | tf_op jit(solution)/shard_map/ppermute | solution.py:468
  32.5 0.0 collective-permute-start.3
  32.5 0.5 collective-permute-start.2
  33.0 2.2 %collective-permute-done.2.pull_other = bf16[2,256,512]{2,1,0:T(8,128)(2,1)S(1)} collective-permute-done((bf16[2,256,512]{2,1,0:T(8,128)(2,1)S(1)}, bf16[2,256,512]{2,1,0:T(8,128)(2,1)S(1)}, u32[]{:S(2)}, u32[]{:S(2)}) %collective-permute-start.2) | collective-permute-done | bytes 524320 | tf_op jit(solution)/shard_map/ppermute | solution.py:471
  35.2 0.0 collective-permute-done.3.push_other
  35.2 0.0 copy-done.10
  35.2 0.8 copy-done.11
  36.0 0.2 copy-done.9
  36.2 14.7 %cross.1 = (bf16[2,128,2048]{2,1,0:T(8,128)(2,1)}, bf16[2,128,2048]{2,1,0:T(8,128)(2,1)}, f32[2,2048]{1,0:T(2,128)}, bf16[2,128,1024]{2,1,0:T(8,128)(2,1)}, f32[...) custom-call(s32[4]{0:T(128)} %pad_add_fusion.scal, ...), custom_call_target="tpu_custom_call", output_to_operand_aliasing={{0}: (5, {}), {1}: (6, {})} | custom-call | flops 4000000000 | bytes 8000000 | tf_op jit(solution)/shard_map/cross/pallas_call | solution.py:542
  50.9 0.0 copy-start.5
  50.9 0.0 copy-start.6
  50.9 0.0 copy-start.7
  50.9 0.2 collective-permute-start.4
  51.1 10.9 %all-to-all-start = ((bf16[64,32,128]{2,1,0:T(8,128)(2,1)}), bf16[64,32,128]{2,1,0:T(8,128)(2,1)S(1)}, u32[]{:S(2)}, u32[]{:S(2)}) async-start(bf16[64,32,128]{2,1,0:T(8,128)(2,1)} %get-tuple-element.67), calls=%async_computation | async-start | bytes 1048576 | tf_op jit(solution)/shard_map/all_to_all | solution.py:557
  62.1 0.2 collective-permute-start.5
  62.2 0.4 collective-permute-start.6
  62.7 1.0 collective-permute-done.6
  63.7 0.6 add.9.gain
  64.3 0.6 collective-permute-start.7
  64.9 0.0 collective-permute-done.5.stats_received
  64.9 0.0 collective-permute-done.4.received
  65.0 1.2 %copy-done.1 = bf16[2,128,2048]{2,1,0:T(8,128)(2,1)S(1)} copy-done((bf16[2,128,2048]{2,1,0:T(8,128)(2,1)S(1)}, bf16[2,128,2048]{2,1,0:T(8,128)(2,1)}, u32[]{:S(2)}) %copy-start.1) | copy-done | bytes 1048600
  66.2 0.7 copy-done.3
  66.9 1.0 pair.1
  67.9 1.5 %collective-permute-done.7.gain_received = f32[1,512]{1,0:T(1,128)S(1)} collective-permute-done((f32[1,512]{1,0:T(1,128)S(1)}, f32[1,512]{1,0:T(1,128)S(1)}, u32[]{:S(2)}, u32[]{:S(2)}) %collective-permute-start.7) | collective-permute-done | bytes 2080 | tf_op jit(solution)/shard_map/ppermute | solution.py:471
  69.4 1.7 %collective-permute-start.8 = (bf16[128,2048]{1,0:T(8,128)(2,1)S(1)}, bf16[128,2048]{1,0:T(8,128)(2,1)S(1)}, u32[]{:S(2)}, u32[]{:S(2)}) collective-permute-start(bf16[128,2048]{1,0:T(8,128)(2,1)S(1)} %get-tuple-element.60), channel_id=1, source_target_pairs={{0,2},{1,3},{2,0},{3,1},{4,6},{5,7},{6,4},{7,5},{8,10},{9,11},{10,... | collective-permute-start | bytes 1572872 | tf_op jit(solution)/shard_map/ppermute | solution.py:471
  71.1 1.8 %collective-permute-start.9 = (f32[2,2048]{1,0:T(2,128)S(1)}, f32[2,2048]{1,0:T(2,128)S(1)}, u32[]{:S(2)}, u32[]{:S(2)}) collective-permute-start(f32[2,2048]{1,0:T(2,128)S(1)} %get-tuple-element.61.stats), channel_id=1, source_target_pairs={{0,2},{1,3},{2,0},{3,1},{4,6},{5,7},{6,4},{7,5},{8,10},{9,11},{10,... | collective-permute-start | bytes 49160 | tf_op jit(solution)/shard_map/ppermute | solution.py:471
  72.9 7.7 %all-to-all-done.received = bf16[64,32,128]{2,1,0:T(8,128)(2,1)S(1)} async-done(((bf16[64,32,128]{2,1,0:T(8,128)(2,1)}), bf16[64,32,128]{2,1,0:T(8,128)(2,1)S(1)}, u32[]{:S(2)}, u32[]{:S(2)}) %all-to-all-start) | async-done | bytes 524320 | tf_op jit(solution)/shard_map/all_to_all | solution.py:557
  80.6 1.5 %total.1 = bf16[64,40,128]{2,1,0:T(8,128)(2,1)} custom-call(s32[4]{0:T(128)S(1)} %copy-done.4, bf16[64,32,128]{2,1,0:T(8,128)(2,1)S(1)} %all-to-all-done.received, f32[1,512]{1,0:T(1,128)S(1)} %add.9.gain, f32[1,512]{1,0:T(1,128)S(1)} %collective-permute-done.7.gain_received), custom_call_target="tpu_custom_call" | custom-call | tf_op jit(solution)/shard_map/total/pallas_call | solution.py:596
  82.2 5.5 %all-to-all-start.1 = ((bf16[64,40,128]{2,1,0:T(8,128)(2,1)}), bf16[64,40,128]{2,1,0:T(8,128)(2,1)S(1)}, u32[]{:S(2)}, u32[]{:S(2)}) async-start(bf16[64,40,128]{2,1,0:T(8,128)(2,1)} %total.1), calls=%async_computation.1 | async-start | bytes 1310720 | tf_op jit(solution)/shard_map/all_to_all | solution.py:604
  87.7 0.0 collective-permute-done.9.stats_received
  87.7 0.0 collective-permute-done.8.received
  87.7 0.0 copy-start
  87.7 0.0 copy-start.2
  87.7 1.2 %branch.1 = (bf16[2,128,1024]{2,1,0:T(8,128)(2,1)S(1)}, bf16[128,512]{1,0:T(8,128)(2,1)S(1)}, bf16[128,512]{1,0:T(8,128)(2,1)S(1)}) custom-call(s32[4]{0:T(128)S(1)} %copy-done.4, bf16[128,2048]{1,0:T(8,128)(2,1)S(1)} %get-tuple-element.57.kept, bf16[128,2048]{1,0:T(8,128)(2,1)S(1)} %collective-permute-done.8.received, ...), custom_call_target="tpu_custom_call" | custom-call | flops 10000000000 | bytes 1000 | tf_op jit(solution)/shard_map/branch/pallas_call | solution.py:583
  88.9 1.6 %collective-permute-start.10 = (bf16[128,512]{1,0:T(8,128)(2,1)S(1)}, bf16[128,512]{1,0:T(8,128)(2,1)S(1)}, u32[]{:S(2)}, u32[]{:S(2)}) collective-permute-start(bf16[128,512]{1,0:T(8,128)(2,1)S(1)} %get-tuple-element.65), channel_id=1, source_target_pairs={{0,4},{4,8},{8,12},{12,16},{16,20},{20,24},{24,28},{28,32},{32,36}... | collective-permute-start | bytes 393224 | tf_op jit(solution)/shard_map/ppermute | solution.py:468
  90.5 4.7 %collective-permute-start.11 = (bf16[128,512]{1,0:T(8,128)(2,1)S(1)}, bf16[128,512]{1,0:T(8,128)(2,1)S(1)}, u32[]{:S(2)}, u32[]{:S(2)}) collective-permute-start(bf16[128,512]{1,0:T(8,128)(2,1)S(1)} %get-tuple-element.66), channel_id=1, source_target_pairs={{0,252},{4,0},{8,4},{12,8},{16,12},{20,16},{24,20},{28,24},{32,28}... | collective-permute-start | bytes 393224 | tf_op jit(solution)/shard_map/ppermute | solution.py:468
  95.2 14.7 %collective-permute-done.10.from_before = bf16[128,512]{1,0:T(8,128)(2,1)S(1)} collective-permute-done((bf16[128,512]{1,0:T(8,128)(2,1)S(1)}, bf16[128,512]{1,0:T(8,128)(2,1)S(1)}, u32[]{:S(2)}, u32[]{:S(2)}) %collective-permute-start.10) | collective-permute-done | bytes 131104 | tf_op jit(solution)/shard_map/ppermute | solution.py:468
  109.9 0.0 collective-permute-done.11.from_after
  110.0 3.5 %place.1 = bf16[3,1024,128]{2,1,0:T(8,128)(2,1)} custom-call(s32[4]{0:T(128)S(1)} %copy-done.4, s32[3,1024]{1,0:T(4,128)S(1)} %copy-done.2, s32[1]{0:T(128)} %get-tuple-element.53.before, bf16[3,1024,512]{2,1,0:T(8,128)(2,1)S(1)} %copy-done, bf16[2,128,1024]{2,1,0:T(8,128)(2,1)S(1)} %get-tuple-element.64.branch, ...), custom_call_target="tpu_custom_call" | custom-call | flops 10000000000 | bytes 1000 | tf_op jit(solution)/shard_map/place/pallas_call | solution.py:606
  113.5 0.0 all-to-all-done.1.received
  113.5 1.1 finish.1
  (14 shorter events, 0.0 us)
Async XLA Ops:
  5.1 20.3 %collective-permute-start = (bf16[2,256,512]{2,1,0:T(8,128)(2,1)}, bf16[2,256,512]{2,1,0:T(8,128)(2,1)S(1)}, u32[]{:S(2)}, u32[]{:S(2)}) collective-permute-start(bf16[2,256,512]{2,1,0:T(8,128)(2,1)} %get-tuple-element.38), channel_id=1, source_target_pairs={{0,252},{4,0},{8,4},{12,8},{16,12},{20,16},{24,20},{28,24},{32,28}... | collective-permute-start | bytes 1572872 | tf_op jit(solution)/shard_map/ppermute | solution.py:468
  14.0 18.5 %collective-permute-start.1 = (bf16[2,272,512]{2,1,0:T(8,128)(2,1)}, bf16[2,272,512]{2,1,0:T(8,128)(2,1)S(1)}, u32[]{:S(2)}, u32[]{:S(2)}) collective-permute-start(bf16[2,272,512]{2,1,0:T(8,128)(2,1)} %get-tuple-element.39), channel_id=1, source_target_pairs={{0,4},{4,8},{8,12},{12,16},{16,20},{20,24},{24,28},{28,32},{32,36}... | collective-permute-start | bytes 1671176 | tf_op jit(solution)/shard_map/ppermute | solution.py:468
  25.5 9.7 %copy-start.10 = (bf16[2,256,512]{2,1,0:T(8,128)(2,1)}, bf16[2,256,512]{2,1,0:T(8,128)(2,1)S(1)}, u32[]{:S(2)}) copy-start(bf16[2,256,512]{2,1,0:T(8,128)(2,1)S(1)} %collective-permute-done.pull) | copy-start | bytes 1572868
  32.5 2.7 %copy-start.8 = (bf16[2,272,512]{2,1,0:T(8,128)(2,1)}, bf16[2,272,512]{2,1,0:T(8,128)(2,1)S(1)}, u32[]{:S(2)}) copy-start(bf16[2,272,512]{2,1,0:T(8,128)(2,1)S(1)} %collective-permute-done.1.push) | copy-start | bytes 1671172
  32.5 2.7 %collective-permute-start.3 = (bf16[2,272,512]{2,1,0:T(8,128)(2,1)S(1)}, bf16[2,272,512]{2,1,0:T(8,128)(2,1)S(1)}, u32[]{:S(2)}, u32[]{:S(2)}) collective-permute-start(bf16[2,272,512]{2,1,0:T(8,128)(2,1)S(1)} %collective-permute-done.1.push), channel_id=1, source_target_pairs={{0,1},{1,0},{2,3},{3,2},{4,5},{5,4},{6,7},{7,6},{8,9},{9,8},{10,11... | collective-permute-start | bytes 1671176 | tf_op jit(solution)/shard_map/ppermute | solution.py:471
  32.5 2.7 %collective-permute-start.2 = (bf16[2,256,512]{2,1,0:T(8,128)(2,1)S(1)}, bf16[2,256,512]{2,1,0:T(8,128)(2,1)S(1)}, u32[]{:S(2)}, u32[]{:S(2)}) collective-permute-start(bf16[2,256,512]{2,1,0:T(8,128)(2,1)S(1)} %collective-permute-done.pull), channel_id=1, source_target_pairs={{0,1},{1,0},{2,3},{3,2},{4,5},{5,4},{6,7},{7,6},{8,9},{9,8},{10,11... | collective-permute-start | bytes 1572872 | tf_op jit(solution)/shard_map/ppermute | solution.py:471
  35.2 0.8 copy-start.11
  35.2 1.0 copy-start.9
  36.2 28.8 %copy-start.4 = (s32[4]{0:T(128)S(1)}, s32[4]{0:T(128)}, u32[]{:S(2)}) copy-start(s32[4]{0:T(128)} %pad_add_fusion.scal) | copy-start | bytes 52
  50.9 36.8 %copy-start.5 = (f32[512]{0:T(512)S(1)}, f32[512]{0:T(512)}, u32[]{:S(2)}) copy-start(f32[512]{0:T(512)} %param.11) | copy-start | bytes 6148
  50.9 36.8 %copy-start.6 = (bf16[2,128,1024]{2,1,0:T(8,128)(2,1)S(1)}, bf16[2,128,1024]{2,1,0:T(8,128)(2,1)}, u32[]{:S(2)}) copy-start(bf16[2,128,1024]{2,1,0:T(8,128)(2,1)} %get-tuple-element.62.unit) | copy-start | bytes 1572868
  50.9 36.8 %copy-start.7 = (f32[2,8,1024]{2,1,0:T(8,128)S(1)}, f32[2,8,1024]{2,1,0:T(8,128)}, u32[]{:S(2)}) copy-start(f32[2,8,1024]{2,1,0:T(8,128)} %get-tuple-element.63.stat) | copy-start | bytes 196612
  50.9 14.0 %collective-permute-start.4 = (bf16[2,128,2048]{2,1,0:T(8,128)(2,1)}, bf16[2,128,2048]{2,1,0:T(8,128)(2,1)S(1)}, u32[]{:S(2)}, u32[]{:S(2)}) collective-permute-start(bf16[2,128,2048]{2,1,0:T(8,128)(2,1)} %get-tuple-element.55), channel_id=1, source_target_pairs={{0,1},{1,0},{2,3},{3,2},{4,5},{5,4},{6,7},{7,6},{8,9},{9,8},{10,11... | collective-permute-start | bytes 3145736 | tf_op jit(solution)/shard_map/ppermute | solution.py:471
  51.1 29.5 %all-to-all-start = ((bf16[64,32,128]{2,1,0:T(8,128)(2,1)}), bf16[64,32,128]{2,1,0:T(8,128)(2,1)S(1)}, u32[]{:S(2)}, u32[]{:S(2)}) async-start(bf16[64,32,128]{2,1,0:T(8,128)(2,1)} %get-tuple-element.67), calls=%async_computation | async-start | bytes 1048576 | tf_op jit(solution)/shard_map/all_to_all | solution.py:557
  62.1 2.9 %collective-permute-start.5 = (f32[2,2048]{1,0:T(2,128)}, f32[2,2048]{1,0:T(2,128)S(1)}, u32[]{:S(2)}, u32[]{:S(2)}) collective-permute-start(f32[2,2048]{1,0:T(2,128)} %get-tuple-element.56.stats), channel_id=1, source_target_pairs={{0,1},{1,0},{2,3},{3,2},{4,5},{5,4},{6,7},{7,6},{8,9},{9,8},{10,11... | collective-permute-start | bytes 49160 | tf_op jit(solution)/shard_map/ppermute | solution.py:471
  62.2 1.5 %collective-permute-start.6 = (f32[1,512]{1,0:T(1,128)}, f32[1,512]{1,0:T(1,128)S(1)}, u32[]{:S(2)}, u32[]{:S(2)}) collective-permute-start(f32[1,512]{1,0:T(1,128)} %get-tuple-element.59), channel_id=1, source_target_pairs={{0,1},{1,0},{2,3},{3,2},{4,5},{5,4},{6,7},{7,6},{8,9},{9,8},{10,11... | collective-permute-start | bytes 6152 | tf_op jit(solution)/shard_map/ppermute | solution.py:471
  64.3 5.1 %collective-permute-start.7 = (f32[1,512]{1,0:T(1,128)S(1)}, f32[1,512]{1,0:T(1,128)S(1)}, u32[]{:S(2)}, u32[]{:S(2)}) collective-permute-start(f32[1,512]{1,0:T(1,128)S(1)} %add.9.gain), channel_id=1, source_target_pairs={{0,2},{1,3},{2,0},{3,1},{4,6},{5,7},{6,4},{7,5},{8,10},{9,11},{10,... | collective-permute-start | bytes 6152 | tf_op jit(solution)/shard_map/ppermute | solution.py:471
  65.0 1.2 %copy-start.1 = (bf16[2,128,2048]{2,1,0:T(8,128)(2,1)S(1)}, bf16[2,128,2048]{2,1,0:T(8,128)(2,1)}, u32[]{:S(2)}) copy-start(bf16[2,128,2048]{2,1,0:T(8,128)(2,1)} %get-tuple-element.54.keep) | copy-start | bytes 3145732
  66.2 0.7 copy-start.3
  69.4 18.3 %collective-permute-start.8 = (bf16[128,2048]{1,0:T(8,128)(2,1)S(1)}, bf16[128,2048]{1,0:T(8,128)(2,1)S(1)}, u32[]{:S(2)}, u32[]{:S(2)}) collective-permute-start(bf16[128,2048]{1,0:T(8,128)(2,1)S(1)} %get-tuple-element.60), channel_id=1, source_target_pairs={{0,2},{1,3},{2,0},{3,1},{4,6},{5,7},{6,4},{7,5},{8,10},{9,11},{10,... | collective-permute-start | bytes 1572872 | tf_op jit(solution)/shard_map/ppermute | solution.py:471
  71.1 16.5 %collective-permute-start.9 = (f32[2,2048]{1,0:T(2,128)S(1)}, f32[2,2048]{1,0:T(2,128)S(1)}, u32[]{:S(2)}, u32[]{:S(2)}) collective-permute-start(f32[2,2048]{1,0:T(2,128)S(1)} %get-tuple-element.61.stats), channel_id=1, source_target_pairs={{0,2},{1,3},{2,0},{3,1},{4,6},{5,7},{6,4},{7,5},{8,10},{9,11},{10,... | collective-permute-start | bytes 49160 | tf_op jit(solution)/shard_map/ppermute | solution.py:471
  82.2 31.3 %all-to-all-start.1 = ((bf16[64,40,128]{2,1,0:T(8,128)(2,1)}), bf16[64,40,128]{2,1,0:T(8,128)(2,1)S(1)}, u32[]{:S(2)}, u32[]{:S(2)}) async-start(bf16[64,40,128]{2,1,0:T(8,128)(2,1)} %total.1), calls=%async_computation.1 | async-start | bytes 1310720 | tf_op jit(solution)/shard_map/all_to_all | solution.py:604
  87.7 22.2 %copy-start = (bf16[3,1024,512]{2,1,0:T(8,128)(2,1)S(1)}, bf16[3,1024,512]{2,1,0:T(8,128)(2,1)}, u32[]{:S(2)}) copy-start(bf16[3,1024,512]{2,1,0:T(8,128)(2,1)} %cotangent.5) | copy-start | bytes 9437188
  87.7 22.2 %copy-start.2 = (s32[3,1024]{1,0:T(4,128)S(1)}, s32[3,1024]{1,0:T(4,128)}, u32[]{:S(2)}) copy-start(s32[3,1024]{1,0:T(4,128)} %order.3) | copy-start | bytes 36868
  88.9 21.0 %collective-permute-start.10 = (bf16[128,512]{1,0:T(8,128)(2,1)S(1)}, bf16[128,512]{1,0:T(8,128)(2,1)S(1)}, u32[]{:S(2)}, u32[]{:S(2)}) collective-permute-start(bf16[128,512]{1,0:T(8,128)(2,1)S(1)} %get-tuple-element.65), channel_id=1, source_target_pairs={{0,4},{4,8},{8,12},{12,16},{16,20},{20,24},{24,28},{28,32},{32,36}... | collective-permute-start | bytes 393224 | tf_op jit(solution)/shard_map/ppermute | solution.py:468
  90.5 19.4 %collective-permute-start.11 = (bf16[128,512]{1,0:T(8,128)(2,1)S(1)}, bf16[128,512]{1,0:T(8,128)(2,1)S(1)}, u32[]{:S(2)}, u32[]{:S(2)}) collective-permute-start(bf16[128,512]{1,0:T(8,128)(2,1)S(1)} %get-tuple-element.66), channel_id=1, source_target_pairs={{0,252},{4,0},{8,4},{12,8},{16,12},{20,16},{24,20},{28,24},{32,28}... | collective-permute-start | bytes 393224 | tf_op jit(solution)/shard_map/ppermute | solution.py:468
